TPU v7x, 32 devices: a whole 2x2x4 slice. The times are simulated.
32 devices in a mesh: dp: 4 (over y, core), expert: 8 (over z, x).
Axes of the slice: x: 2, y: 2, z: 4, core: 2. Of those that a mesh axis runs over, the one named last changes fastest.
Arguments:
- tokens: bfloat16 [4096, 2048], P(('dp', 'expert')), may hold values from -6 to 6
- cotangent: bfloat16 [4096, 2048], P(('dp', 'expert')), may hold values from -6 to 6
- gate_probs: float32 [4096, 8], P(('dp', 'expert')), may hold values from 0.05 to 0.5
- routes: int32 [4096, 8], P(('dp', 'expert')), may hold values from 0 to 15, all different within a row; in each aligned block of 128 rows (0 to 127, 128 to 255, ...) at most 96 rows name the same one
- w_in: bfloat16 [32, 1024, 384], P(('expert', 'dp')), may hold values from -0.125 to 0.125
- w_out: bfloat16 [32, 192, 2048], P(('expert', 'dp')), may hold values from -0.3125 to 0.3125
- mom_in: float32 [32, 1024, 384], P(('expert', 'dp')), may hold values from -48 to 48
- mom_out: float32 [32, 192, 2048], P(('expert', 'dp')), may hold values from -48 to 48
Outputs:
- input_grad: bfloat16 [4096, 2048], P(('dp', 'expert'))
- new_mom_in: float32 [32, 1024, 384], P(('expert', 'dp'))
- new_mom_out: float32 [32, 192, 2048], P(('expert', 'dp'))
Inputs may be any that keep to these rules, and one draw needn't show every extreme that they name: `routes`: each row names 8 different experts; within the rows of one device no expert is named more than 96 times, a bound that some block reaches.
All inputs are finite; a program needn't handle non-finite values.
Results may differ from a plain program's by a relative error of at most 0.0064.
Values may be sent and summed in bfloat16 or wider, within the bound.
No kernel may reach another device: no remote copies, remote signals or barrier semaphores. Data moves between devices by JAX's collectives and lax.ppermute only.
A program may use at most 128 MiB of HBM per device.

v0:
```python
import jax
import jax.numpy as jnp
from jax import lax
from jax.sharding import PartitionSpec as P

momentum_beta = 0.9


def from_partner(shard, axis, stride):
    return lax.ppermute(shard, axis, [(i, i ^ 1 << stride) for i in range(lax.axis_size(axis))])


def earlier_counts(flat_route, experts):
    block_len = 128
    assign_total = flat_route.shape[0]
    n_blocks = assign_total // block_len
    onehot = (flat_route[:, None] == jnp.arange(experts, dtype=jnp.int32)[None, :]).astype(
        jnp.bfloat16
    )
    onehot = onehot.reshape(n_blocks, block_len, experts)
    inner_idx = jnp.arange(block_len, dtype=jnp.int32)
    tri_inner = (inner_idx[:, None] > inner_idx[None, :]).astype(jnp.bfloat16)
    inside = jnp.einsum("ij,bje->bie", tri_inner, onehot, preferred_element_type=jnp.float32)
    totals = jnp.sum(onehot.astype(jnp.float32), axis=1)
    outer_idx = jnp.arange(n_blocks, dtype=jnp.int32)
    tri_outer = (outer_idx[:, None] > outer_idx[None, :]).astype(jnp.float32)
    before = jnp.dot(
        tri_outer, totals, precision=lax.Precision.HIGHEST, preferred_element_type=jnp.float32
    )
    counts = inside + before[:, None, :]
    ranks = jnp.sum(counts * onehot.astype(jnp.float32), axis=2)
    return ranks.reshape(assign_total).astype(jnp.int32)


def per_device(tokens, cotangent, gate_probs, routes, w_in, w_out, mom_in, mom_out):
    n_data = lax.axis_size("dp")
    n_expert = lax.axis_size("expert")
    per_index = n_data // 2
    experts = n_expert * per_index
    tok_count = tokens.shape[0]
    width_d = tokens.shape[1]
    top_k = routes.shape[1]
    capacity = 2 * max(1, 3 * tok_count * top_k // (4 * experts))
    half_cap = capacity // 2
    flat_route = routes.reshape(-1)
    assign_total = flat_route.shape[0]
    rank_in = earlier_counts(flat_route, experts)
    target_dp = 2 * (flat_route % per_index) + rank_in % 2
    target_ex = flat_route // per_index
    position = (target_dp * n_expert + target_ex) * half_cap + rank_in // 2
    slot_total = n_data * n_expert * half_cap
    source_row = jnp.full((slot_total,), tok_count, jnp.int32)
    source_row = source_row.at[position].set(jnp.arange(assign_total, dtype=jnp.int32) // top_k)
    slot_prob = jnp.zeros((slot_total,), jnp.float32).at[position].set(gate_probs.reshape(-1))
    zero_row = jnp.zeros((1, width_d), jnp.bfloat16)
    send_x = jnp.concatenate([tokens, zero_row], 0)[source_row]
    cot_rows = jnp.concatenate([cotangent, zero_row], 0)[source_row]
    send_e = (slot_prob[:, None] * cot_rows.astype(jnp.float32)).astype(jnp.bfloat16)
    shape_four = (n_data, n_expert, half_cap, width_d)
    send_x = send_x.reshape(shape_four)
    send_e = send_e.reshape(shape_four)
    recv_x, recv_e = (
        lax.all_to_all(
            lax.all_to_all(send_x, "dp", split_axis=0, concat_axis=0, tiled=True),
            "expert",
            split_axis=1,
            concat_axis=1,
            tiled=True,
        ),
        lax.all_to_all(
            lax.all_to_all(send_e, "dp", split_axis=0, concat_axis=0, tiled=True),
            "expert",
            split_axis=1,
            concat_axis=1,
            tiled=True,
        ),
    )
    other_in, other_out = from_partner((w_in[0], w_out[0]), "dp", 0)
    half_idx = lax.axis_index("dp") % 2
    lower = half_idx == 0
    full_in = jnp.concatenate(
        [jnp.where(lower, w_in[0], other_in), jnp.where(lower, other_in, w_in[0])], 0
    )
    full_out = jnp.concatenate(
        [jnp.where(lower, w_out[0], other_out), jnp.where(lower, other_out, w_out[0])], 0
    )
    rows_x = recv_x.reshape(-1, width_d)
    rows_e = recv_e.reshape(-1, width_d)
    pre_act = jnp.dot(rows_x, full_in, preferred_element_type=jnp.float32)
    sigmoid_v = jax.nn.sigmoid(pre_act)
    hidden = (pre_act * sigmoid_v).astype(jnp.bfloat16)
    back_h = lax.dot_general(
        rows_e, full_out, (((1,), (1,)), ((), ())), preferred_element_type=jnp.float32
    )
    d_pre = (back_h * sigmoid_v * (1.0 + pre_act * (1.0 - sigmoid_v))).astype(jnp.bfloat16)
    dx_rows = lax.dot_general(
        d_pre, full_in, (((1,), (1,)), ((), ())), preferred_element_type=jnp.float32
    ).astype(jnp.bfloat16)
    grad_out = lax.dot_general(
        hidden, rows_e, (((0,), (0,)), ((), ())), preferred_element_type=jnp.float32
    )
    grad_in = lax.dot_general(
        rows_x, d_pre, (((0,), (0,)), ((), ())), preferred_element_type=jnp.float32
    )
    rows_half_in = width_d // 2
    rows_half_out = grad_out.shape[0] // 2
    keep_in = lax.dynamic_slice_in_dim(grad_in, half_idx * rows_half_in, rows_half_in, 0)
    give_in = lax.dynamic_slice_in_dim(grad_in, (1 - half_idx) * rows_half_in, rows_half_in, 0)
    keep_out = lax.dynamic_slice_in_dim(grad_out, half_idx * rows_half_out, rows_half_out, 0)
    give_out = lax.dynamic_slice_in_dim(grad_out, (1 - half_idx) * rows_half_out, rows_half_out, 0)
    took_in, took_out = (
        from_partner(give_in.astype(jnp.bfloat16), "dp", 0).astype(give_in.dtype),
        from_partner(give_out.astype(jnp.bfloat16), "dp", 0).astype(give_out.dtype),
    )
    new_mom_in = (momentum_beta * mom_in[0] + (keep_in + took_in))[None]
    new_mom_out = (momentum_beta * mom_out[0] + (keep_out + took_out))[None]
    dx_four = dx_rows.reshape(shape_four)
    back_rows = lax.all_to_all(
        lax.all_to_all(dx_four, "dp", split_axis=0, concat_axis=0, tiled=True),
        "expert",
        split_axis=1,
        concat_axis=1,
        tiled=True,
    )
    picked = back_rows.reshape(slot_total, width_d)[position]
    picked = picked.reshape(tok_count, top_k, width_d).astype(jnp.float32)
    input_grad = jnp.sum(picked, axis=1).astype(jnp.bfloat16)
    return (input_grad, new_mom_in, new_mom_out)


def solution(mesh):
    return jax.shard_map(
        per_device,
        mesh=mesh,
        in_specs=(
            P(("dp", "expert"), None),
            P(("dp", "expert"), None),
            P(("dp", "expert"), None),
            P(("dp", "expert"), None),
            P(("expert", "dp"), None, None),
            P(("expert", "dp"), None, None),
            P(("expert", "dp"), None, None),
            P(("expert", "dp"), None, None),
        ),
        out_specs=(
            P(("dp", "expert"), None),
            P(("expert", "dp"), None, None),
            P(("expert", "dp"), None, None),
        ),
        check_vma=False,
    )
```

profile of v0, /device:TPU:0, one launch (start us, length us, event | category | flops | bytes accessed | tf_op | source)
XLA Modules:
  0.0 710.8 jit_solution(17256513401370044897)
XLA Ops:
  0.6 0.8 copy.31
  1.4 0.1 eq.25
  1.5 0.1 reshape.261
  1.6 0.1 convert_reduce_fusion
  1.7 0.1 fusion.26
  1.8 0.2 fusion.12
  2.0 0.1 compare_select_fusion
  2.1 4.3 scatter_custom_fusion.1
  6.5 1.1 concatenate.14
  7.6 7.1 %gather_fusion.1 = bf16[1536,2048]{1,0:T(8,128)(2,1)} fusion(bf16[129,2048]{1,0:T(8,128)(2,1)S(1)} %concatenate.14, s32[2048]{0:T(1024)S(1)} %pad_clamp_fusion), kind=kCustom, calls=%fused_computation.1 | custom fusion | bytes 12589056 | tf_op jit(solution)/shard_map/gather | solution.py:56
  14.7 5.4 all-to-all-start.2
  20.1 0.1 copy.33
  20.2 0.1 reshape.298
  20.3 4.3 scatter_custom_fusion
  24.6 0.1 mul.99
  24.7 7.1 %gather_fusion = bf16[1536,2048]{1,0:T(8,128)(2,1)} fusion(bf16[129,2048]{1,0:T(8,128)(2,1)S(1)} %concatenate.12, s32[2048]{0:T(1024)S(1)} %pad_clamp_fusion), kind=kCustom, calls=%fused_computation | custom fusion | bytes 12589056 | tf_op jit(solution)/shard_map/gather | solution.py:57
  31.8 6.5 fusion
  38.3 53.1 %all-to-all-done.2 = bf16[4,8,48,2048]{3,2,1,0:T(8,128)(2,1)} async-done(((bf16[4,8,48,2048]{3,2,1,0:T(8,128)(2,1)}), bf16[4,8,48,2048]{3,2,1,0:T(8,128)(2,1)}, u32[]{:S(2)}, u32[]{:S(2)}) %all-to-all-start.2) | async-done | bytes 6291488 | tf_op jit(solution)/shard_map/all_to_all | solution.py:64
  91.4 5.2 all-to-all-start
  96.6 6.5 copy.36
  103.2 64.2 %all-to-all-done = bf16[4,8,48,2048]{3,2,1,0:T(8,128)(2,1)} async-done(((bf16[4,8,48,2048]{3,2,1,0:T(8,128)(2,1)}), bf16[4,8,48,2048]{3,2,1,0:T(8,128)(2,1)}, u32[]{:S(2)}, u32[]{:S(2)}) %all-to-all-start) | async-done | bytes 6291488 | tf_op jit(solution)/shard_map/all_to_all | solution.py:71
  167.3 6.6 all-to-all-start.3
  173.9 6.6 copy.34
  180.5 131.5 %all-to-all-done.3 = bf16[4,8,48,2048]{3,2,0,1:T(8,128)(2,1)} async-done(((bf16[4,8,48,2048]{3,2,0,1:T(8,128)(2,1)}), bf16[4,8,48,2048]{3,2,0,1:T(8,128)(2,1)}, u32[]{:S(2)}, u32[]{:S(2)}) %all-to-all-start.3) | async-done | bytes 6291488 | tf_op jit(solution)/shard_map/all_to_all | solution.py:63
  312.0 4.9 all-to-all-start.1
  316.9 0.1 collective-permute-start.1
  317.0 0.0 copy-done.7
  317.0 0.5 collective-permute-start
  317.5 1.8 collective-permute-done.1
  319.3 0.1 broadcast_select_fusion.1
  319.4 0.0 copy-start.8
  319.4 0.0 copy-start.10
  319.5 0.9 collective-permute-done
  320.4 0.1 broadcast_select_fusion.3
  320.5 3.4 copy.37
  323.9 2.6 copy-done.1
  326.5 4.9 fusion.13
  331.4 122.7 %all-to-all-done.1 = bf16[4,8,48,2048]{3,2,0,1:T(8,128)(2,1)} async-done(((bf16[4,8,48,2048]{3,2,0,1:T(8,128)(2,1)}), bf16[4,8,48,2048]{3,2,0,1:T(8,128)(2,1)}, u32[]{:S(2)}, u32[]{:S(2)}) %all-to-all-start.1) | async-done | bytes 6291488 | tf_op jit(solution)/shard_map/all_to_all | solution.py:70
  454.1 3.5 copy.35
  457.6 0.0 copy-start.9
  457.6 0.0 copy-start.11
  457.7 4.2 fusion.2
  461.9 0.0 copy-start.14
  461.9 4.7 convolution_convert_fusion
  466.6 73.3 %all_to_all.30 = bf16[4,8,48,2048]{3,2,1,0:T(8,128)(2,1)S(1)} all-to-all(bf16[4,8,48,2048]{3,2,1,0:T(8,128)(2,1)S(1)} %bitcast.56), channel_id=1, replica_groups=mesh['dp'=4,'expert'=8] {'dp'}, dimensions={0} | all-to-all | bytes 12582912 | tf_op jit(solution)/shard_map/all_to_all | solution.py:119
  539.9 3.2 copy.38
  543.1 5.1 all-to-all-start.5
  548.2 0.0 slice-start.1
  548.2 6.0 fusion.32
  554.3 1.6 copy-done.2
  555.9 1.0 dynamic-slice_convert_fusion.1
  556.9 0.0 collective-permute-start.2
  556.9 2.9 fusion.8
  559.8 1.7 copy-done.3
  561.5 1.0 dynamic-slice_convert_fusion
  562.5 0.5 collective-permute-start.3
  563.0 0.0 collective-permute-done.2
  563.0 3.7 fusion.7
  566.7 0.0 collective-permute-done.3
  566.7 2.6 fusion.6
  569.3 116.7 %all-to-all-done.5 = bf16[4,8,48,2048]{3,2,0,1:T(8,128)(2,1)} async-done(((bf16[4,8,48,2048]{3,2,0,1:T(8,128)(2,1)}), bf16[4,8,48,2048]{3,2,0,1:T(8,128)(2,1)}, u32[]{:S(2)}, u32[]{:S(2)}) %all-to-all-start.5) | async-done | bytes 6291488 | tf_op jit(solution)/shard_map/all_to_all | solution.py:118
  686.0 6.5 copy.39
  692.5 12.4 %gather_fusion.2 = bf16[1024,2048]{1,0:T(8,128)(2,1)} fusion(bf16[1536,2048]{1,0:T(8,128)(2,1)} %bitcast.47, s32[1024]{0:T(1024)S(1)} %broadcast_clamp_fusion), kind=kCustom, calls=%fused_computation.2 | custom fusion | bytes 8392704 | tf_op jit(solution)/shard_map/gather | solution.py:125
  704.9 5.9 bitcast_reduce_fusion
  (35 shorter events, 0.1 us)
Async XLA Ops:
  14.7 5.4 copy-start.13
  14.7 10.0 %copy-start.12 = (bf16[128,2048]{1,0:T(8,128)(2,1)S(1)}, bf16[128,2048]{1,0:T(8,128)(2,1)}, u32[]{:S(2)}) copy-start(bf16[128,2048]{1,0:T(8,128)(2,1)} %param.9) | copy-start | bytes 1572868
  14.7 76.7 %all-to-all-start.2 = ((bf16[4,8,48,2048]{3,2,1,0:T(8,128)(2,1)}), bf16[4,8,48,2048]{3,2,1,0:T(8,128)(2,1)}, u32[]{:S(2)}, u32[]{:S(2)}) async-start(bf16[4,8,48,2048]{3,2,1,0:T(8,128)(2,1)} %bitcast.48), calls=%async_computation.2 | async-start | bytes 12582912 | tf_op jit(solution)/shard_map/all_to_all | solution.py:64
  91.4 75.9 %all-to-all-start = ((bf16[4,8,48,2048]{3,2,1,0:T(8,128)(2,1)}), bf16[4,8,48,2048]{3,2,1,0:T(8,128)(2,1)}, u32[]{:S(2)}, u32[]{:S(2)}) async-start(bf16[4,8,48,2048]{3,2,1,0:T(8,128)(2,1)} %fusion), calls=%async_computation | async-start | bytes 12582912 | tf_op jit(solution)/shard_map/all_to_all | solution.py:71
  167.3 144.6 %all-to-all-start.3 = ((bf16[4,8,48,2048]{3,2,0,1:T(8,128)(2,1)}), bf16[4,8,48,2048]{3,2,0,1:T(8,128)(2,1)}, u32[]{:S(2)}, u32[]{:S(2)}) async-start(bf16[4,8,48,2048]{3,2,0,1:T(8,128)(2,1)} %copy.36), calls=%async_computation.3 | async-start | bytes 12582912 | tf_op jit(solution)/shard_map/all_to_all | solution.py:63
  180.5 136.4 %copy-start.6 = (bf16[1,1024,384]{2,1,0:T(8,128)(2,1)S(1)}, bf16[1,1024,384]{2,1,0:T(8,128)(2,1)}, u32[]{:S(2)}) copy-start(bf16[1,1024,384]{2,1,0:T(8,128)(2,1)} %param.12) | copy-start | bytes 2359300
  180.5 136.5 %copy-start.7 = (bf16[1,192,2048]{2,1,0:T(8,128)(2,1)S(1)}, bf16[1,192,2048]{2,1,0:T(8,128)(2,1)}, u32[]{:S(2)}) copy-start(bf16[1,192,2048]{2,1,0:T(8,128)(2,1)} %param.13) | copy-start | bytes 2359300
  312.0 142.1 %all-to-all-start.1 = ((bf16[4,8,48,2048]{3,2,0,1:T(8,128)(2,1)}), bf16[4,8,48,2048]{3,2,0,1:T(8,128)(2,1)}, u32[]{:S(2)}, u32[]{:S(2)}) async-start(bf16[4,8,48,2048]{3,2,0,1:T(8,128)(2,1)} %copy.34), calls=%async_computation.1 | async-start | bytes 12582912 | tf_op jit(solution)/shard_map/all_to_all | solution.py:70
  316.9 2.4 collective-permute-start.1
  317.0 3.4 collective-permute-start
  319.4 4.5 copy-start.8
  319.4 4.5 copy-start.10
  323.9 2.6 copy-start.1
  454.1 3.5 copy-start.15
  457.6 4.2 copy-start
  457.6 4.2 copy-start.9
  457.6 4.2 copy-start.11
  461.9 4.7 copy-start.14
  543.1 13.8 %slice-start = ((s8[6291456]{0:T(1024)(128)(4,1)}), s8[2097152]{0:T(1024)(128)(4,1)S(1)}, s32[]{:S(2)}) async-start(s8[6291456]{0:T(1024)(128)(4,1)} %bitcast.51), calls=%async_computation.6 | async-start | bytes 4194304
  543.1 142.9 %all-to-all-start.5 = ((bf16[4,8,48,2048]{3,2,0,1:T(8,128)(2,1)}), bf16[4,8,48,2048]{3,2,0,1:T(8,128)(2,1)}, u32[]{:S(2)}, u32[]{:S(2)}) async-start(bf16[4,8,48,2048]{3,2,0,1:T(8,128)(2,1)} %copy.38), calls=%async_computation.5 | async-start | bytes 12582912 | tf_op jit(solution)/shard_map/all_to_all | solution.py:118
  548.2 8.7 %slice-start.1 = ((s8[6291456]{0:T(1024)(128)(4,1)}), s8[4194304]{0:T(1024)(128)(4,1)S(1)}, s32[]{:S(2)}) async-start(s8[6291456]{0:T(1024)(128)(4,1)} %bitcast.51), calls=%async_computation.7 | async-start | bytes 8388608
  548.2 8.7 %copy-start.16 = (f32[1536,384]{1,0:T(8,128)S(1)}, f32[1536,384]{1,0:T(8,128)}, u32[]{:S(2)}) copy-start(f32[1536,384]{1,0:T(8,128)} %fusion.13) | copy-start | bytes 7077892
  554.2 1.6 copy-start.2
  556.9 6.1 collective-permute-start.2
  559.7 1.7 copy-start.3
  562.5 4.2 copy-start.4
  562.5 4.2 collective-permute-start.3
  563.0 3.7 copy-start.5
where the time goes:
time: 712 us; the launch traced here: 711 us
  waiting for transfers between devices  491 us (69%)
  local copies, waits for them, and re-layouts  75.3 us (11%)
  blocking collectives  73.3 us (10%)
  starting transfers between devices  28.3 us (4%)
  matrix products  23 us (3%)
  other arithmetic  19.1 us (3%)
    all_to_all x1, waiting for transfers between devices, per_device(): lax.all_to_all(lax.all_to_all(send_x, 'dp', split_axis=0, concat_axis=0,...  131 us
    all_to_all x1, waiting for transfers between devices, per_device(): lax.all_to_all(lax.all_to_all(send_e, 'dp', split_axis=0, concat_axis=0,...  123 us
    all_to_all x1, waiting for transfers between devices, per_device(): lax.all_to_all(lax.all_to_all(dx_four, 'dp', split_axis=0, concat_axis=0,...  117 us
    all_to_all x1, blocking collectives, per_device(): lax.all_to_all(dx_four, 'dp', split_axis=0, concat_axis=0, tiled=True)  73.3 us
    all_to_all x1, waiting for transfers between devices, per_device(): lax.all_to_all(send_e, 'dp', split_axis=0, concat_axis=0, tiled=True)  64.2 us
    all_to_all x1, waiting for transfers between devices, per_device(): lax.all_to_all(send_x, 'dp', split_axis=0, concat_axis=0, tiled=True)  53.1 us
  transfers between devices with their start and end apart: 9, of which 7 were waited for; matrix products, arithmetic and copies ran while one was open for 8% of the time, Pallas kernels for 0%

commit v1 on v0

v1 whole, which is shorter than its diff:
```python
import jax
import jax.numpy as jnp
from jax import lax
from jax.sharding import PartitionSpec as P

momentum_beta = 0.9
f32 = jnp.float32
bf16 = jnp.bfloat16


def ring_order(n, nx):
    nz = n // nx
    if n % nx or nx < 2 or nz < 2 or nz % 2:
        return list(range(n))
    order = []
    for z in range(nz):
        xs = list(range(1, nx))
        order += [z * nx + x for x in (xs if z % 2 == 0 else xs[::-1])]
    return order + [z * nx for z in reversed(range(nz))]


def after(x, *others):
    return lax.optimization_barrier((x,) + others)[0]


def per_device(tokens, cotangent, gate_probs, routes, w_in, w_out, mom_in, mom_out):
    n_data = lax.axis_size("dp")
    n = lax.axis_size("expert")
    ny = n_data // 2
    tok, width = tokens.shape
    half = tok // 2
    ff = w_in.shape[2]
    core = lax.axis_index("dp") % 2
    y_idx = lax.axis_index("dp") // 2
    ex = lax.axis_index("expert")
    lower = core == 0

    order = ring_order(n, ny)
    place = [order.index(i) for i in range(n)]

    def ring(x, step):
        return lax.ppermute(x, "expert", [(i, order[(place[i] + step) % n]) for i in range(n)])

    def swap_core(x):
        return lax.ppermute(x, "dp", [(i, i ^ 1) for i in range(n_data)])

    def shift_y(x, r):
        return lax.ppermute(x, "dp", [(i, (i // 2 + r) % ny * 2 + i % 2) for i in range(n_data)])

    top = routes.shape[1]
    parts, rest = [], gate_probs
    for _ in range(3):
        part = lax.reduce_precision(rest, 8, 7)
        parts.append(part)
        rest = rest - part
    lanes = -(-4 * top // 128) * 128
    side = jnp.concatenate(parts + [routes.astype(f32), jnp.zeros((tok, lanes - 4 * top), f32)], 1)
    cot_side = jnp.concatenate([cotangent, side.astype(bf16)], 1)
    column = lax.broadcasted_iota(jnp.int32, (1, ny * ff), 1)

    def gate_of(side):
        side = side.astype(f32)
        gate = side[:, :top] + side[:, top : 2 * top] + side[:, 2 * top : 3 * top]
        named = side[:, 3 * top : 4 * top]
        out = None
        for r in range(ny):
            expert = (ex * ny + (y_idx + r) % ny).astype(f32)
            p = jnp.sum(jnp.where(named == expert, gate, 0.0), axis=1, keepdims=True)
            out = p if out is None else jnp.where(column < r * ff, out, p)
        return jnp.broadcast_to(out, (side.shape[0], ny * ff))

    far = n // 2
    got_x, got_c = {0: tokens}, {0: cot_side}

    def pass_on(got, s):
        if s < far:
            got[-s], got[s] = ring(got[1 - s], 1), ring(got[s - 1], -1)
        else:
            fwd, bwd = ring(got[1 - s][:half], 1), ring(got[s - 1][half:], -1)
            got[s] = jnp.concatenate([fwd, bwd], 0)

    full_in = jnp.zeros((width, ny * ff), bf16)
    wout_rows = []
    rows_in = w_in.shape[1]

    def weights(r, full_in, tie):
        a, b = w_in[0], w_out[0]
        if r:
            a, b = shift_y(a, -r), shift_y(b, -r)
        oa, ob = swap_core(after(a, *tie)), swap_core(after(b, *tie))
        for piece, at in ((a, core), (oa, 1 - core)):
            full_in = lax.dynamic_update_slice(full_in, piece, (at * rows_in, r * ff))
        wout_rows.append(jnp.concatenate([jnp.where(lower, b, ob), jnp.where(lower, ob, b)], 0))
        return full_in

    span = max(1, n // 8)
    groups = [[0]]
    for s in range(1, far, span):
        groups.append([d for t in range(s, min(s + span, far)) for d in (-t, t)])
    groups.append([far])

    def within(step):
        return sum(max(group) <= step for group in groups)

    xs, cs, hs, ds, dxs = [], [], [], [], {}

    def work(group, full_in, full_out):
        x = jnp.concatenate([got_x[d] for d in group], 0)
        c = jnp.concatenate([got_c[d][:, :width] for d in group], 0)
        prob = gate_of(jnp.concatenate([got_c[d][:, width:] for d in group], 0))
        pre = jnp.dot(x, full_in, preferred_element_type=f32)
        back = lax.dot_general(c, full_out, (((1,), (1,)), ((), ())), preferred_element_type=f32)
        sig = jax.nn.sigmoid(pre)
        hid = (prob * pre * sig).astype(bf16)
        d_pre = (prob * back * sig * (1.0 + pre * (1.0 - sig))).astype(bf16)
        dx = lax.dot_general(d_pre, full_in, (((1,), (1,)), ((), ())), preferred_element_type=f32)
        for i, d in enumerate(group):
            dxs[d] = dx[i * tok : (i + 1) * tok].astype(f32 if n <= 16 else bf16)
        xs.append(x)
        cs.append(c)
        hs.append(hid)
        ds.append(d_pre)

    tn = (((0,), (0,)), ((), ()))
    grads = {}

    def add_up(which, r, block, *others):
        cols = slice(r * ff, (r + 1) * ff)
        p, q = (hs, cs) if which == "out" else (xs, ds)
        p, q = jnp.concatenate(p[block], 0), jnp.concatenate(q[block], 0)
        if which == "out":
            p = after(p[:, cols], *others)
        else:
            q = after(q[:, cols], *others)
        g = lax.dot_general(p, q, tn, preferred_element_type=f32)
        grads[which, r] = g + grads[which, r] if (which, r) in grads else g

    pairs = [(which, r) for r in list(range(1, ny)) + [0] for which in ("out", "in")]
    done = 0

    def work_up_to(count):
        nonlocal done
        while done < count:
            tie = tuple(grads.values()) if span > 1 else ()
            work(groups[done], after(full_in, *tie), full_out)
            done += 1
            if span > 1 and done < len(groups):
                for which, r in pairs:
                    add_up(which, r, slice(done - 1, done))
        return [dxs[d] for d in groups[done - 1]]

    def hold(got, s, *others):
        for d in (s, -s) if 0 < s < far else (s,):
            got[d] = after(got[d], *others)

    for s in range(1, far + 1):
        if s == min(3, far):
            for r in range(ny):
                tie = (got_c[min(2, s - 1)], got_c[-min(2, s - 1)]) if r else (got_x[1], got_x[-1])
                full_in = weights(r, full_in, tie)
            full_out = jnp.concatenate(wout_rows, 0)
        if s == far and far > 2:
            hold(got_x, far - 1, *work_up_to(within(far - 3)))
        pass_on(got_x, s)
        if s == far and far > 2:
            hold(got_c, far - 1, *work_up_to(within(far - 2)))
        pass_on(got_c, s)

    cut = within(far - 2)
    if span == 1 and cut:
        for which, r in pairs:
            add_up(which, r, slice(0, cut))
    hold(got_c, far, *grads.values())
    work_up_to(len(groups))
    last = dxs[far].astype(bf16)
    sums = {}
    for which, r in pairs:
        add_up(which, r, slice(cut if span == 1 else len(groups) - 1, None), last)
        g = grads[which, r]
        rows = g.shape[0] // 2
        keep = lax.dynamic_slice_in_dim(g, core * rows, rows, 0)
        give = lax.dynamic_slice_in_dim(g, (1 - core) * rows, rows, 0).astype(bf16)
        part = keep + swap_core(give).astype(f32)
        sums[which, r] = part.astype(bf16) if r else part
    early = [sums[which, r] for which in ("out", "in") for r in range(1, ny)]
    theirs = {(which, r): shift_y(sums[which, r], r) for which, r in pairs if r}

    def flow(lo, hi, sign, start):
        acc = dxs[sign * start if start < far else far][lo:hi].astype(bf16)
        for d in range(start - 1, -1, -1):
            acc = ring(acc, sign)
            if d == far - 1:
                acc = after(acc, *early)
            if d == min(far - 2, 1):
                acc = after(acc, *[theirs["out", r] for r in range(1, ny)])
            acc = acc.astype(f32)
            if d:
                acc = (acc + dxs[sign * d][lo:hi]).astype(bf16)
        return acc

    upper = flow(0, half, 1, far) + flow(0, half, -1, far - 1) + dxs[0][:half]
    under = flow(half, tok, -1, far) + flow(half, tok, 1, far - 1) + dxs[0][half:]
    input_grad = jnp.concatenate([upper, under], 0).astype(bf16)

    new = {}
    for which, mom in (("out", mom_out), ("in", mom_in)):
        total = sums[which, 0]
        for r in range(1, ny):
            total = total + theirs[which, r].astype(f32)
        new[which] = (momentum_beta * mom[0] + total)[None]
    return (input_grad, new["in"], new["out"])


def solution(mesh):
    rows = P(("dp", "expert"), None)
    entries = P(("expert", "dp"), None, None)
    return jax.shard_map(
        per_device,
        mesh=mesh,
        in_specs=(rows,) * 4 + (entries,) * 4,
        out_specs=(rows, entries, entries),
        check_vma=False,
    )
```

time: 712 us -> 179 us (0.25)
  waiting for transfers between devices: 491 us -> 80.4 us
  blocking collectives: 73.3 us -> 0 us
  local copies, waits for them, and re-layouts: 75.3 us -> 17.5 us
  starting transfers between devices: 28.3 us -> 41.5 us
  other arithmetic: 19.1 us -> 9.23 us
    all_to_all x5 -> x0, waiting for transfers between devices: 488 us -> none  [the longest x1 131 us: per_device(): lax.all_to_all(lax.all_to_all(send_x, 'dp', split_axis=0, concat_axis=0,...]
    ppermute x4 -> x42, waiting for transfers between devices: 2.72 us -> 80.4 us  [the longest x30 58.5 us: ring(): lax.ppermute(x, 'expert', [(i, order[(place[i] + step) % n]) for i in ran...]
    all_to_all x1 -> x0, blocking collectives: 73.3 us -> none  [per_device(): lax.all_to_all(dx_four, 'dp', split_axis=0, concat_axis=0, tiled=True)]
    ppermute x4 -> x42, starting transfers between devices: 1.06 us -> 41.5 us  [the longest x30 34.9 us: ring(): lax.ppermute(x, 'expert', [(i, order[(place[i] + step) % n]) for i in ran...]
    all_to_all x6 -> x0, local copies, waits for them, and re-layouts: 29.7 us -> none  [the longest x1 6.57 us: per_device(): lax.all_to_all(send_e, 'dp', split_axis=0, concat_axis=0, tiled=True)]
    all_to_all x5 -> x0, starting transfers between devices: 27.2 us -> none  [the longest x1 6.6 us: per_device(): lax.all_to_all(lax.all_to_all(send_x, 'dp', split_axis=0, concat_axis=0,...]
    gather x3 -> x0, local copies, waits for them, and re-layouts: 26.6 us -> none  [the longest x1 12.4 us: per_device(): picked = back_rows.reshape(slot_total, width_d)[position]]
    scatter x2 -> x0, local copies, waits for them, and re-layouts: 8.63 us -> none  [the longest x1 4.32 us: per_device(): source_row.at[position]]
  transfers between devices with their start and end apart: 9 -> 42, of which waited for: 7 -> 16; matrix products, arithmetic and copies ran while one was open for 8% -> 25% of each run, Pallas kernels for 0% -> 0%
where the time goes in v1:
time: 179 us; the launch traced here: 178 us
  waiting for transfers between devices  80.4 us (45%)
  starting transfers between devices  41.5 us (23%)
  matrix products  28.1 us (16%)
  local copies, waits for them, and re-layouts  17.5 us (10%)
  other arithmetic  9.23 us (5%)
    ppermute x30, waiting for transfers between devices, ring(): lax.ppermute(x, 'expert', [(i, order[(place[i] + step) % n]) for i in ran...  58.5 us
    ppermute x30, starting transfers between devices, ring(): lax.ppermute(x, 'expert', [(i, order[(place[i] + step) % n]) for i in ran...  34.9 us
    ppermute x4, waiting for transfers between devices, shift_y(): lax.ppermute(x, 'dp', [(i, (i // 2 + r) % ny * 2 + i % 2) for i in range(...  21.9 us
    dot_general x8, matrix products, add_up(): g = lax.dot_general(p, q, tn, preferred_element_type=f32)  11 us
    unnamed x25, local copies, waits for them, and re-layouts  8.4 us
    dot_general x5, matrix products, work(): lax.dot_general(c, full_out, (((1,), (1,)), ((), ())), preferred_element_...  5.91 us
    dot_general x5, matrix products, work(): pre = jnp.dot(x, full_in, preferred_element_type=f32)  5.83 us
    ppermute x4, starting transfers between devices, shift_y(): lax.ppermute(x, 'dp', [(i, (i // 2 + r) % ny * 2 + i % 2) for i in range(...  5.32 us
  transfers between devices with their start and end apart: 42, of which 16 were waited for; matrix products, arithmetic and copies ran while one was open for 25% of the time, Pallas kernels for 0%

profile of v1, /device:TPU:0, one launch (start us, length us, event | category | flops | bytes accessed | tf_op | source)
XLA Modules:
  0.0 178.0 jit_solution(12847441824018030869)
XLA Ops:
  0.6 3.1 %collective-permute-start.5 = (bf16[128,2048]{1,0:T(8,128)(2,1)}, bf16[128,2048]{1,0:T(8,128)(2,1)}, u32[]{:S(2)}, u32[]{:S(2)}) collective-permute-start(bf16[128,2048]{1,0:T(8,128)(2,1)} %param.8), channel_id=1, source_target_pairs={{0,2},{1,0},{2,4},{3,1},{4,6},{5,3},{6,7},{7,5},{8,10},{9,8},{10,1... | collective-permute-start | bytes 1572872 | tf_op jit(solution)/shard_map/ppermute | solution.py:42
  6.2 1.9 %concatenate.88 = bf16[128,2176]{1,0:T(8,128)(2,1)} concatenate(bf16[128,2048]{1,0:T(8,128)(2,1)} %param.9, bf16[128,8]{1,0:T(8,128)(2,1)S(1)} %copy.11, bf16[128,8]{1,0:T(8,128)(2,1)S(1)} %copy.12, bf16[128,8]{1,0:T(8,128)(2,1)S(1)} %copy.13, bf16[128,8]{1,0:T(8,128)(2,1)S(1)} %copy.14, bf16[128,96]{1,0:T(8,128)(2,1)} %broadcast_in_dim.132), dimensions={1} | concatenate | bytes 1114112 | tf_op jit(solution)/shard_map/concatenate | solution.py:58
  8.1 1.9 %collective-permute-start = (bf16[128,2176]{1,0:T(8,128)(2,1)}, bf16[128,2176]{1,0:T(8,128)(2,1)}, u32[]{:S(2)}, u32[]{:S(2)}) collective-permute-start(bf16[128,2176]{1,0:T(8,128)(2,1)} %concatenate.88), channel_id=1, source_target_pairs={{0,1},{1,3},{2,0},{3,5},{4,2},{5,7},{6,4},{7,6},{8,9},{9,11},{10,8... | collective-permute-start | bytes 1671176 | tf_op jit(solution)/shard_map/ppermute | solution.py:42
  10.2 1.9 %collective-permute-start.13 = (bf16[1024,384]{1,0:T(8,128)(2,1)}, bf16[1024,384]{1,0:T(8,128)(2,1)}, u32[]{:S(2)}, u32[]{:S(2)}) collective-permute-start(bf16[1024,384]{1,0:T(8,128)(2,1)} %bitcast.60), channel_id=1, source_target_pairs={{0,16},{8,24},{16,0},{24,8},{1,17},{9,25},{17,1},{25,9},{2,18},{10... | collective-permute-start | bytes 2359304 | tf_op jit(solution)/shard_map/ppermute | solution.py:48
  12.1 1.1 constant_dynamic-update-slice_fusion.4
  13.2 1.9 %constant_dynamic-update-slice_fusion.9 = bf16[640,2048]{1,0:T(8,128)(2,1)} fusion(bf16[128,2048]{1,0:T(8,128)(2,1)} %param.8), kind=kLoop, calls=%fused_computation.157 | loop fusion | bytes 1048576
  15.0 1.5 concatenate.94
  18.9 1.6 collective-permute-start.10
  20.4 1.1 constant_dynamic-update-slice_fusion.8
  21.6 1.1 constant_dynamic-update-slice_fusion.7
  22.6 8.2 %collective-permute-done = bf16[128,2176]{1,0:T(8,128)(2,1)} collective-permute-done((bf16[128,2176]{1,0:T(8,128)(2,1)}, bf16[128,2176]{1,0:T(8,128)(2,1)}, u32[]{:S(2)}, u32[]{:S(2)}) %collective-permute-start) | collective-permute-done | bytes 557088 | tf_op jit(solution)/shard_map/ppermute | solution.py:42
  30.8 1.6 collective-permute-start.11
  32.4 1.2 constant_dynamic-update-slice_fusion.3
  34.1 1.2 constant_dynamic-update-slice_fusion.2
  37.0 4.9 %collective-permute-done.10 = bf16[128,2048]{1,0:T(8,128)(2,1)S(1)} collective-permute-done((bf16[128,2048]{1,0:T(8,128)(2,1)}, bf16[128,2048]{1,0:T(8,128)(2,1)S(1)}, u32[]{:S(2)}, u32[]{:S(2)}) %collective-permute-start.10) | collective-permute-done | bytes 524320 | tf_op jit(solution)/shard_map/ppermute | solution.py:42
  42.0 1.6 collective-permute-start.4
  43.7 8.7 %collective-permute-done.1 = bf16[128,2176]{1,0:T(8,128)(2,1)S(1)} collective-permute-done((bf16[128,2176]{1,0:T(8,128)(2,1)}, bf16[128,2176]{1,0:T(8,128)(2,1)S(1)}, u32[]{:S(2)}, u32[]{:S(2)}) %collective-permute-start.1) | collective-permute-done | bytes 557088 | tf_op jit(solution)/shard_map/ppermute | solution.py:42
  52.5 4.8 %collective-permute-done.4 = bf16[128,2176]{1,0:T(8,128)(2,1)S(1)} collective-permute-done((bf16[128,2176]{1,0:T(8,128)(2,1)}, bf16[128,2176]{1,0:T(8,128)(2,1)S(1)}, u32[]{:S(2)}, u32[]{:S(2)}) %collective-permute-start.4) | collective-permute-done | bytes 557088 | tf_op jit(solution)/shard_map/ppermute | solution.py:42
  57.6 1.9 %collective-permute-start.20 = (bf16[128,2048]{1,0:T(8,128)(2,1)S(1)}, bf16[128,2048]{1,0:T(8,128)(2,1)S(1)}, u32[]{:S(2)}, u32[]{:S(2)}) collective-permute-start(bf16[128,2048]{1,0:T(8,128)(2,1)S(1)} %collective-permute-done.11), channel_id=1, source_target_pairs={{0,2},{1,0},{2,4},{3,1},{4,6},{5,3},{6,7},{7,5},{8,10},{9,8},{10,1... | collective-permute-start | bytes 1572872 | tf_op jit(solution)/shard_map/ppermute | solution.py:42
  61.0 1.3 constant_dynamic-update-slice_fusion.17
  62.4 2.1 %collective-permute-start.16 = (bf16[128,2176]{1,0:T(8,128)(2,1)S(1)}, bf16[128,2176]{1,0:T(8,128)(2,1)S(1)}, u32[]{:S(2)}, u32[]{:S(2)}) collective-permute-start(bf16[128,2176]{1,0:T(8,128)(2,1)S(1)} %collective-permute-done.4), channel_id=1, source_target_pairs={{0,2},{1,0},{2,4},{3,1},{4,6},{5,3},{6,7},{7,5},{8,10},{9,8},{10,1... | collective-permute-start | bytes 1671176 | tf_op jit(solution)/shard_map/ppermute | solution.py:42
  65.6 1.2 fusion.15
  67.8 1.2 fusion.20
  69.0 1.0 fusion.90
  70.1 2.2 %fusion.29 = f32[256,768]{1,0:T(8,128)S(1)} fusion(bf16[2048,768]{1,0:T(8,128)(2,1)S(1)} %constant_dynamic-update-slice_fusion.16, bf16[128,2048]{1,0:T(8,128)(2,1)} %collective-permute-done.5, bf16[128,2048]{1,0:T(8,128)(2,1)} %collective-permute-done.6), kind=kOutput, calls=%fused_computation.49 | convolution fusion | flops 807403520 | bytes 4980736 | tf_op jit(solution)/shard_map/dot_general | solution.py:111
  72.2 1.2 fusion.7
  73.5 1.0 fusion.95
  74.6 8.2 %collective-permute-done.2 = bf16[128,2176]{1,0:T(8,128)(2,1)S(1)} collective-permute-done((bf16[128,2176]{1,0:T(8,128)(2,1)S(1)}, bf16[128,2176]{1,0:T(8,128)(2,1)S(1)}, u32[]{:S(2)}, u32[]{:S(2)}) %collective-permute-start.2) | collective-permute-done | bytes 557088 | tf_op jit(solution)/shard_map/ppermute | solution.py:42
  83.4 1.4 fusion.48
  85.0 1.7 fusion.94
  86.7 2.0 %fusion.92 = f32[2048,384]{1,0:T(8,128)S(1)} fusion(bf16[640,2048]{1,0:T(8,128)(2,1)S(1)} %constant_dynamic-update-slice_fusion.5, bf16[640,384]{1,0:T(8,128)(2,1)S(1)} %get-tuple-element.74), kind=kOutput, calls=%fused_computation.193 | convolution fusion | flops 1006632960 | bytes 6258688 | tf_op jit(solution)/shard_map/dot_general | solution.py:135
  88.6 1.4 fusion.93
  90.1 1.4 fusion.91
  91.5 1.7 collective-permute-start.15
  93.2 1.6 collective-permute-start.19
  94.8 1.1 fusion.8
  95.9 1.0 fusion.89
  98.0 1.8 %collective-permute-start.29 = (bf16[64,2048]{1,0:T(8,128)(2,1)S(1)}, bf16[64,2048]{1,0:T(8,128)(2,1)S(1)}, u32[]{:S(2)}, u32[]{:S(2)}) collective-permute-start(bf16[64,2048]{1,0:T(8,128)(2,1)S(1)} %get-tuple-element.71), channel_id=1, source_target_pairs={{0,2},{1,0},{2,4},{3,1},{4,6},{5,3},{6,7},{7,5},{8,10},{9,8},{10,1... | collective-permute-start | bytes 786440 | tf_op jit(solution)/shard_map/ppermute | solution.py:42
  99.8 4.6 %collective-permute-done.19 = bf16[64,2048]{1,0:T(8,128)(2,1)S(1)} collective-permute-done((bf16[64,2048]{1,0:T(8,128)(2,1)S(1)}, bf16[64,2048]{1,0:T(8,128)(2,1)S(1)}, u32[]{:S(2)}, u32[]{:S(2)}) %collective-permute-start.19) | collective-permute-done | bytes 262176 | tf_op jit(solution)/shard_map/ppermute | solution.py:42
  104.5 1.4 collective-permute-start.36
  105.9 6.2 %collective-permute-done.21 = bf16[64,2048]{1,0:T(8,128)(2,1)S(1)} collective-permute-done((bf16[64,2048]{1,0:T(8,128)(2,1)S(1)}, bf16[64,2048]{1,0:T(8,128)(2,1)S(1)}, u32[]{:S(2)}, u32[]{:S(2)}) %collective-permute-start.21) | collective-permute-done | bytes 262176 | tf_op jit(solution)/shard_map/ppermute | solution.py:42
  113.1 1.2 fusion.14
  114.3 1.1 convolution_convert_fusion
  115.6 1.1 convolution_add_fusion.3
  116.9 1.2 convolution_add_fusion.2
  119.3 1.6 collective-permute-start.22
  121.3 5.8 %collective-permute-done.32 = bf16[64,2048]{1,0:T(8,128)(2,1)S(1)} collective-permute-done((bf16[64,2048]{1,0:T(8,128)(2,1)S(1)}, bf16[64,2048]{1,0:T(8,128)(2,1)S(1)}, u32[]{:S(2)}, u32[]{:S(2)}) %collective-permute-start.32) | collective-permute-done | bytes 262176 | tf_op jit(solution)/shard_map/ppermute | solution.py:42
  127.6 1.6 collective-permute-start.25
  129.7 1.1 fusion.96
  130.8 4.2 %collective-permute-done.25 = bf16[64,2048]{1,0:T(8,128)(2,1)S(1)} collective-permute-done((bf16[64,2048]{1,0:T(8,128)(2,1)S(1)}, bf16[64,2048]{1,0:T(8,128)(2,1)S(1)}, u32[]{:S(2)}, u32[]{:S(2)}) %collective-permute-start.25) | collective-permute-done | bytes 262176 | tf_op jit(solution)/shard_map/ppermute | solution.py:42
  135.0 1.3 collective-permute-done.33
  137.3 1.0 convolution_add_fusion
  138.4 1.6 collective-permute-start.27
  140.5 1.7 collective-permute-start.37
  142.2 1.0 collective-permute-done.30
  143.2 1.6 collective-permute-start.26
  144.8 1.2 convolution_add_fusion.1
  146.1 9.4 %collective-permute-done.27 = bf16[192,2048]{1,0:T(8,128)(2,1)S(1)} collective-permute-done((bf16[192,2048]{1,0:T(8,128)(2,1)S(1)}, bf16[192,2048]{1,0:T(8,128)(2,1)S(1)}, u32[]{:S(2)}, u32[]{:S(2)}) %collective-permute-start.27) | collective-permute-done | bytes 786464 | tf_op jit(solution)/shard_map/ppermute | solution.py:48
  155.6 1.5 collective-permute-start.40
  157.4 1.7 collective-permute-start.28
  159.7 1.6 fusion
  161.3 1.7 collective-permute-start.38
  163.1 12.5 %collective-permute-done.40 = bf16[1024,384]{1,0:T(8,128)(2,1)S(1)} collective-permute-done((bf16[1024,384]{1,0:T(8,128)(2,1)S(1)}, bf16[1024,384]{1,0:T(8,128)(2,1)S(1)}, u32[]{:S(2)}, u32[]{:S(2)}) %collective-permute-start.40) | collective-permute-done | bytes 786464 | tf_op jit(solution)/shard_map/ppermute | solution.py:48
  175.5 1.4 fusion.1
  (133 shorter events, 21.0 us)
Async XLA Ops:
  0.6 17.3 %collective-permute-start.5 = (bf16[128,2048]{1,0:T(8,128)(2,1)}, bf16[128,2048]{1,0:T(8,128)(2,1)}, u32[]{:S(2)}, u32[]{:S(2)}) collective-permute-start(bf16[128,2048]{1,0:T(8,128)(2,1)} %param.8), channel_id=1, source_target_pairs={{0,2},{1,0},{2,4},{3,1},{4,6},{5,3},{6,7},{7,5},{8,10},{9,8},{10,1... | collective-permute-start | bytes 1572872 | tf_op jit(solution)/shard_map/ppermute | solution.py:42
  3.7 15.2 %collective-permute-start.6 = (bf16[128,2048]{1,0:T(8,128)(2,1)}, bf16[128,2048]{1,0:T(8,128)(2,1)}, u32[]{:S(2)}, u32[]{:S(2)}) collective-permute-start(bf16[128,2048]{1,0:T(8,128)(2,1)} %param.8), channel_id=1, source_target_pairs={{0,1},{1,3},{2,0},{3,5},{4,2},{5,7},{6,4},{7,6},{8,9},{9,11},{10,8... | collective-permute-start | bytes 1572872 | tf_op jit(solution)/shard_map/ppermute | solution.py:42
  8.1 9.6 %copy-start.3 = (bf16[1,1024,384]{2,1,0:T(8,128)(2,1)S(1)}, bf16[1,1024,384]{2,1,0:T(8,128)(2,1)}, u32[]{:S(2)}) copy-start(bf16[1,1024,384]{2,1,0:T(8,128)(2,1)} %param.12) | copy-start | bytes 2359300
  8.1 22.7 %collective-permute-start = (bf16[128,2176]{1,0:T(8,128)(2,1)}, bf16[128,2176]{1,0:T(8,128)(2,1)}, u32[]{:S(2)}, u32[]{:S(2)}) collective-permute-start(bf16[128,2176]{1,0:T(8,128)(2,1)} %concatenate.88), channel_id=1, source_target_pairs={{0,1},{1,3},{2,0},{3,5},{4,2},{5,7},{6,4},{7,6},{8,9},{9,11},{10,8... | collective-permute-start | bytes 1671176 | tf_op jit(solution)/shard_map/ppermute | solution.py:42
  10.0 23.5 %collective-permute-start.3 = (bf16[128,2176]{1,0:T(8,128)(2,1)}, bf16[128,2176]{1,0:T(8,128)(2,1)}, u32[]{:S(2)}, u32[]{:S(2)}) collective-permute-start(bf16[128,2176]{1,0:T(8,128)(2,1)} %concatenate.88), channel_id=1, source_target_pairs={{0,2},{1,0},{2,4},{3,1},{4,6},{5,3},{6,7},{7,5},{8,10},{9,8},{10,1... | collective-permute-start | bytes 1671176 | tf_op jit(solution)/shard_map/ppermute | solution.py:42
  10.2 47.5 %collective-permute-start.13 = (bf16[1024,384]{1,0:T(8,128)(2,1)}, bf16[1024,384]{1,0:T(8,128)(2,1)}, u32[]{:S(2)}, u32[]{:S(2)}) collective-permute-start(bf16[1024,384]{1,0:T(8,128)(2,1)} %bitcast.60), channel_id=1, source_target_pairs={{0,16},{8,24},{16,0},{24,8},{1,17},{9,25},{17,1},{25,9},{2,18},{10... | collective-permute-start | bytes 2359304 | tf_op jit(solution)/shard_map/ppermute | solution.py:48
  17.3 1.1 copy-start.4
  17.3 3.1 %copy-start.6 = (bf16[640,2048]{1,0:T(8,128)(2,1)S(1)}, bf16[640,2048]{1,0:T(8,128)(2,1)}, u32[]{:S(2)}) copy-start(bf16[640,2048]{1,0:T(8,128)(2,1)} %constant_dynamic-update-slice_fusion.9) | copy-start | bytes 7864324
  18.4 41.1 %collective-permute-start.8 = (bf16[192,2048]{1,0:T(8,128)(2,1)S(1)}, bf16[192,2048]{1,0:T(8,128)(2,1)S(1)}, u32[]{:S(2)}, u32[]{:S(2)}) collective-permute-start(bf16[192,2048]{1,0:T(8,128)(2,1)S(1)} %bitcast.62), channel_id=1, source_target_pairs={{0,16},{8,24},{16,0},{24,8},{1,17},{9,25},{17,1},{25,9},{2,18},{10... | collective-permute-start | bytes 2359304 | tf_op jit(solution)/shard_map/ppermute | solution.py:48
  18.9 23.1 %collective-permute-start.10 = (bf16[128,2048]{1,0:T(8,128)(2,1)}, bf16[128,2048]{1,0:T(8,128)(2,1)S(1)}, u32[]{:S(2)}, u32[]{:S(2)}) collective-permute-start(bf16[128,2048]{1,0:T(8,128)(2,1)} %collective-permute-done.6), channel_id=1, source_target_pairs={{0,1},{1,3},{2,0},{3,5},{4,2},{5,7},{6,4},{7,6},{8,9},{9,11},{10,8... | collective-permute-start | bytes 1572872 | tf_op jit(solution)/shard_map/ppermute | solution.py:42
  30.8 11.2 %collective-permute-start.11 = (bf16[128,2048]{1,0:T(8,128)(2,1)}, bf16[128,2048]{1,0:T(8,128)(2,1)S(1)}, u32[]{:S(2)}, u32[]{:S(2)}) collective-permute-start(bf16[128,2048]{1,0:T(8,128)(2,1)} %collective-permute-done.5), channel_id=1, source_target_pairs={{0,2},{1,0},{2,4},{3,1},{4,6},{5,3},{6,7},{7,5},{8,10},{9,8},{10,1... | collective-permute-start | bytes 1572872 | tf_op jit(solution)/shard_map/ppermute | solution.py:42
  33.6 18.9 %collective-permute-start.1 = (bf16[128,2176]{1,0:T(8,128)(2,1)}, bf16[128,2176]{1,0:T(8,128)(2,1)S(1)}, u32[]{:S(2)}, u32[]{:S(2)}) collective-permute-start(bf16[128,2176]{1,0:T(8,128)(2,1)} %collective-permute-done), channel_id=1, source_target_pairs={{0,1},{1,3},{2,0},{3,5},{4,2},{5,7},{6,4},{7,6},{8,9},{9,11},{10,8... | collective-permute-start | bytes 1671176 | tf_op jit(solution)/shard_map/ppermute | solution.py:42
  41.9 18.7 %collective-permute-start.12 = (bf16[1024,384]{1,0:T(8,128)(2,1)S(1)}, bf16[1024,384]{1,0:T(8,128)(2,1)S(1)}, u32[]{:S(2)}, u32[]{:S(2)}) collective-permute-start(bf16[1024,384]{1,0:T(8,128)(2,1)S(1)} %bitcast.61), channel_id=1, source_target_pairs={{0,8},{8,0},{16,24},{24,16},{1,9},{9,1},{17,25},{25,17},{2,10},{10... | collective-permute-start | bytes 2359304 | tf_op jit(solution)/shard_map/ppermute | solution.py:45
  42.0 15.3 %collective-permute-start.4 = (bf16[128,2176]{1,0:T(8,128)(2,1)}, bf16[128,2176]{1,0:T(8,128)(2,1)S(1)}, u32[]{:S(2)}, u32[]{:S(2)}) collective-permute-start(bf16[128,2176]{1,0:T(8,128)(2,1)} %collective-permute-done.3), channel_id=1, source_target_pairs={{0,2},{1,0},{2,4},{3,1},{4,6},{5,3},{6,7},{7,5},{8,10},{9,8},{10,1... | collective-permute-start | bytes 1671176 | tf_op jit(solution)/shard_map/ppermute | solution.py:42
  52.4 7.4 %collective-permute-start.7 = (bf16[192,2048]{1,0:T(8,128)(2,1)S(1)}, bf16[192,2048]{1,0:T(8,128)(2,1)S(1)}, u32[]{:S(2)}, u32[]{:S(2)}) collective-permute-start(bf16[192,2048]{1,0:T(8,128)(2,1)S(1)} %bitcast.63), channel_id=1, source_target_pairs={{0,8},{8,0},{16,24},{24,16},{1,9},{9,1},{17,25},{25,17},{2,10},{10... | collective-permute-start | bytes 2359304 | tf_op jit(solution)/shard_map/ppermute | solution.py:45
  57.3 25.7 %collective-permute-start.18 = (bf16[128,2048]{1,0:T(8,128)(2,1)S(1)}, bf16[128,2048]{1,0:T(8,128)(2,1)S(1)}, u32[]{:S(2)}, u32[]{:S(2)}) collective-permute-start(bf16[128,2048]{1,0:T(8,128)(2,1)S(1)} %collective-permute-done.10), channel_id=1, source_target_pairs={{0,1},{1,3},{2,0},{3,5},{4,2},{5,7},{6,4},{7,6},{8,9},{9,11},{10,8... | collective-permute-start | bytes 1572872 | tf_op jit(solution)/shard_map/ppermute | solution.py:42
  57.6 25.4 %collective-permute-start.20 = (bf16[128,2048]{1,0:T(8,128)(2,1)S(1)}, bf16[128,2048]{1,0:T(8,128)(2,1)S(1)}, u32[]{:S(2)}, u32[]{:S(2)}) collective-permute-start(bf16[128,2048]{1,0:T(8,128)(2,1)S(1)} %collective-permute-done.11), channel_id=1, source_target_pairs={{0,2},{1,0},{2,4},{3,1},{4,6},{5,3},{6,7},{7,5},{8,10},{9,8},{10,1... | collective-permute-start | bytes 1572872 | tf_op jit(solution)/shard_map/ppermute | solution.py:42
  59.5 2.8 %collective-permute-start.14 = (bf16[1024,384]{1,0:T(8,128)(2,1)}, bf16[1024,384]{1,0:T(8,128)(2,1)S(1)}, u32[]{:S(2)}, u32[]{:S(2)}) collective-permute-start(bf16[1024,384]{1,0:T(8,128)(2,1)} %collective-permute-done.13), channel_id=1, source_target_pairs={{0,8},{8,0},{16,24},{24,16},{1,9},{9,1},{17,25},{25,17},{2,10},{10... | collective-permute-start | bytes 2359304 | tf_op jit(solution)/shard_map/ppermute | solution.py:45
  59.8 5.4 %collective-permute-start.9 = (bf16[192,2048]{1,0:T(8,128)(2,1)S(1)}, bf16[192,2048]{1,0:T(8,128)(2,1)S(1)}, u32[]{:S(2)}, u32[]{:S(2)}) collective-permute-start(bf16[192,2048]{1,0:T(8,128)(2,1)S(1)} %collective-permute-done.8), channel_id=1, source_target_pairs={{0,8},{8,0},{16,24},{24,16},{1,9},{9,1},{17,25},{25,17},{2,10},{10... | collective-permute-start | bytes 2359304 | tf_op jit(solution)/shard_map/ppermute | solution.py:45
  60.6 4.0 %copy-start.5 = (bf16[128,2048]{1,0:T(8,128)(2,1)S(1)}, bf16[128,2048]{1,0:T(8,128)(2,1)}, u32[]{:S(2)}) copy-start(bf16[128,2048]{1,0:T(8,128)(2,1)} %param.8) | copy-start | bytes 1572868
  60.6 22.2 %collective-permute-start.2 = (bf16[128,2176]{1,0:T(8,128)(2,1)S(1)}, bf16[128,2176]{1,0:T(8,128)(2,1)S(1)}, u32[]{:S(2)}, u32[]{:S(2)}) collective-permute-start(bf16[128,2176]{1,0:T(8,128)(2,1)S(1)} %collective-permute-done.1), channel_id=1, source_target_pairs={{0,1},{1,3},{2,0},{3,5},{4,2},{5,7},{6,4},{7,6},{8,9},{9,11},{10,8... | collective-permute-start | bytes 1671176 | tf_op jit(solution)/shard_map/ppermute | solution.py:42
  62.4 20.6 %collective-permute-start.16 = (bf16[128,2176]{1,0:T(8,128)(2,1)S(1)}, bf16[128,2176]{1,0:T(8,128)(2,1)S(1)}, u32[]{:S(2)}, u32[]{:S(2)}) collective-permute-start(bf16[128,2176]{1,0:T(8,128)(2,1)S(1)} %collective-permute-done.4), channel_id=1, source_target_pairs={{0,2},{1,0},{2,4},{3,1},{4,6},{5,3},{6,7},{7,5},{8,10},{9,8},{10,1... | collective-permute-start | bytes 1671176 | tf_op jit(solution)/shard_map/ppermute | solution.py:42
  64.6 1.0 copy-start
  91.5 20.7 %collective-permute-start.15 = (bf16[64,2176]{1,0:T(8,128)(2,1)S(1)}, bf16[64,2176]{1,0:T(8,128)(2,1)S(1)}, u32[]{:S(2)}, u32[]{:S(2)}) collective-permute-start(bf16[64,2176]{1,0:T(8,128)(2,1)S(1)} %slice.226), channel_id=1, source_target_pairs={{0,1},{1,3},{2,0},{3,5},{4,2},{5,7},{6,4},{7,6},{8,9},{9,11},{10,8... | collective-permute-start | bytes 835592 | tf_op jit(solution)/shard_map/ppermute | solution.py:42
  93.2 11.3 %collective-permute-start.19 = (bf16[64,2048]{1,0:T(8,128)(2,1)S(1)}, bf16[64,2048]{1,0:T(8,128)(2,1)S(1)}, u32[]{:S(2)}, u32[]{:S(2)}) collective-permute-start(bf16[64,2048]{1,0:T(8,128)(2,1)S(1)} %slice.252), channel_id=1, source_target_pairs={{0,1},{1,3},{2,0},{3,5},{4,2},{5,7},{6,4},{7,6},{8,9},{9,11},{10,8... | collective-permute-start | bytes 786440 | tf_op jit(solution)/shard_map/ppermute | solution.py:42
  97.1 15.1 %collective-permute-start.17 = (bf16[64,2176]{1,0:T(8,128)(2,1)S(1)}, bf16[64,2176]{1,0:T(8,128)(2,1)S(1)}, u32[]{:S(2)}, u32[]{:S(2)}) collective-permute-start(bf16[64,2176]{1,0:T(8,128)(2,1)S(1)} %slice.227), channel_id=1, source_target_pairs={{0,2},{1,0},{2,4},{3,1},{4,6},{5,3},{6,7},{7,5},{8,10},{9,8},{10,1... | collective-permute-start | bytes 835592 | tf_op jit(solution)/shard_map/ppermute | solution.py:42
  97.6 14.5 %collective-permute-start.21 = (bf16[64,2048]{1,0:T(8,128)(2,1)S(1)}, bf16[64,2048]{1,0:T(8,128)(2,1)S(1)}, u32[]{:S(2)}, u32[]{:S(2)}) collective-permute-start(bf16[64,2048]{1,0:T(8,128)(2,1)S(1)} %slice.253), channel_id=1, source_target_pairs={{0,2},{1,0},{2,4},{3,1},{4,6},{5,3},{6,7},{7,5},{8,10},{9,8},{10,1... | collective-permute-start | bytes 786440 | tf_op jit(solution)/shard_map/ppermute | solution.py:42
  98.0 32.8 %collective-permute-start.29 = (bf16[64,2048]{1,0:T(8,128)(2,1)S(1)}, bf16[64,2048]{1,0:T(8,128)(2,1)S(1)}, u32[]{:S(2)}, u32[]{:S(2)}) collective-permute-start(bf16[64,2048]{1,0:T(8,128)(2,1)S(1)} %get-tuple-element.71), channel_id=1, source_target_pairs={{0,2},{1,0},{2,4},{3,1},{4,6},{5,3},{6,7},{7,5},{8,10},{9,8},{10,1... | collective-permute-start | bytes 786440 | tf_op jit(solution)/shard_map/ppermute | solution.py:42
  104.5 26.4 %collective-permute-start.36 = (bf16[64,2048]{1,0:T(8,128)(2,1)S(1)}, bf16[64,2048]{1,0:T(8,128)(2,1)S(1)}, u32[]{:S(2)}, u32[]{:S(2)}) collective-permute-start(bf16[64,2048]{1,0:T(8,128)(2,1)S(1)} %get-tuple-element.72), channel_id=1, source_target_pairs={{0,1},{1,3},{2,0},{3,5},{4,2},{5,7},{6,4},{7,6},{8,9},{9,11},{10,8... | collective-permute-start | bytes 786440 | tf_op jit(solution)/shard_map/ppermute | solution.py:42
  116.8 2.5 %collective-permute-start.23 = (bf16[192,2048]{1,0:T(8,128)(2,1)S(1)}, bf16[192,2048]{1,0:T(8,128)(2,1)S(1)}, u32[]{:S(2)}, u32[]{:S(2)}) collective-permute-start(bf16[192,2048]{1,0:T(8,128)(2,1)S(1)} %dynamic-slice_convert_fusion.3), channel_id=1, source_target_pairs={{0,8},{8,0},{16,24},{24,16},{1,9},{9,1},{17,25},{25,17},{2,10},{10... | collective-permute-start | bytes 2359304 | tf_op jit(solution)/shard_map/ppermute | solution.py:45
  118.2 2.9 %collective-permute-start.24 = (bf16[1024,384]{1,0:T(8,128)(2,1)S(1)}, bf16[1024,384]{1,0:T(8,128)(2,1)S(1)}, u32[]{:S(2)}, u32[]{:S(2)}) collective-permute-start(bf16[1024,384]{1,0:T(8,128)(2,1)S(1)} %dynamic-slice_convert_fusion.2), channel_id=1, source_target_pairs={{0,8},{8,0},{16,24},{24,16},{1,9},{9,1},{17,25},{25,17},{2,10},{10... | collective-permute-start | bytes 2359304 | tf_op jit(solution)/shard_map/ppermute | solution.py:45
  118.8 8.3 %collective-permute-start.32 = (bf16[64,2048]{1,0:T(8,128)(2,1)S(1)}, bf16[64,2048]{1,0:T(8,128)(2,1)S(1)}, u32[]{:S(2)}, u32[]{:S(2)}) collective-permute-start(bf16[64,2048]{1,0:T(8,128)(2,1)S(1)} %get-tuple-element.90), channel_id=1, source_target_pairs={{0,2},{1,0},{2,4},{3,1},{4,6},{5,3},{6,7},{7,5},{8,10},{9,8},{10,1... | collective-permute-start | bytes 786440 | tf_op jit(solution)/shard_map/ppermute | solution.py:42
  119.3 8.2 %collective-permute-start.22 = (bf16[64,2048]{1,0:T(8,128)(2,1)S(1)}, bf16[64,2048]{1,0:T(8,128)(2,1)S(1)}, u32[]{:S(2)}, u32[]{:S(2)}) collective-permute-start(bf16[64,2048]{1,0:T(8,128)(2,1)S(1)} %get-tuple-element.89), channel_id=1, source_target_pairs={{0,1},{1,3},{2,0},{3,5},{4,2},{5,7},{6,4},{7,6},{8,9},{9,11},{10,8... | collective-permute-start | bytes 786440 | tf_op jit(solution)/shard_map/ppermute | solution.py:42
  127.6 7.4 %collective-permute-start.25 = (bf16[64,2048]{1,0:T(8,128)(2,1)S(1)}, bf16[64,2048]{1,0:T(8,128)(2,1)S(1)}, u32[]{:S(2)}, u32[]{:S(2)}) collective-permute-start(bf16[64,2048]{1,0:T(8,128)(2,1)S(1)} %get-tuple-element.59), channel_id=1, source_target_pairs={{0,1},{1,3},{2,0},{3,5},{4,2},{5,7},{6,4},{7,6},{8,9},{9,11},{10,8... | collective-permute-start | bytes 786440 | tf_op jit(solution)/shard_map/ppermute | solution.py:42
  129.2 7.0 %collective-permute-start.33 = (bf16[64,2048]{1,0:T(8,128)(2,1)S(1)}, bf16[64,2048]{1,0:T(8,128)(2,1)S(1)}, u32[]{:S(2)}, u32[]{:S(2)}) collective-permute-start(bf16[64,2048]{1,0:T(8,128)(2,1)S(1)} %get-tuple-element.60), channel_id=1, source_target_pairs={{0,2},{1,0},{2,4},{3,1},{4,6},{5,3},{6,7},{7,5},{8,10},{9,8},{10,1... | collective-permute-start | bytes 786440 | tf_op jit(solution)/shard_map/ppermute | solution.py:42
  136.5 6.7 %collective-permute-start.30 = (bf16[64,2048]{1,0:T(8,128)(2,1)S(1)}, bf16[64,2048]{1,0:T(8,128)(2,1)S(1)}, u32[]{:S(2)}, u32[]{:S(2)}) collective-permute-start(bf16[64,2048]{1,0:T(8,128)(2,1)S(1)} %get-tuple-element.58), channel_id=1, source_target_pairs={{0,2},{1,0},{2,4},{3,1},{4,6},{5,3},{6,7},{7,5},{8,10},{9,8},{10,1... | collective-permute-start | bytes 786440 | tf_op jit(solution)/shard_map/ppermute | solution.py:42
  138.4 17.2 %collective-permute-start.27 = (bf16[192,2048]{1,0:T(8,128)(2,1)S(1)}, bf16[192,2048]{1,0:T(8,128)(2,1)S(1)}, u32[]{:S(2)}, u32[]{:S(2)}) collective-permute-start(bf16[192,2048]{1,0:T(8,128)(2,1)S(1)} %add_convert_fusion.1), channel_id=1, source_target_pairs={{0,16},{8,24},{16,0},{24,8},{1,17},{9,25},{17,1},{25,9},{2,18},{10... | collective-permute-start | bytes 2359304 | tf_op jit(solution)/shard_map/ppermute | solution.py:48
  140.1 19.4 %collective-permute-start.41 = (bf16[192,2048]{1,0:T(8,128)(2,1)S(1)}, bf16[192,2048]{1,0:T(8,128)(2,1)S(1)}, u32[]{:S(2)}, u32[]{:S(2)}) collective-permute-start(bf16[192,2048]{1,0:T(8,128)(2,1)S(1)} %dynamic-slice_convert_fusion), channel_id=1, source_target_pairs={{0,8},{8,0},{16,24},{24,16},{1,9},{9,1},{17,25},{25,17},{2,10},{10... | collective-permute-start | bytes 2359304 | tf_op jit(solution)/shard_map/ppermute | solution.py:45
  140.1 15.4 %collective-permute-start.34 = (bf16[64,2048]{1,0:T(8,128)(2,1)S(1)}, bf16[64,2048]{1,0:T(8,128)(2,1)S(1)}, u32[]{:S(2)}, u32[]{:S(2)}) collective-permute-start(bf16[64,2048]{1,0:T(8,128)(2,1)S(1)} %get-tuple-element.57), channel_id=1, source_target_pairs={{0,2},{1,0},{2,4},{3,1},{4,6},{5,3},{6,7},{7,5},{8,10},{9,8},{10,1... | collective-permute-start | bytes 786440 | tf_op jit(solution)/shard_map/ppermute | solution.py:42
  140.5 16.6 %collective-permute-start.37 = (bf16[64,2048]{1,0:T(8,128)(2,1)S(1)}, bf16[64,2048]{1,0:T(8,128)(2,1)S(1)}, u32[]{:S(2)}, u32[]{:S(2)}) collective-permute-start(bf16[64,2048]{1,0:T(8,128)(2,1)S(1)} %get-tuple-element.56), channel_id=1, source_target_pairs={{0,1},{1,3},{2,0},{3,5},{4,2},{5,7},{6,4},{7,6},{8,9},{9,11},{10,8... | collective-permute-start | bytes 786440 | tf_op jit(solution)/shard_map/ppermute | solution.py:42
  143.2 13.8 %collective-permute-start.26 = (bf16[64,2048]{1,0:T(8,128)(2,1)S(1)}, bf16[64,2048]{1,0:T(8,128)(2,1)S(1)}, u32[]{:S(2)}, u32[]{:S(2)}) collective-permute-start(bf16[64,2048]{1,0:T(8,128)(2,1)S(1)} %get-tuple-element.55), channel_id=1, source_target_pairs={{0,1},{1,3},{2,0},{3,5},{4,2},{5,7},{6,4},{7,6},{8,9},{9,11},{10,8... | collective-permute-start | bytes 786440 | tf_op jit(solution)/shard_map/ppermute | solution.py:42
  146.0 13.7 %copy-start.1 = (f32[1,192,2048]{2,1,0:T(8,128)S(1)}, f32[1,192,2048]{2,1,0:T(8,128)}, u32[]{:S(2)}) copy-start(f32[1,192,2048]{2,1,0:T(8,128)} %param.15) | copy-start | bytes 4718596
  155.6 5.8 %collective-permute-start.39 = (bf16[1024,384]{1,0:T(8,128)(2,1)S(1)}, bf16[1024,384]{1,0:T(8,128)(2,1)S(1)}, u32[]{:S(2)}, u32[]{:S(2)}) collective-permute-start(bf16[1024,384]{1,0:T(8,128)(2,1)S(1)} %dynamic-slice_convert_fusion.1), channel_id=1, source_target_pairs={{0,8},{8,0},{16,24},{24,16},{1,9},{9,1},{17,25},{25,17},{2,10},{10... | collective-permute-start | bytes 2359304 | tf_op jit(solution)/shard_map/ppermute | solution.py:45
  155.6 20.0 %collective-permute-start.40 = (bf16[1024,384]{1,0:T(8,128)(2,1)S(1)}, bf16[1024,384]{1,0:T(8,128)(2,1)S(1)}, u32[]{:S(2)}, u32[]{:S(2)}) collective-permute-start(bf16[1024,384]{1,0:T(8,128)(2,1)S(1)} %add_convert_fusion), channel_id=1, source_target_pairs={{0,16},{8,24},{16,0},{24,8},{1,17},{9,25},{17,1},{25,9},{2,18},{10... | collective-permute-start | bytes 2359304 | tf_op jit(solution)/shard_map/ppermute | solution.py:48
  157.4 19.6 %collective-permute-start.28 = (bf16[64,2048]{1,0:T(8,128)(2,1)S(1)}, bf16[64,2048]{1,0:T(8,128)(2,1)S(1)}, u32[]{:S(2)}, u32[]{:S(2)}) collective-permute-start(bf16[64,2048]{1,0:T(8,128)(2,1)S(1)} %get-tuple-element.51), channel_id=1, source_target_pairs={{0,1},{1,3},{2,0},{3,5},{4,2},{5,7},{6,4},{7,6},{8,9},{9,11},{10,8... | collective-permute-start | bytes 786440 | tf_op jit(solution)/shard_map/ppermute | solution.py:42
  159.0 18.0 %collective-permute-start.31 = (bf16[64,2048]{1,0:T(8,128)(2,1)S(1)}, bf16[64,2048]{1,0:T(8,128)(2,1)S(1)}, u32[]{:S(2)}, u32[]{:S(2)}) collective-permute-start(bf16[64,2048]{1,0:T(8,128)(2,1)S(1)} %get-tuple-element.54), channel_id=1, source_target_pairs={{0,2},{1,0},{2,4},{3,1},{4,6},{5,3},{6,7},{7,5},{8,10},{9,8},{10,1... | collective-permute-start | bytes 786440 | tf_op jit(solution)/shard_map/ppermute | solution.py:42
  159.4 16.1 %copy-start.2 = (f32[1,1024,384]{2,1,0:T(8,128)S(1)}, f32[1,1024,384]{2,1,0:T(8,128)}, u32[]{:S(2)}) copy-start(f32[1,1024,384]{2,1,0:T(8,128)} %param.14) | copy-start | bytes 4718596
  159.4 17.5 %collective-permute-start.35 = (bf16[64,2048]{1,0:T(8,128)(2,1)S(1)}, bf16[64,2048]{1,0:T(8,128)(2,1)S(1)}, u32[]{:S(2)}, u32[]{:S(2)}) collective-permute-start(bf16[64,2048]{1,0:T(8,128)(2,1)S(1)} %get-tuple-element.53), channel_id=1, source_target_pairs={{0,2},{1,0},{2,4},{3,1},{4,6},{5,3},{6,7},{7,5},{8,10},{9,8},{10,1... | collective-permute-start | bytes 786440 | tf_op jit(solution)/shard_map/ppermute | solution.py:42
  161.3 15.7 %collective-permute-start.38 = (bf16[64,2048]{1,0:T(8,128)(2,1)S(1)}, bf16[64,2048]{1,0:T(8,128)(2,1)S(1)}, u32[]{:S(2)}, u32[]{:S(2)}) collective-permute-start(bf16[64,2048]{1,0:T(8,128)(2,1)S(1)} %get-tuple-element.52), channel_id=1, source_target_pairs={{0,1},{1,3},{2,0},{3,5},{4,2},{5,7},{6,4},{7,6},{8,9},{9,11},{10,8... | collective-permute-start | bytes 786440 | tf_op jit(solution)/shard_map/ppermute | solution.py:42

commit v2 on v1

v2 whole, which is shorter than its diff:
```python
import jax
import jax.numpy as jnp
from jax import lax
from jax.experimental import pallas as pl
from jax.experimental.pallas import tpu as pltpu
from jax.sharding import PartitionSpec as P

momentum_beta = 0.9
f32 = jnp.float32
bf16 = jnp.bfloat16


def ring_order(n, nx):
    nz = n // nx
    if n % nx or nx < 2 or nz < 2 or nz % 2:
        return list(range(n))
    order = []
    for z in range(nz):
        xs = list(range(1, nx))
        order += [z * nx + x for x in (xs if z % 2 == 0 else xs[::-1])]
    return order + [z * nx for z in reversed(range(nz))]


def after(x, *others):
    return lax.optimization_barrier((x,) + others)[0]


def pack(tokens, cotangent, gate_probs, routes, experts):
    tok, width = tokens.shape
    top = routes.shape[1]
    half = tok // 2
    lanes = -(-3 * experts // 128) * 128

    def kernel(tok_ref, cot_ref, gate_ref, route_ref, *outs):
        gate = gate_ref[...].T
        route = route_ref[...].astype(f32).T
        lane = lax.broadcasted_iota(jnp.int32, (tok, lanes), 1)
        part = sum((lane >= i * experts).astype(jnp.int32) for i in range(1, 4))
        expert = (lane - part * experts).astype(f32)
        p = jnp.zeros((tok, lanes), f32)
        for j in range(top):
            p = jnp.where(route[:, j : j + 1] == expert, gate[:, j : j + 1], p)
        high = p.astype(bf16).astype(f32)
        middle = (p - high).astype(bf16).astype(f32)
        low = p - high - middle
        side = jnp.where(part == 0, high, jnp.where(part == 1, middle, jnp.where(part == 2, low, 0.0)))
        for i, out in enumerate(outs):
            rows = slice(i * half, (i + 1) * half)
            out[:, :width] = tok_ref[rows, :]
            out[:, width : 2 * width] = cot_ref[rows, :]
            out[:, 2 * width :] = side[rows, :].astype(bf16)

    return pl.pallas_call(
        kernel,
        out_shape=[jax.ShapeDtypeStruct((half, 2 * width + lanes), bf16)] * 2,
        cost_estimate=pl.CostEstimate(flops=0, bytes_accessed=8 * tok * width, transcendentals=0),
    )(tokens, cotangent, gate_probs.T, routes.T)


NT = (((1,), (1,)), ((), ()))
TN = (((0,), (0,)), ((), ()))
hint = pl.CostEstimate(flops=1 << 20, bytes_accessed=1 << 16, transcendentals=0)


def expert_rows(rows, ids, full_in, full_out, ny, experts):
    width, n_ff = full_in.shape
    ff = n_ff // ny
    total = sum(part.shape[0] for part in rows)
    lanes = rows[0].shape[1] - 2 * width

    def kernel(id_ref, in_ref, out_ref, *refs):
        row_refs, (hid_ref, pre_ref, dx_ref, x_ref, c_ref, gate_ref) = refs[: len(rows)], refs[len(rows) :]
        at = 0
        for ref in row_refs:
            here = slice(at, at + ref.shape[0])
            at += ref.shape[0]
            x_ref[here, :] = ref[:, :width]
            c_ref[here, :] = ref[:, width : 2 * width]
            side = ref[:, 2 * width :].astype(f32)
            lane = lax.broadcasted_iota(jnp.int32, side.shape, 1)
            for r in range(ny):
                own = id_ref[r]
                named = (lane == own) | (lane == own + experts) | (lane == own + 2 * experts)
                p = jnp.sum(jnp.where(named, side, 0.0), axis=1, keepdims=True)
                gate_ref[here, r * 128 : (r + 1) * 128] = jnp.broadcast_to(p, (side.shape[0], 128))
        for t in range(0, n_ff, 256):
            cols = slice(t, min(t + 256, n_ff))
            pre = jnp.dot(x_ref[...], in_ref[:, cols], preferred_element_type=f32)
            back = lax.dot_general(c_ref[...], out_ref[cols, :], NT, preferred_element_type=f32)
            gates = [gate_ref[:, u // ff * 128 : u // ff * 128 + 128] for u in range(cols.start, cols.stop, 128)]
            gate = jnp.concatenate(gates, 1)
            sig = jax.nn.sigmoid(pre)
            hid_ref[:, cols] = (gate * pre * sig).astype(bf16)
            pre_ref[:, cols] = (gate * back * sig * (1.0 + pre * (1.0 - sig))).astype(bf16)
        for t in range(0, width, 512):
            cols = slice(t, min(t + 512, width))
            dx = lax.dot_general(pre_ref[...], in_ref[cols, :], NT, preferred_element_type=f32)
            dx_ref[:, cols] = dx.astype(bf16)

    need = 2 * (4 * width * n_ff + total * (6 * width + lanes + 2 * n_ff)) + 4 * total * (2 * width + ny * 128)
    return pl.pallas_call(
        kernel,
        in_specs=[pl.BlockSpec(memory_space=pltpu.SMEM)] + [pl.BlockSpec(memory_space=pltpu.VMEM)] * (2 + len(rows)),
        out_shape=[
            jax.ShapeDtypeStruct((total, n_ff), bf16),
            jax.ShapeDtypeStruct((total, n_ff), bf16),
            jax.ShapeDtypeStruct((total, width), bf16),
            jax.ShapeDtypeStruct((total, width), bf16),
            jax.ShapeDtypeStruct((total, width), bf16),
        ],
        scratch_shapes=[pltpu.VMEM((total, ny * 128), f32)],
        compiler_params=pltpu.CompilerParams(vmem_limit_bytes=min(need + (8 << 20), 58 << 20)),
        cost_estimate=hint,
    )(ids, full_in, full_out, *rows)


def per_device(tokens, cotangent, gate_probs, routes, w_in, w_out, mom_in, mom_out):
    n_data = lax.axis_size("dp")
    n = lax.axis_size("expert")
    ny = n_data // 2
    tok, width = tokens.shape
    half = tok // 2
    ff = w_in.shape[2]
    core = lax.axis_index("dp") % 2
    y_idx = lax.axis_index("dp") // 2
    ex = lax.axis_index("expert")
    lower = core == 0

    order = ring_order(n, ny)
    place = [order.index(i) for i in range(n)]

    def ring(x, step):
        return lax.ppermute(x, "expert", [(i, order[(place[i] + step) % n]) for i in range(n)])

    def swap_core(x):
        return lax.ppermute(x, "dp", [(i, i ^ 1) for i in range(n_data)])

    def shift_y(x, r):
        return lax.ppermute(x, "dp", [(i, (i // 2 + r) % ny * 2 + i % 2) for i in range(n_data)])

    experts = n * ny
    mine = pack(tokens, cotangent, gate_probs, routes, experts)
    ids = ex * ny + (y_idx + jnp.arange(ny, dtype=jnp.int32)) % ny

    far = n // 2
    got = {0: list(mine)}

    def pass_on(s):
        if s < far:
            got[-s] = [ring(part, 1) for part in got[1 - s]]
            got[s] = [ring(part, -1) for part in got[s - 1]]
        else:
            got[s] = [ring(got[1 - s][0], 1), ring(got[s - 1][1], -1)]

    def both(s):
        return got[-s] + got[s]

    def hold(s, *others):
        for d in (s, -s) if s < far else (s,):
            got[d] = [after(part, *others) for part in got[d]]

    def gather_in():
        full = jnp.zeros((width, ny * ff), bf16)
        rows = w_in.shape[1]
        for r in range(ny):
            own = shift_y(after(w_in[0], mine[0]), -r) if r else w_in[0]
            if r and far > 1:
                hold(1, own)
            other = swap_core(after(own, *both(1)) if far > 1 else own)
            for piece, at in ((own, core), (other, 1 - core)):
                full = lax.dynamic_update_slice(full, piece, (at * rows, r * ff))
        return full

    def gather_out():
        full = []
        for r in range(ny):
            own = w_out[0]
            if r:
                own = shift_y(after(own, *both(1)) if far > 1 else own, -r)
            own = after(own, *both(2)) if far > 2 else own
            other = swap_core(own)
            full += [jnp.where(lower, own, other), jnp.where(lower, other, own)]
        return jnp.concatenate(full, 0)

    if n <= 16:
        groups = [[0] + [d for t in range(1, far - 1) for d in (-t, t)], [d for d in (1 - far, far - 1) if d] + [far]]
    else:
        groups = [[0]]
        for s in range(1, far, n // 8):
            groups.append([d for t in range(s, min(s + n // 8, far)) for d in (-t, t)])
        groups.append([far])

    def within(step):
        return sum(max(group) <= step for group in groups)

    held, dxs = [], {}

    def work(group, full_in, full_out):
        tie = []
        if max(group) < far - 1 and far > 2:
            tie = both(far - 2) if n <= 16 else both(max(group) + 1)
        rows = [after(part, *tie) for d in group for part in got[d]]
        hid, d_pre, dx, x, c = expert_rows(rows, ids, full_in, full_out, ny, experts)
        for i, d in enumerate(group):
            dxs[d] = dx[i * tok : (i + 1) * tok]
        held.append((x, c, hid, d_pre))

    grads = {}

    def add_up(r, arrays, *others):
        x, c, hid, d_pre = arrays
        cols = slice(r * ff, (r + 1) * ff)
        for which, p, q in (("out", hid[:, cols], c), ("in", x, d_pre[:, cols])):
            g = lax.dot_general(after(p, *others), q, TN, preferred_element_type=f32)
            grads[which, r] = g + grads[which, r] if (which, r) in grads else g

    def to_core(r):
        for which in ("out", "in"):
            g = grads[which, r]
            rows = g.shape[0] // 2
            keep = lax.dynamic_slice_in_dim(g, core * rows, rows, 0)
            give = lax.dynamic_slice_in_dim(g, (1 - core) * rows, rows, 0).astype(bf16)
            sums[which, r] = keep + swap_core(give).astype(f32)

    sums = {}
    at_once = range(1, ny) if n <= 16 else range(ny)
    done = 0

    def work_up_to(count):
        nonlocal done
        while done < count:
            work(groups[done], after(full_in, *grads.values()), full_out)
            done += 1
            if done < len(groups):
                for r in at_once:
                    add_up(r, held[-1])
        return list(grads.values()) + list(dxs.values())

    for s in range(1, far + 1):
        if s == min(2, far):
            full_in = gather_in()
        if s == min(3, far):
            if far > 2:
                hold(2, full_in)
            full_out = gather_out()
        if s == far > 2 and n <= 16:
            hold(s - 1, *work_up_to(within(far - 2)))
        pass_on(s)

    hold(far, *work_up_to(len(groups) - 1))
    work_up_to(len(groups))
    for r in range(1, ny):
        add_up(r, held[-1])
        to_core(r)
        for which in ("out", "in"):
            sums[which, r] = sums[which, r].astype(bf16)

    count = max(1, min(3, far - 1))
    theirs = {key: [] for key in sums if key[1]}

    def piece(key, i):
        unit = -(-sums[key].shape[0] // (16 * count)) * 16
        return sums[key][i * unit : (i + 1) * unit]

    upper, under, ends = slice(0, half), slice(half, tok), []
    flows = [(1, upper, far), (-1, under, far)] + ([(1, under, far - 1), (-1, upper, far - 1)] if far > 1 else [])
    accs = [dxs[sign * d if d < far else d][rows].astype(bf16) for sign, rows, d in flows]
    for step in range(far):
        i = step - 1 if far > 1 else 0
        keys = list(theirs) if 0 <= i < count else []
        sent = [ring(acc, sign) for (sign, _, _), acc in zip(flows, accs)]
        moved = [shift_y(piece(key, i), key[1]) for key in keys]
        tied = [sums[key] for key in theirs] if step == 0 else []
        out = lax.optimization_barrier((sent, moved, tied))
        sent, moved = out[0], out[1]
        if step == 0:
            sums.update(zip(theirs, out[2]))
            for arrays in held if n <= 16 else held[-1:]:
                add_up(0, arrays, *sent)
            to_core(0)
        for key, part in zip(keys, moved):
            theirs[key].append(part)
        following, accs = [], []
        for (sign, rows, d), acc in zip(flows, sent):
            if d > 1:
                following.append((sign, rows, d - 1))
                accs.append((acc.astype(f32) + dxs[sign * (d - 1)][rows]).astype(bf16))
            else:
                ends.append((rows, acc))
        flows = following
    grad = {rows.start: dxs[0][rows].astype(f32) for rows in (upper, under)}
    for rows, acc in ends:
        grad[rows.start] = grad[rows.start] + acc.astype(f32)
    input_grad = jnp.concatenate([grad[0], grad[half]], 0).astype(bf16)

    new = {}
    for which, mom in (("out", mom_out), ("in", mom_in)):
        total = sums[which, 0]
        for r in range(1, ny):
            total = total + jnp.concatenate(theirs[which, r], 0).astype(f32)
        new[which] = (momentum_beta * mom[0] + total)[None]
    return (input_grad, new["in"], new["out"])


def solution(mesh):
    rows = P(("dp", "expert"), None)
    entries = P(("expert", "dp"), None, None)
    return jax.shard_map(
        per_device,
        mesh=mesh,
        in_specs=(rows,) * 4 + (entries,) * 4,
        out_specs=(rows, entries, entries),
        check_vma=False,
    )
```

time: 179 us -> 174 us (0.972)
  Pallas kernels: 0 us -> 21.7 us
  matrix products: 28.1 us -> 16.1 us
  local copies, waits for them, and re-layouts: 17.5 us -> 9.17 us
  waiting for transfers between devices: 80.4 us -> 74 us
    pallas_call x0 -> x3, Pallas kernels: none -> 21.7 us  [the longest x2 18.9 us: expert_rows(): pl.pallas_call(kernel, in_specs=[pl.BlockSpec(memory_space=pltpu.SMEM)] +...]
    ppermute x4 -> x8, waiting for transfers between devices: 21.9 us -> 9.61 us  [shift_y(): lax.ppermute(x, 'dp', [(i, (i // 2 + r) % ny * 2 + i % 2) for i in range(...]
    dot_general x23 -> x8, matrix products: 28.1 us -> 16.1 us  [add_up(): g = lax.dot_general(after(p, *others), q, TN, preferred_element_type=f32)]
    ppermute x30 -> x28, waiting for transfers between devices: 58.5 us -> 63.7 us  [ring(): lax.ppermute(x, 'expert', [(i, order[(place[i] + step) % n]) for i in ran...]
    ppermute x4 -> x8, starting transfers between devices: 5.32 us -> 9.76 us  [shift_y(): lax.ppermute(x, 'dp', [(i, (i // 2 + r) % ny * 2 + i % 2) for i in range(...]
    ppermute x30 -> x28, starting transfers between devices: 34.9 us -> 30.9 us  [ring(): lax.ppermute(x, 'expert', [(i, order[(place[i] + step) % n]) for i in ran...]
    unnamed x25 -> x38, local copies, waits for them, and re-layouts: 8.4 us -> 4.48 us
    concatenate x5 -> x0, local copies, waits for them, and re-layouts: 3.53 us -> none  [the longest x1 1.87 us: per_device(): cot_side = jnp.concatenate([cotangent, side.astype(bf16)], 1)]
  transfers between devices with their start and end apart: 42 -> 44, of which waited for: 16 -> 22; matrix products, arithmetic and copies ran while one was open for 25% -> 16% of each run, Pallas kernels for 0% -> 7%
where the time goes in v2:
time: 174 us
  waiting for transfers between devices  74 us (43%)
  starting transfers between devices  41.9 us (24%)
  Pallas kernels  21.7 us (12%)
  matrix products  16.1 us (9%)
  other arithmetic  10.1 us (6%)
  local copies, waits for them, and re-layouts  9.17 us (5%)
    ppermute x28, waiting for transfers between devices, ring(): lax.ppermute(x, 'expert', [(i, order[(place[i] + step) % n]) for i in ran...  63.7 us
    ppermute x28, starting transfers between devices, ring(): lax.ppermute(x, 'expert', [(i, order[(place[i] + step) % n]) for i in ran...  30.9 us
    pallas_call x2, Pallas kernels, expert_rows(): pl.pallas_call(kernel, in_specs=[pl.BlockSpec(memory_space=pltpu.SMEM)] +...  18.9 us
    dot_general x8, matrix products, add_up(): g = lax.dot_general(after(p, *others), q, TN, preferred_element_type=f32)  16.1 us
    ppermute x8, starting transfers between devices, shift_y(): lax.ppermute(x, 'dp', [(i, (i // 2 + r) % ny * 2 + i % 2) for i in range(...  9.76 us
    ppermute x8, waiting for transfers between devices, shift_y(): lax.ppermute(x, 'dp', [(i, (i // 2 + r) % ny * 2 + i % 2) for i in range(...  9.61 us
    unnamed x38, local copies, waits for them, and re-layouts  4.48 us
  transfers between devices with their start and end apart: 44, of which 22 were waited for; matrix products, arithmetic and copies ran while one was open for 16% of the time, Pallas kernels for 7%

profile of v2, /device:TPU:0, one launch (start us, length us, event | category | flops | bytes accessed | tf_op | source)
XLA Modules:
  0.0 174.1 jit_solution(18407016432966181855)
XLA Ops:
  0.6 2.7 %shard_map.103 = (bf16[64,4224]{1,0:T(8,128)(2,1)}, bf16[64,4224]{1,0:T(8,128)(2,1)}) custom-call(bf16[128,2048]{1,0:T(8,128)(2,1)} %tok_ref.1, bf16[128,2048]{1,0:T(8,128)(2,1)} %cot_ref.1, f32[8,128]{1,0:T(8,128)} %bitcast.31, s32[8,128]{1,0:T(8,128)} %bitcast.32), custom_call_target="tpu_custom_call" | custom-call | bytes 2097152 | tf_op jit(solution)/shard_map/pallas_call | solution.py:53
  3.3 3.0 %collective-permute-start.3 = (bf16[64,4224]{1,0:T(8,128)(2,1)}, bf16[64,4224]{1,0:T(8,128)(2,1)}, u32[]{:S(2)}, u32[]{:S(2)}) collective-permute-start(bf16[64,4224]{1,0:T(8,128)(2,1)} %get-tuple-element.89.refs_1_), channel_id=1, source_target_pairs={{0,2},{1,0},{2,4},{3,1},{4,6},{5,3},{6,7},{7,5},{8,10},{9,8},{10,1... | collective-permute-start | bytes 1622024 | tf_op jit(solution)/shard_map/ppermute | solution.py:133
  6.4 2.0 %collective-permute-start.2 = (bf16[64,4224]{1,0:T(8,128)(2,1)}, bf16[64,4224]{1,0:T(8,128)(2,1)}, u32[]{:S(2)}, u32[]{:S(2)}) collective-permute-start(bf16[64,4224]{1,0:T(8,128)(2,1)} %get-tuple-element.88.refs_0_), channel_id=1, source_target_pairs={{0,2},{1,0},{2,4},{3,1},{4,6},{5,3},{6,7},{7,5},{8,10},{9,8},{10,1... | collective-permute-start | bytes 1622024 | tf_op jit(solution)/shard_map/ppermute | solution.py:133
  8.4 2.0 %collective-permute-start.5 = (bf16[1024,384]{1,0:T(8,128)(2,1)}, bf16[1024,384]{1,0:T(8,128)(2,1)}, u32[]{:S(2)}, u32[]{:S(2)}) collective-permute-start(bf16[1024,384]{1,0:T(8,128)(2,1)} %bitcast.29), channel_id=1, source_target_pairs={{0,16},{8,24},{16,0},{24,8},{1,17},{9,25},{17,1},{25,9},{2,18},{10... | collective-permute-start | bytes 2359304 | tf_op jit(solution)/shard_map/ppermute | solution.py:139
  10.4 9.3 %collective-permute-done.3.refs_5_ = bf16[64,4224]{1,0:T(8,128)(2,1)} collective-permute-done((bf16[64,4224]{1,0:T(8,128)(2,1)}, bf16[64,4224]{1,0:T(8,128)(2,1)}, u32[]{:S(2)}, u32[]{:S(2)}) %collective-permute-start.3) | collective-permute-done | bytes 540704 | tf_op jit(solution)/shard_map/ppermute | solution.py:133
  19.7 2.2 %collective-permute-done.1.refs_3_ = bf16[64,4224]{1,0:T(8,128)(2,1)} collective-permute-done((bf16[64,4224]{1,0:T(8,128)(2,1)}, bf16[64,4224]{1,0:T(8,128)(2,1)}, u32[]{:S(2)}, u32[]{:S(2)}) %collective-permute-start.1) | collective-permute-done | bytes 540704 | tf_op jit(solution)/shard_map/ppermute | solution.py:133
  21.9 8.6 %collective-permute-done.2.refs_4_ = bf16[64,4224]{1,0:T(8,128)(2,1)} collective-permute-done((bf16[64,4224]{1,0:T(8,128)(2,1)}, bf16[64,4224]{1,0:T(8,128)(2,1)}, u32[]{:S(2)}, u32[]{:S(2)}) %collective-permute-start.2) | collective-permute-done | bytes 540704 | tf_op jit(solution)/shard_map/ppermute | solution.py:133
  30.5 1.5 collective-permute-done.refs_2_
  32.8 1.6 collective-permute-start.8
  34.9 0.7 collective-permute-done.4
  35.6 0.9 copy-done.13
  36.4 1.6 collective-permute-start.10
  38.4 0.7 copy-done.14
  39.3 1.6 collective-permute-start.12
  40.9 1.3 constant_dynamic-update-slice_fusion.3
  42.2 1.3 constant_dynamic-update-slice_fusion.2.in_ref
  43.5 16.5 %collective-permute-done.10.refs_9_ = bf16[64,4224]{1,0:T(8,128)(2,1)} collective-permute-done((bf16[64,4224]{1,0:T(8,128)(2,1)}, bf16[64,4224]{1,0:T(8,128)(2,1)}, u32[]{:S(2)}, u32[]{:S(2)}) %collective-permute-start.10) | collective-permute-done | bytes 540704 | tf_op jit(solution)/shard_map/ppermute | solution.py:133
  60.7 1.6 collective-permute-start.14
  62.3 1.6 collective-permute-start.15
  64.8 1.5 broadcast_select_fusion.3
  66.2 1.5 broadcast_select_fusion.1
  67.8 1.9 %pad_maximum_fusion.out_ref = bf16[768,2048]{1,0:T(8,128)(2,1)} fusion(bf16[192,2048]{1,0:T(8,128)(2,1)S(1)} %get-tuple-element.165, bf16[192,2048]{1,0:T(8,128)(2,1)S(1)} %get-tuple-element.164, bf16[192,2048]{1,0:T(8,128)(2,1)S(1)} %get-tuple-element.163, bf16[192,2048]{1,0:T(8,128)(2,1)S(1)} %get-tuple-element.162), kind=kLoop, calls=%fused_computation | loop fusion | flops 12582912 | bytes 6291456 | tf_op jit(solution)/shard_map/concatenate | solution.py:183
  69.6 12.8 %shard_map.104 = (bf16[640,768]{1,0:T(8,128)(2,1)S(1)}, bf16[640,768]{1,0:T(8,128)(2,1)}, bf16[640,2048]{1,0:T(8,128)(2,1)}, bf16[640,2048]{1,0:T(8,128)(2,1)}, bf16[640,2048]{1,0:T(8,128)(2,1)}) custom-call(s32[2]{0:T(128)S(1)} %fusion.8.id_ref, bf16[2048,768]{1,0:T(8,128)(2,1)} %copy-done.1, bf16[768,2048]{1,0:T(8,128)(2,1)} %pad_maximum_fusion.out_ref, ...), custom_call_target="tpu_custom_call" | custom-call | flops 1048576 | bytes 65536 | tf_op jit(solution)/shard_map/pallas_call | solution.py:101
  82.5 0.9 fusion.12
  83.4 5.1 %fusion.17 = f32[384,2048]{1,0:T(8,128)} fusion(bf16[640,384]{1,0:T(8,128)(2,1)S(1)} %get-tuple-element.167, bf16[640,2048]{1,0:T(8,128)(2,1)} %get-tuple-element.100), kind=kOutput, calls=%fused_computation.53 | convolution fusion | flops 1006632960 | bytes 6258688 | tf_op jit(solution)/shard_map/dot_general | solution.py:214
  88.5 3.5 %fusion.4 = f32[2048,384]{1,0:T(8,128)} fusion(bf16[640,2048]{1,0:T(8,128)(2,1)S(1)} %copy-done.15, bf16[640,768]{1,0:T(8,128)(2,1)S(1)} %copy-done.17), kind=kOutput, calls=%fused_computation.33 | convolution fusion | flops 1006632960 | bytes 6258688 | tf_op jit(solution)/shard_map/dot_general | solution.py:214
  91.9 1.6 collective-permute-start.18
  93.9 11.4 %collective-permute-done.18.refs_4_ = bf16[64,4224]{1,0:T(8,128)(2,1)} collective-permute-done((bf16[64,4224]{1,0:T(8,128)(2,1)}, bf16[64,4224]{1,0:T(8,128)(2,1)}, u32[]{:S(2)}, u32[]{:S(2)}) %collective-permute-start.18) | collective-permute-done | bytes 540704 | tf_op jit(solution)/shard_map/ppermute | solution.py:133
  105.4 1.3 collective-permute-done.19.refs_5_
  106.7 1.9 %copy-done.2 = bf16[2048,768]{1,0:T(8,128)(2,1)S(1)} copy-done((bf16[2048,768]{1,0:T(8,128)(2,1)S(1)}, bf16[2048,768]{1,0:T(8,128)(2,1)}, u32[]{:S(2)}) %copy-start.2) | copy-done | bytes 3145752
  108.6 6.1 %shard_map.105 = (bf16[384,768]{1,0:T(8,128)(2,1)S(1)}, bf16[384,768]{1,0:T(8,128)(2,1)S(1)}, bf16[384,2048]{1,0:T(8,128)(2,1)S(1)}, bf16[384,2048]{1,0:T(8,128)(2,1)S(1)}, bf16[384,2048]{1,0:T(8,128)(2,1)S(1)}) custom-call(s32[2]{0:T(128)S(1)} %fusion.8.id_ref, bf16[2048,768]{1,0:T(8,128)(2,1)S(1)} %copy-done.2, bf16[768,2048]{1,0:T(8,128)(2,1)S(1)} %copy-done, ...), custom_call_target="tpu_custom_call" | custom-call | flops 1048576 | bytes 65536 | tf_op jit(solution)/shard_map/pallas_call | solution.py:101
  114.8 1.0 convolution_add_fusion.2
  116.0 0.7 copy-done.7
  116.6 1.2 convolution_add_fusion.1
  118.6 1.6 collective-permute-start.22
  120.6 1.6 collective-permute-start.20
  122.7 4.5 %collective-permute-done.23 = bf16[64,2048]{1,0:T(8,128)(2,1)S(1)} collective-permute-done((bf16[64,2048]{1,0:T(8,128)(2,1)S(1)}, bf16[64,2048]{1,0:T(8,128)(2,1)S(1)}, u32[]{:S(2)}, u32[]{:S(2)}) %collective-permute-start.23) | collective-permute-done | bytes 262176 | tf_op jit(solution)/shard_map/ppermute | solution.py:133
  127.7 4.7 %collective-permute-done.21 = bf16[64,2048]{1,0:T(8,128)(2,1)S(1)} collective-permute-done((bf16[64,2048]{1,0:T(8,128)(2,1)S(1)}, bf16[64,2048]{1,0:T(8,128)(2,1)S(1)}, u32[]{:S(2)}, u32[]{:S(2)}) %collective-permute-start.21) | collective-permute-done | bytes 262176 | tf_op jit(solution)/shard_map/ppermute | solution.py:133
  133.1 1.6 collective-permute-start.30
  134.7 1.1 collective-permute-start.27
  135.8 0.9 collective-permute-start.26
  137.2 1.1 collective-permute-start.29
  138.3 1.7 fusion.2
  140.0 2.3 %collective-permute-done.30 = bf16[64,2048]{1,0:T(8,128)(2,1)S(1)} collective-permute-done((bf16[64,2048]{1,0:T(8,128)(2,1)S(1)}, bf16[64,2048]{1,0:T(8,128)(2,1)S(1)}, u32[]{:S(2)}, u32[]{:S(2)}) %collective-permute-start.30) | collective-permute-done | bytes 262176 | tf_op jit(solution)/shard_map/ppermute | solution.py:139
  142.4 1.6 collective-permute-start.28
  143.9 1.2 convolution_add_fusion
  145.3 1.6 collective-permute-start.36
  147.7 1.0 collective-permute-done.28
  149.1 1.3 collective-permute-start.35
  150.4 0.8 collective-permute-start.34
  151.2 1.3 collective-permute-start.33
  152.4 2.2 %collective-permute-done.36 = bf16[64,2048]{1,0:T(8,128)(2,1)S(1)} collective-permute-done((bf16[64,2048]{1,0:T(8,128)(2,1)S(1)}, bf16[64,2048]{1,0:T(8,128)(2,1)S(1)}, u32[]{:S(2)}, u32[]{:S(2)}) %collective-permute-start.36) | collective-permute-done | bytes 262176 | tf_op jit(solution)/shard_map/ppermute | solution.py:139
  154.7 1.6 collective-permute-start.32
  156.2 1.0 fusion.18
  157.2 0.8 collective-permute-done.37
  158.1 1.5 collective-permute-start.41
  160.3 1.0 collective-permute-done.32
  161.5 1.5 collective-permute-start.39
  163.5 1.4 fusion.16
  165.1 1.4 collective-permute-done.41
  166.5 2.8 %collective-permute-done.40 = bf16[64,2048]{1,0:T(8,128)(2,1)S(1)} collective-permute-done((bf16[64,2048]{1,0:T(8,128)(2,1)S(1)}, bf16[64,2048]{1,0:T(8,128)(2,1)S(1)}, u32[]{:S(2)}, u32[]{:S(2)}) %collective-permute-start.40) | collective-permute-done | bytes 262176 | tf_op jit(solution)/shard_map/ppermute | solution.py:139
  170.0 0.8 pad_maximum_fusion.1
  170.8 1.5 fusion.1
  172.5 1.6 fusion
  (102 shorter events, 10.9 us)
Async XLA Ops:
  3.3 16.4 %collective-permute-start.3 = (bf16[64,4224]{1,0:T(8,128)(2,1)}, bf16[64,4224]{1,0:T(8,128)(2,1)}, u32[]{:S(2)}, u32[]{:S(2)}) collective-permute-start(bf16[64,4224]{1,0:T(8,128)(2,1)} %get-tuple-element.89.refs_1_), channel_id=1, source_target_pairs={{0,2},{1,0},{2,4},{3,1},{4,6},{5,3},{6,7},{7,5},{8,10},{9,8},{10,1... | collective-permute-start | bytes 1622024 | tf_op jit(solution)/shard_map/ppermute | solution.py:133
  6.4 15.5 %collective-permute-start.1 = (bf16[64,4224]{1,0:T(8,128)(2,1)}, bf16[64,4224]{1,0:T(8,128)(2,1)}, u32[]{:S(2)}, u32[]{:S(2)}) collective-permute-start(bf16[64,4224]{1,0:T(8,128)(2,1)} %get-tuple-element.89.refs_1_), channel_id=1, source_target_pairs={{0,1},{1,3},{2,0},{3,5},{4,2},{5,7},{6,4},{7,6},{8,9},{9,11},{10,8... | collective-permute-start | bytes 1622024 | tf_op jit(solution)/shard_map/ppermute | solution.py:133
  6.4 24.1 %collective-permute-start.2 = (bf16[64,4224]{1,0:T(8,128)(2,1)}, bf16[64,4224]{1,0:T(8,128)(2,1)}, u32[]{:S(2)}, u32[]{:S(2)}) collective-permute-start(bf16[64,4224]{1,0:T(8,128)(2,1)} %get-tuple-element.88.refs_0_), channel_id=1, source_target_pairs={{0,2},{1,0},{2,4},{3,1},{4,6},{5,3},{6,7},{7,5},{8,10},{9,8},{10,1... | collective-permute-start | bytes 1622024 | tf_op jit(solution)/shard_map/ppermute | solution.py:133
  8.4 23.6 %collective-permute-start = (bf16[64,4224]{1,0:T(8,128)(2,1)}, bf16[64,4224]{1,0:T(8,128)(2,1)}, u32[]{:S(2)}, u32[]{:S(2)}) collective-permute-start(bf16[64,4224]{1,0:T(8,128)(2,1)} %get-tuple-element.88.refs_0_), channel_id=1, source_target_pairs={{0,1},{1,3},{2,0},{3,5},{4,2},{5,7},{6,4},{7,6},{8,9},{9,11},{10,8... | collective-permute-start | bytes 1622024 | tf_op jit(solution)/shard_map/ppermute | solution.py:133
  8.4 23.6 %collective-permute-start.5 = (bf16[1024,384]{1,0:T(8,128)(2,1)}, bf16[1024,384]{1,0:T(8,128)(2,1)}, u32[]{:S(2)}, u32[]{:S(2)}) collective-permute-start(bf16[1024,384]{1,0:T(8,128)(2,1)} %bitcast.29), channel_id=1, source_target_pairs={{0,16},{8,24},{16,0},{24,8},{1,17},{9,25},{17,1},{25,9},{2,18},{10... | collective-permute-start | bytes 2359304 | tf_op jit(solution)/shard_map/ppermute | solution.py:139
  32.0 3.5 %collective-permute-start.4 = (bf16[1024,384]{1,0:T(8,128)(2,1)}, bf16[1024,384]{1,0:T(8,128)(2,1)S(1)}, u32[]{:S(2)}, u32[]{:S(2)}) collective-permute-start(bf16[1024,384]{1,0:T(8,128)(2,1)} %bitcast.30), channel_id=1, source_target_pairs={{0,8},{8,0},{16,24},{24,16},{1,9},{9,1},{17,25},{25,17},{2,10},{10... | collective-permute-start | bytes 2359304 | tf_op jit(solution)/shard_map/ppermute | solution.py:136
  32.0 7.3 %collective-permute-start.6 = (bf16[1024,384]{1,0:T(8,128)(2,1)}, bf16[1024,384]{1,0:T(8,128)(2,1)}, u32[]{:S(2)}, u32[]{:S(2)}) collective-permute-start(bf16[1024,384]{1,0:T(8,128)(2,1)} %collective-permute-done.5), channel_id=1, source_target_pairs={{0,8},{8,0},{16,24},{24,16},{1,9},{9,1},{17,25},{25,17},{2,10},{10... | collective-permute-start | bytes 2359304 | tf_op jit(solution)/shard_map/ppermute | solution.py:136
  32.5 5.7 %copy-start.12 = (bf16[1,1024,384]{2,1,0:T(8,128)(2,1)S(1)}, bf16[1,1024,384]{2,1,0:T(8,128)(2,1)}, u32[]{:S(2)}) copy-start(bf16[1,1024,384]{2,1,0:T(8,128)(2,1)} %param.12) | copy-start | bytes 2359300
  32.5 27.5 %collective-permute-start.7 = (bf16[64,4224]{1,0:T(8,128)(2,1)}, bf16[64,4224]{1,0:T(8,128)(2,1)}, u32[]{:S(2)}, u32[]{:S(2)}) collective-permute-start(bf16[64,4224]{1,0:T(8,128)(2,1)} %collective-permute-done.refs_2_), channel_id=1, source_target_pairs={{0,1},{1,3},{2,0},{3,5},{4,2},{5,7},{6,4},{7,6},{8,9},{9,11},{10,8... | collective-permute-start | bytes 1622024 | tf_op jit(solution)/shard_map/ppermute | solution.py:133
  32.8 27.2 %collective-permute-start.8 = (bf16[64,4224]{1,0:T(8,128)(2,1)}, bf16[64,4224]{1,0:T(8,128)(2,1)}, u32[]{:S(2)}, u32[]{:S(2)}) collective-permute-start(bf16[64,4224]{1,0:T(8,128)(2,1)} %collective-permute-done.1.refs_3_), channel_id=1, source_target_pairs={{0,1},{1,3},{2,0},{3,5},{4,2},{5,7},{6,4},{7,6},{8,9},{9,11},{10,8... | collective-permute-start | bytes 1622024 | tf_op jit(solution)/shard_map/ppermute | solution.py:133
  34.5 25.6 %collective-permute-start.9 = (bf16[64,4224]{1,0:T(8,128)(2,1)}, bf16[64,4224]{1,0:T(8,128)(2,1)}, u32[]{:S(2)}, u32[]{:S(2)}) collective-permute-start(bf16[64,4224]{1,0:T(8,128)(2,1)} %collective-permute-done.2.refs_4_), channel_id=1, source_target_pairs={{0,2},{1,0},{2,4},{3,1},{4,6},{5,3},{6,7},{7,5},{8,10},{9,8},{10,1... | collective-permute-start | bytes 1622024 | tf_op jit(solution)/shard_map/ppermute | solution.py:133
  35.6 0.9 copy-start.13
  36.4 23.6 %collective-permute-start.10 = (bf16[64,4224]{1,0:T(8,128)(2,1)}, bf16[64,4224]{1,0:T(8,128)(2,1)}, u32[]{:S(2)}, u32[]{:S(2)}) collective-permute-start(bf16[64,4224]{1,0:T(8,128)(2,1)} %collective-permute-done.3.refs_5_), channel_id=1, source_target_pairs={{0,2},{1,0},{2,4},{3,1},{4,6},{5,3},{6,7},{7,5},{8,10},{9,8},{10,1... | collective-permute-start | bytes 1622024 | tf_op jit(solution)/shard_map/ppermute | solution.py:133
  38.0 1.1 copy-start.14
  39.3 20.8 %collective-permute-start.12 = (bf16[192,2048]{1,0:T(8,128)(2,1)}, bf16[192,2048]{1,0:T(8,128)(2,1)}, u32[]{:S(2)}, u32[]{:S(2)}) collective-permute-start(bf16[192,2048]{1,0:T(8,128)(2,1)} %bitcast.3), channel_id=1, source_target_pairs={{0,16},{8,24},{16,0},{24,8},{1,17},{9,25},{17,1},{25,9},{2,18},{10... | collective-permute-start | bytes 2359304 | tf_op jit(solution)/shard_map/ppermute | solution.py:139
  43.5 24.2 %copy-start.1 = (bf16[2048,768]{1,0:T(8,128)(2,1)}, bf16[2048,768]{1,0:T(8,128)(2,1)S(1)}, u32[]{:S(2)}) copy-start(bf16[2048,768]{1,0:T(8,128)(2,1)S(1)} %constant_dynamic-update-slice_fusion.2.in_ref) | copy-start | bytes 9437188
  60.1 4.2 %collective-permute-start.11 = (bf16[192,2048]{1,0:T(8,128)(2,1)}, bf16[192,2048]{1,0:T(8,128)(2,1)}, u32[]{:S(2)}, u32[]{:S(2)}) collective-permute-start(bf16[192,2048]{1,0:T(8,128)(2,1)} %bitcast.3), channel_id=1, source_target_pairs={{0,8},{8,0},{16,24},{24,16},{1,9},{9,1},{17,25},{25,17},{2,10},{10... | collective-permute-start | bytes 2359304 | tf_op jit(solution)/shard_map/ppermute | solution.py:136
  60.2 6.1 %collective-permute-start.13 = (bf16[192,2048]{1,0:T(8,128)(2,1)}, bf16[192,2048]{1,0:T(8,128)(2,1)}, u32[]{:S(2)}, u32[]{:S(2)}) collective-permute-start(bf16[192,2048]{1,0:T(8,128)(2,1)} %collective-permute-done.12), channel_id=1, source_target_pairs={{0,8},{8,0},{16,24},{24,16},{1,9},{9,1},{17,25},{25,17},{2,10},{10... | collective-permute-start | bytes 2359304 | tf_op jit(solution)/shard_map/ppermute | solution.py:136
  60.7 31.3 %collective-permute-start.14 = (bf16[64,4224]{1,0:T(8,128)(2,1)}, bf16[64,4224]{1,0:T(8,128)(2,1)}, u32[]{:S(2)}, u32[]{:S(2)}) collective-permute-start(bf16[64,4224]{1,0:T(8,128)(2,1)} %collective-permute-done.7.refs_6_), channel_id=1, source_target_pairs={{0,1},{1,3},{2,0},{3,5},{4,2},{5,7},{6,4},{7,6},{8,9},{9,11},{10,8... | collective-permute-start | bytes 1622024 | tf_op jit(solution)/shard_map/ppermute | solution.py:133
  62.3 31.7 %collective-permute-start.15 = (bf16[64,4224]{1,0:T(8,128)(2,1)}, bf16[64,4224]{1,0:T(8,128)(2,1)}, u32[]{:S(2)}, u32[]{:S(2)}) collective-permute-start(bf16[64,4224]{1,0:T(8,128)(2,1)} %collective-permute-done.8.refs_7_), channel_id=1, source_target_pairs={{0,1},{1,3},{2,0},{3,5},{4,2},{5,7},{6,4},{7,6},{8,9},{9,11},{10,8... | collective-permute-start | bytes 1622024 | tf_op jit(solution)/shard_map/ppermute | solution.py:133
  63.8 30.1 %collective-permute-start.16 = (bf16[64,4224]{1,0:T(8,128)(2,1)}, bf16[64,4224]{1,0:T(8,128)(2,1)}, u32[]{:S(2)}, u32[]{:S(2)}) collective-permute-start(bf16[64,4224]{1,0:T(8,128)(2,1)} %collective-permute-done.9.refs_8_), channel_id=1, source_target_pairs={{0,2},{1,0},{2,4},{3,1},{4,6},{5,3},{6,7},{7,5},{8,10},{9,8},{10,1... | collective-permute-start | bytes 1622024 | tf_op jit(solution)/shard_map/ppermute | solution.py:133
  64.3 29.2 %collective-permute-start.17 = (bf16[64,4224]{1,0:T(8,128)(2,1)}, bf16[64,4224]{1,0:T(8,128)(2,1)}, u32[]{:S(2)}, u32[]{:S(2)}) collective-permute-start(bf16[64,4224]{1,0:T(8,128)(2,1)} %collective-permute-done.10.refs_9_), channel_id=1, source_target_pairs={{0,2},{1,0},{2,4},{3,1},{4,6},{5,3},{6,7},{7,5},{8,10},{9,8},{10,1... | collective-permute-start | bytes 1622024 | tf_op jit(solution)/shard_map/ppermute | solution.py:133
  67.7 1.9 %copy-start.3 = (bf16[64,4224]{1,0:T(8,128)(2,1)S(1)}, bf16[64,4224]{1,0:T(8,128)(2,1)}, u32[]{:S(2)}) copy-start(bf16[64,4224]{1,0:T(8,128)(2,1)} %get-tuple-element.88.refs_0_) | copy-start | bytes 1622020
  67.7 1.9 %copy-start.4 = (bf16[64,4224]{1,0:T(8,128)(2,1)S(1)}, bf16[64,4224]{1,0:T(8,128)(2,1)}, u32[]{:S(2)}) copy-start(bf16[64,4224]{1,0:T(8,128)(2,1)} %get-tuple-element.89.refs_1_) | copy-start | bytes 1622020
  83.3 5.1 %copy-start.15 = (bf16[640,2048]{1,0:T(8,128)(2,1)S(1)}, bf16[640,2048]{1,0:T(8,128)(2,1)}, u32[]{:S(2)}) copy-start(bf16[640,2048]{1,0:T(8,128)(2,1)} %get-tuple-element.132) | copy-start | bytes 7864324
  83.3 5.1 %copy-start.17 = (bf16[640,768]{1,0:T(8,128)(2,1)S(1)}, bf16[640,768]{1,0:T(8,128)(2,1)}, u32[]{:S(2)}) copy-start(bf16[640,768]{1,0:T(8,128)(2,1)} %get-tuple-element.102) | copy-start | bytes 2949124
  88.4 18.2 %copy-start = (bf16[768,2048]{1,0:T(8,128)(2,1)S(1)}, bf16[768,2048]{1,0:T(8,128)(2,1)}, u32[]{:S(2)}) copy-start(bf16[768,2048]{1,0:T(8,128)(2,1)} %pad_maximum_fusion.out_ref) | copy-start | bytes 9437188
  91.9 13.5 %collective-permute-start.18 = (bf16[64,4224]{1,0:T(8,128)(2,1)}, bf16[64,4224]{1,0:T(8,128)(2,1)}, u32[]{:S(2)}, u32[]{:S(2)}) collective-permute-start(bf16[64,4224]{1,0:T(8,128)(2,1)} %collective-permute-done.14.refs_0_), channel_id=1, source_target_pairs={{0,1},{1,3},{2,0},{3,5},{4,2},{5,7},{6,4},{7,6},{8,9},{9,11},{10,8... | collective-permute-start | bytes 1622024 | tf_op jit(solution)/shard_map/ppermute | solution.py:133
  93.5 13.2 %collective-permute-start.19 = (bf16[64,4224]{1,0:T(8,128)(2,1)}, bf16[64,4224]{1,0:T(8,128)(2,1)}, u32[]{:S(2)}, u32[]{:S(2)}) collective-permute-start(bf16[64,4224]{1,0:T(8,128)(2,1)} %collective-permute-done.17.refs_3_), channel_id=1, source_target_pairs={{0,2},{1,0},{2,4},{3,1},{4,6},{5,3},{6,7},{7,5},{8,10},{9,8},{10,1... | collective-permute-start | bytes 1622024 | tf_op jit(solution)/shard_map/ppermute | solution.py:133
  106.7 1.9 %copy-start.2 = (bf16[2048,768]{1,0:T(8,128)(2,1)S(1)}, bf16[2048,768]{1,0:T(8,128)(2,1)}, u32[]{:S(2)}) copy-start(bf16[2048,768]{1,0:T(8,128)(2,1)} %copy-done.1) | copy-start | bytes 9437188
  108.6 6.2 %copy-start.5 = (f32[384,2048]{1,0:T(8,128)S(1)}, f32[384,2048]{1,0:T(8,128)}, u32[]{:S(2)}) copy-start(f32[384,2048]{1,0:T(8,128)} %fusion.17) | copy-start | bytes 9437188
  114.8 1.9 %copy-start.7 = (f32[2048,384]{1,0:T(8,128)S(1)}, f32[2048,384]{1,0:T(8,128)}, u32[]{:S(2)}) copy-start(f32[2048,384]{1,0:T(8,128)} %fusion.4) | copy-start | bytes 9437188
  115.9 4.7 %collective-permute-start.24 = (bf16[192,2048]{1,0:T(8,128)(2,1)S(1)}, bf16[192,2048]{1,0:T(8,128)(2,1)S(1)}, u32[]{:S(2)}, u32[]{:S(2)}) collective-permute-start(bf16[192,2048]{1,0:T(8,128)(2,1)S(1)} %dynamic-slice_convert_fusion.3), channel_id=1, source_target_pairs={{0,8},{8,0},{16,24},{24,16},{1,9},{9,1},{17,25},{25,17},{2,10},{10... | collective-permute-start | bytes 2359304 | tf_op jit(solution)/shard_map/ppermute | solution.py:136
  117.9 4.5 %collective-permute-start.25 = (bf16[1024,384]{1,0:T(8,128)(2,1)S(1)}, bf16[1024,384]{1,0:T(8,128)(2,1)S(1)}, u32[]{:S(2)}, u32[]{:S(2)}) collective-permute-start(bf16[1024,384]{1,0:T(8,128)(2,1)S(1)} %dynamic-slice_convert_fusion.2), channel_id=1, source_target_pairs={{0,8},{8,0},{16,24},{24,16},{1,9},{9,1},{17,25},{25,17},{2,10},{10... | collective-permute-start | bytes 2359304 | tf_op jit(solution)/shard_map/ppermute | solution.py:136
  118.1 9.2 %collective-permute-start.23 = (bf16[64,2048]{1,0:T(8,128)(2,1)S(1)}, bf16[64,2048]{1,0:T(8,128)(2,1)S(1)}, u32[]{:S(2)}, u32[]{:S(2)}) collective-permute-start(bf16[64,2048]{1,0:T(8,128)(2,1)S(1)} %get-tuple-element.158), channel_id=1, source_target_pairs={{0,2},{1,0},{2,4},{3,1},{4,6},{5,3},{6,7},{7,5},{8,10},{9,8},{10,1... | collective-permute-start | bytes 786440 | tf_op jit(solution)/shard_map/ppermute | solution.py:133
  118.6 9.1 %collective-permute-start.22 = (bf16[64,2048]{1,0:T(8,128)(2,1)S(1)}, bf16[64,2048]{1,0:T(8,128)(2,1)S(1)}, u32[]{:S(2)}, u32[]{:S(2)}) collective-permute-start(bf16[64,2048]{1,0:T(8,128)(2,1)S(1)} %get-tuple-element.159), channel_id=1, source_target_pairs={{0,1},{1,3},{2,0},{3,5},{4,2},{5,7},{6,4},{7,6},{8,9},{9,11},{10,8... | collective-permute-start | bytes 786440 | tf_op jit(solution)/shard_map/ppermute | solution.py:133
  120.2 12.3 %collective-permute-start.21 = (bf16[64,2048]{1,0:T(8,128)(2,1)S(1)}, bf16[64,2048]{1,0:T(8,128)(2,1)S(1)}, u32[]{:S(2)}, u32[]{:S(2)}) collective-permute-start(bf16[64,2048]{1,0:T(8,128)(2,1)S(1)} %get-tuple-element.160), channel_id=1, source_target_pairs={{0,2},{1,0},{2,4},{3,1},{4,6},{5,3},{6,7},{7,5},{8,10},{9,8},{10,1... | collective-permute-start | bytes 786440 | tf_op jit(solution)/shard_map/ppermute | solution.py:133
  120.6 12.0 %collective-permute-start.20 = (bf16[64,2048]{1,0:T(8,128)(2,1)S(1)}, bf16[64,2048]{1,0:T(8,128)(2,1)S(1)}, u32[]{:S(2)}, u32[]{:S(2)}) collective-permute-start(bf16[64,2048]{1,0:T(8,128)(2,1)S(1)} %get-tuple-element.161), channel_id=1, source_target_pairs={{0,1},{1,3},{2,0},{3,5},{4,2},{5,7},{6,4},{7,6},{8,9},{9,11},{10,8... | collective-permute-start | bytes 786440 | tf_op jit(solution)/shard_map/ppermute | solution.py:133
  122.5 10.3 %copy-start.8 = (bf16[640,2048]{1,0:T(8,128)(2,1)S(1)}, bf16[640,2048]{1,0:T(8,128)(2,1)}, u32[]{:S(2)}) copy-start(bf16[640,2048]{1,0:T(8,128)(2,1)} %get-tuple-element.98) | copy-start | bytes 7864324
  122.7 15.6 %copy-start.16 = (bf16[640,2048]{1,0:T(8,128)(2,1)S(1)}, bf16[640,2048]{1,0:T(8,128)(2,1)}, u32[]{:S(2)}) copy-start(bf16[640,2048]{1,0:T(8,128)(2,1)} %get-tuple-element.132) | copy-start | bytes 7864324
  122.7 15.6 %copy-start.18 = (bf16[640,768]{1,0:T(8,128)(2,1)S(1)}, bf16[640,768]{1,0:T(8,128)(2,1)}, u32[]{:S(2)}) copy-start(bf16[640,768]{1,0:T(8,128)(2,1)} %get-tuple-element.102) | copy-start | bytes 2949124
  133.1 9.3 %collective-permute-start.30 = (bf16[64,2048]{1,0:T(8,128)(2,1)S(1)}, bf16[64,2048]{1,0:T(8,128)(2,1)S(1)}, u32[]{:S(2)}, u32[]{:S(2)}) collective-permute-start(bf16[64,2048]{1,0:T(8,128)(2,1)S(1)} %get-tuple-element.170), channel_id=1, source_target_pairs={{0,16},{8,24},{16,0},{24,8},{1,17},{9,25},{17,1},{25,9},{2,18},{10... | collective-permute-start | bytes 786440 | tf_op jit(solution)/shard_map/ppermute | solution.py:139
  134.7 10.7 %collective-permute-start.27 = (bf16[64,2048]{1,0:T(8,128)(2,1)S(1)}, bf16[64,2048]{1,0:T(8,128)(2,1)S(1)}, u32[]{:S(2)}, u32[]{:S(2)}) collective-permute-start(bf16[64,2048]{1,0:T(8,128)(2,1)S(1)} %get-tuple-element.156), channel_id=1, source_target_pairs={{0,2},{1,0},{2,4},{3,1},{4,6},{5,3},{6,7},{7,5},{8,10},{9,8},{10,1... | collective-permute-start | bytes 786440 | tf_op jit(solution)/shard_map/ppermute | solution.py:133
  135.8 11.2 %collective-permute-start.26 = (bf16[64,2048]{1,0:T(8,128)(2,1)S(1)}, bf16[64,2048]{1,0:T(8,128)(2,1)S(1)}, u32[]{:S(2)}, u32[]{:S(2)}) collective-permute-start(bf16[64,2048]{1,0:T(8,128)(2,1)S(1)} %get-tuple-element.157), channel_id=1, source_target_pairs={{0,1},{1,3},{2,0},{3,5},{4,2},{5,7},{6,4},{7,6},{8,9},{9,11},{10,8... | collective-permute-start | bytes 786440 | tf_op jit(solution)/shard_map/ppermute | solution.py:133
  136.7 12.1 %collective-permute-start.31 = (bf16[352,384]{1,0:T(8,128)(2,1)S(1)}, bf16[352,384]{1,0:T(8,128)(2,1)S(1)}, u32[]{:S(2)}, u32[]{:S(2)}) collective-permute-start(bf16[352,384]{1,0:T(8,128)(2,1)S(1)} %get-tuple-element.172), channel_id=1, source_target_pairs={{0,16},{8,24},{16,0},{24,8},{1,17},{9,25},{17,1},{25,9},{2,18},{10... | collective-permute-start | bytes 811016 | tf_op jit(solution)/shard_map/ppermute | solution.py:139
  137.2 10.6 %collective-permute-start.29 = (bf16[64,2048]{1,0:T(8,128)(2,1)S(1)}, bf16[64,2048]{1,0:T(8,128)(2,1)S(1)}, u32[]{:S(2)}, u32[]{:S(2)}) collective-permute-start(bf16[64,2048]{1,0:T(8,128)(2,1)S(1)} %get-tuple-element.149), channel_id=1, source_target_pairs={{0,2},{1,0},{2,4},{3,1},{4,6},{5,3},{6,7},{7,5},{8,10},{9,8},{10,1... | collective-permute-start | bytes 786440 | tf_op jit(solution)/shard_map/ppermute | solution.py:133
  142.4 6.4 %collective-permute-start.28 = (bf16[64,2048]{1,0:T(8,128)(2,1)S(1)}, bf16[64,2048]{1,0:T(8,128)(2,1)S(1)}, u32[]{:S(2)}, u32[]{:S(2)}) collective-permute-start(bf16[64,2048]{1,0:T(8,128)(2,1)S(1)} %get-tuple-element.150), channel_id=1, source_target_pairs={{0,1},{1,3},{2,0},{3,5},{4,2},{5,7},{6,4},{7,6},{8,9},{9,11},{10,8... | collective-permute-start | bytes 786440 | tf_op jit(solution)/shard_map/ppermute | solution.py:133
  145.3 9.3 %collective-permute-start.36 = (bf16[64,2048]{1,0:T(8,128)(2,1)S(1)}, bf16[64,2048]{1,0:T(8,128)(2,1)S(1)}, u32[]{:S(2)}, u32[]{:S(2)}) collective-permute-start(bf16[64,2048]{1,0:T(8,128)(2,1)S(1)} %get-tuple-element.169), channel_id=1, source_target_pairs={{0,16},{8,24},{16,0},{24,8},{1,17},{9,25},{17,1},{25,9},{2,18},{10... | collective-permute-start | bytes 786440 | tf_op jit(solution)/shard_map/ppermute | solution.py:139
  146.9 11.2 %collective-permute-start.37 = (bf16[352,384]{1,0:T(8,128)(2,1)S(1)}, bf16[352,384]{1,0:T(8,128)(2,1)S(1)}, u32[]{:S(2)}, u32[]{:S(2)}) collective-permute-start(bf16[352,384]{1,0:T(8,128)(2,1)S(1)} %get-tuple-element.171), channel_id=1, source_target_pairs={{0,16},{8,24},{16,0},{24,8},{1,17},{9,25},{17,1},{25,9},{2,18},{10... | collective-permute-start | bytes 811016 | tf_op jit(solution)/shard_map/ppermute | solution.py:139
  149.1 10.5 %collective-permute-start.35 = (bf16[64,2048]{1,0:T(8,128)(2,1)S(1)}, bf16[64,2048]{1,0:T(8,128)(2,1)S(1)}, u32[]{:S(2)}, u32[]{:S(2)}) collective-permute-start(bf16[64,2048]{1,0:T(8,128)(2,1)S(1)} %get-tuple-element.145), channel_id=1, source_target_pairs={{0,2},{1,0},{2,4},{3,1},{4,6},{5,3},{6,7},{7,5},{8,10},{9,8},{10,1... | collective-permute-start | bytes 786440 | tf_op jit(solution)/shard_map/ppermute | solution.py:133
  150.4 9.7 %collective-permute-start.34 = (bf16[64,2048]{1,0:T(8,128)(2,1)S(1)}, bf16[64,2048]{1,0:T(8,128)(2,1)S(1)}, u32[]{:S(2)}, u32[]{:S(2)}) collective-permute-start(bf16[64,2048]{1,0:T(8,128)(2,1)S(1)} %get-tuple-element.146), channel_id=1, source_target_pairs={{0,1},{1,3},{2,0},{3,5},{4,2},{5,7},{6,4},{7,6},{8,9},{9,11},{10,8... | collective-permute-start | bytes 786440 | tf_op jit(solution)/shard_map/ppermute | solution.py:133
  151.2 9.2 %collective-permute-start.33 = (bf16[64,2048]{1,0:T(8,128)(2,1)S(1)}, bf16[64,2048]{1,0:T(8,128)(2,1)S(1)}, u32[]{:S(2)}, u32[]{:S(2)}) collective-permute-start(bf16[64,2048]{1,0:T(8,128)(2,1)S(1)} %get-tuple-element.147), channel_id=1, source_target_pairs={{0,2},{1,0},{2,4},{3,1},{4,6},{5,3},{6,7},{7,5},{8,10},{9,8},{10,1... | collective-permute-start | bytes 786440 | tf_op jit(solution)/shard_map/ppermute | solution.py:133
  154.7 8.9 %copy-start.6 = (bf16[640,2048]{1,0:T(8,128)(2,1)S(1)}, bf16[640,2048]{1,0:T(8,128)(2,1)}, u32[]{:S(2)}) copy-start(bf16[640,2048]{1,0:T(8,128)(2,1)} %get-tuple-element.100) | copy-start | bytes 7864324
  154.7 8.9 %copy-start.9 = (bf16[640,384]{1,0:T(8,128)(2,1)S(1)}, bf16[640,384]{1,0:T(8,128)(2,1)}, u32[]{:S(2)}) copy-start(bf16[640,384]{1,0:T(8,128)(2,1)} %get-tuple-element.137) | copy-start | bytes 1474564
  154.7 6.7 %collective-permute-start.32 = (bf16[64,2048]{1,0:T(8,128)(2,1)S(1)}, bf16[64,2048]{1,0:T(8,128)(2,1)S(1)}, u32[]{:S(2)}, u32[]{:S(2)}) collective-permute-start(bf16[64,2048]{1,0:T(8,128)(2,1)S(1)} %get-tuple-element.148), channel_id=1, source_target_pairs={{0,1},{1,3},{2,0},{3,5},{4,2},{5,7},{6,4},{7,6},{8,9},{9,11},{10,8... | collective-permute-start | bytes 786440 | tf_op jit(solution)/shard_map/ppermute | solution.py:133
  158.1 8.4 %collective-permute-start.41 = (bf16[320,384]{1,0:T(8,128)(2,1)S(1)}, bf16[320,384]{1,0:T(8,128)(2,1)S(1)}, u32[]{:S(2)}, u32[]{:S(2)}) collective-permute-start(bf16[320,384]{1,0:T(8,128)(2,1)S(1)} %slice.153), channel_id=1, source_target_pairs={{0,16},{8,24},{16,0},{24,8},{1,17},{9,25},{17,1},{25,9},{2,18},{10... | collective-permute-start | bytes 737288 | tf_op jit(solution)/shard_map/ppermute | solution.py:139
  159.6 9.7 %collective-permute-start.40 = (bf16[64,2048]{1,0:T(8,128)(2,1)S(1)}, bf16[64,2048]{1,0:T(8,128)(2,1)S(1)}, u32[]{:S(2)}, u32[]{:S(2)}) collective-permute-start(bf16[64,2048]{1,0:T(8,128)(2,1)S(1)} %get-tuple-element.168), channel_id=1, source_target_pairs={{0,16},{8,24},{16,0},{24,8},{1,17},{9,25},{17,1},{25,9},{2,18},{10... | collective-permute-start | bytes 786440 | tf_op jit(solution)/shard_map/ppermute | solution.py:139
  160.1 10.7 %collective-permute-start.42 = (bf16[1024,384]{1,0:T(8,128)(2,1)S(1)}, bf16[1024,384]{1,0:T(8,128)(2,1)S(1)}, u32[]{:S(2)}, u32[]{:S(2)}) collective-permute-start(bf16[1024,384]{1,0:T(8,128)(2,1)S(1)} %dynamic-slice_convert_fusion.1), channel_id=1, source_target_pairs={{0,8},{8,0},{16,24},{24,16},{1,9},{9,1},{17,25},{25,17},{2,10},{10... | collective-permute-start | bytes 2359304 | tf_op jit(solution)/shard_map/ppermute | solution.py:136
  161.5 7.9 %collective-permute-start.39 = (bf16[64,2048]{1,0:T(8,128)(2,1)S(1)}, bf16[64,2048]{1,0:T(8,128)(2,1)S(1)}, u32[]{:S(2)}, u32[]{:S(2)}) collective-permute-start(bf16[64,2048]{1,0:T(8,128)(2,1)S(1)} %get-tuple-element.143), channel_id=1, source_target_pairs={{0,2},{1,0},{2,4},{3,1},{4,6},{5,3},{6,7},{7,5},{8,10},{9,8},{10,1... | collective-permute-start | bytes 786440 | tf_op jit(solution)/shard_map/ppermute | solution.py:133
  162.9 6.8 %collective-permute-start.38 = (bf16[64,2048]{1,0:T(8,128)(2,1)S(1)}, bf16[64,2048]{1,0:T(8,128)(2,1)S(1)}, u32[]{:S(2)}, u32[]{:S(2)}) collective-permute-start(bf16[64,2048]{1,0:T(8,128)(2,1)S(1)} %get-tuple-element.144), channel_id=1, source_target_pairs={{0,1},{1,3},{2,0},{3,5},{4,2},{5,7},{6,4},{7,6},{8,9},{9,11},{10,8... | collective-permute-start | bytes 786440 | tf_op jit(solution)/shard_map/ppermute | solution.py:133
  165.0 5.8 %copy-start.10 = (f32[1,1024,384]{2,1,0:T(8,128)S(1)}, f32[1,1024,384]{2,1,0:T(8,128)}, u32[]{:S(2)}) copy-start(f32[1,1024,384]{2,1,0:T(8,128)} %param.14) | copy-start | bytes 4718596
  166.5 5.8 %collective-permute-start.43 = (bf16[192,2048]{1,0:T(8,128)(2,1)S(1)}, bf16[192,2048]{1,0:T(8,128)(2,1)S(1)}, u32[]{:S(2)}, u32[]{:S(2)}) collective-permute-start(bf16[192,2048]{1,0:T(8,128)(2,1)S(1)} %dynamic-slice_convert_fusion), channel_id=1, source_target_pairs={{0,8},{8,0},{16,24},{24,16},{1,9},{9,1},{17,25},{25,17},{2,10},{10... | collective-permute-start | bytes 2359304 | tf_op jit(solution)/shard_map/ppermute | solution.py:136
  170.8 1.7 copy-start.11

commit v3 on v2

--- a/solution.py
+++ b/solution.py
@@ -147,8 +147,9 @@
 
     def pass_on(s):
         if s < far:
-            got[-s] = [ring(part, 1) for part in got[1 - s]]
-            got[s] = [ring(part, -1) for part in got[s - 1]]
+            (fwd, fwd_late), (bwd_late, bwd) = got[1 - s], got[s - 1]
+            fwd_late, bwd_late = ring(fwd_late, 1), ring(bwd_late, -1)
+            got[-s], got[s] = [ring(fwd, 1), fwd_late], [bwd_late, ring(bwd, -1)]
         else:
             got[s] = [ring(got[1 - s][0], 1), ring(got[s - 1][1], -1)]
 
@@ -183,7 +184,9 @@
         return jnp.concatenate(full, 0)
 
     if n <= 16:
-        groups = [[0] + [d for t in range(1, far - 1) for d in (-t, t)], [d for d in (1 - far, far - 1) if d] + [far]]
+        groups = [[0] + [d for t in range(1, far - 1) for d in (-t, t)], [far]]
+        if far > 1:
+            groups.insert(1, [1 - far, far - 1])
     else:
         groups = [[0]]
         for s in range(1, far, n // 8):
@@ -199,19 +202,20 @@
         tie = []
         if max(group) < far - 1 and far > 2:
             tie = both(far - 2) if n <= 16 else both(max(group) + 1)
-        rows = [after(part, *tie) for d in group for part in got[d]]
+        halves = sorted(((d, i) for d in group for i in range(2)), key=lambda at: at[0] * (2 * at[1] - 1) > 0)
+        rows = [after(got[d][i], *tie) for d, i in halves]
         hid, d_pre, dx, x, c = expert_rows(rows, ids, full_in, full_out, ny, experts)
-        for i, d in enumerate(group):
-            dxs[d] = dx[i * tok : (i + 1) * tok]
+        for at, (d, i) in enumerate(halves):
+            dxs[d, i] = dx[at * half : (at + 1) * half]
         held.append((x, c, hid, d_pre))
 
     grads = {}
 
     def add_up(r, arrays, *others):
-        x, c, hid, d_pre = arrays
+        x, c, hid, d_pre = lax.optimization_barrier((arrays, others))[0] if others else arrays
         cols = slice(r * ff, (r + 1) * ff)
         for which, p, q in (("out", hid[:, cols], c), ("in", x, d_pre[:, cols])):
-            g = lax.dot_general(after(p, *others), q, TN, preferred_element_type=f32)
+            g = lax.dot_general(p, q, TN, preferred_element_type=f32)
             grads[which, r] = g + grads[which, r] if (which, r) in grads else g
 
     def to_core(r):
@@ -234,7 +238,7 @@
             if done < len(groups):
                 for r in at_once:
                     add_up(r, held[-1])
-        return list(grads.values()) + list(dxs.values())
+        return list(dxs.values())
 
     for s in range(1, far + 1):
         if s == min(2, far):
@@ -247,7 +251,7 @@
             hold(s - 1, *work_up_to(within(far - 2)))
         pass_on(s)
 
-    hold(far, *work_up_to(len(groups) - 1))
+    hold(far, *work_up_to(len(groups) - 1), *grads.values())
     work_up_to(len(groups))
     for r in range(1, ny):
         add_up(r, held[-1])
@@ -262,9 +266,9 @@
         unit = -(-sums[key].shape[0] // (16 * count)) * 16
         return sums[key][i * unit : (i + 1) * unit]
 
-    upper, under, ends = slice(0, half), slice(half, tok), []
-    flows = [(1, upper, far), (-1, under, far)] + ([(1, under, far - 1), (-1, upper, far - 1)] if far > 1 else [])
-    accs = [dxs[sign * d if d < far else d][rows].astype(bf16) for sign, rows, d in flows]
+    ends = []
+    flows = [(1, 0, far), (-1, 1, far)] + ([(1, 1, far - 1), (-1, 0, far - 1)] if far > 1 else [])
+    accs = [dxs[sign * d if d < far else d, i] for sign, i, d in flows]
     for step in range(far):
         i = step - 1 if far > 1 else 0
         keys = list(theirs) if 0 <= i < count else []
@@ -281,17 +285,17 @@
         for key, part in zip(keys, moved):
             theirs[key].append(part)
         following, accs = [], []
-        for (sign, rows, d), acc in zip(flows, sent):
+        for (sign, part, d), acc in zip(flows, sent):
             if d > 1:
-                following.append((sign, rows, d - 1))
-                accs.append((acc.astype(f32) + dxs[sign * (d - 1)][rows]).astype(bf16))
+                following.append((sign, part, d - 1))
+                accs.append((acc.astype(f32) + dxs[sign * (d - 1), part]).astype(bf16))
             else:
-                ends.append((rows, acc))
+                ends.append((part, acc))
         flows = following
-    grad = {rows.start: dxs[0][rows].astype(f32) for rows in (upper, under)}
-    for rows, acc in ends:
-        grad[rows.start] = grad[rows.start] + acc.astype(f32)
-    input_grad = jnp.concatenate([grad[0], grad[half]], 0).astype(bf16)
+    grad = [dxs[0, 0].astype(f32), dxs[0, 1].astype(f32)]
+    for part, acc in ends:
+        grad[part] = grad[part] + acc.astype(f32)
+    input_grad = jnp.concatenate(grad, 0).astype(bf16)
 
     new = {}
     for which, mom in (("out", mom_out), ("in", mom_in)):

time: 174 us -> 162 us (0.931)
  waiting for transfers between devices: 74 us -> 67.6 us
  local copies, waits for them, and re-layouts: 9.17 us -> 5.85 us
  matrix products: 16.1 us -> 13.4 us
    ppermute x28, waiting for transfers between devices: 63.7 us -> 54.2 us  [ring(): lax.ppermute(x, 'expert', [(i, order[(place[i] + step) % n]) for i in ran...]
    dot_general x8 -> x12, matrix products: 16.1 us -> 13.4 us  [add_up(): g = lax.dot_general(p, q, TN, preferred_element_type=f32)]
    ppermute x8, waiting for transfers between devices: 9.61 us -> 12.3 us  [shift_y(): lax.ppermute(x, 'dp', [(i, (i // 2 + r) % ny * 2 + i % 2) for i in range(...]
    unnamed x38 -> x28, local copies, waits for them, and re-layouts: 4.48 us -> 2.11 us
    pallas_call x2 -> x3, Pallas kernels: 18.9 us -> 19.4 us  [expert_rows(): pl.pallas_call(kernel, in_specs=[pl.BlockSpec(memory_space=pltpu.SMEM)] +...]
  transfers between devices with their start and end apart: 44 -> 44, of which waited for: 22 -> 20; matrix products, arithmetic and copies ran while one was open for 16% -> 16% of each run, Pallas kernels for 7% -> 12%
where the time goes in v3:
time: 162 us; the launch traced here: 161 us
  waiting for transfers between devices  67.6 us (42%)
  starting transfers between devices  41.1 us (25%)
  Pallas kernels  22.1 us (14%)
  matrix products  13.4 us (8%)
  other arithmetic  10 us (6%)
  local copies, waits for them, and re-layouts  5.85 us (4%)
    ppermute x28, waiting for transfers between devices, ring(): lax.ppermute(x, 'expert', [(i, order[(place[i] + step) % n]) for i in ran...  54.2 us
    ppermute x28, starting transfers between devices, ring(): lax.ppermute(x, 'expert', [(i, order[(place[i] + step) % n]) for i in ran...  29.7 us
    pallas_call x3, Pallas kernels, expert_rows(): pl.pallas_call(kernel, in_specs=[pl.BlockSpec(memory_space=pltpu.SMEM)] +...  19.4 us
    dot_general x12, matrix products, add_up(): g = lax.dot_general(p, q, TN, preferred_element_type=f32)  13.4 us
    ppermute x8, waiting for transfers between devices, shift_y(): lax.ppermute(x, 'dp', [(i, (i // 2 + r) % ny * 2 + i % 2) for i in range(...  12.3 us
    ppermute x8, starting transfers between devices, shift_y(): lax.ppermute(x, 'dp', [(i, (i // 2 + r) % ny * 2 + i % 2) for i in range(...  9.83 us
  transfers between devices with their start and end apart: 44, of which 20 were waited for; matrix products, arithmetic and copies ran while one was open for 16% of the time, Pallas kernels for 12%

profile of v3, /device:TPU:0, one launch (start us, length us, event | category | flops | bytes accessed | tf_op | source)
XLA Modules:
  0.0 161.2 jit_solution(10196559515808880818)
XLA Ops:
  0.6 2.7 %shard_map.103 = (bf16[64,4224]{1,0:T(8,128)(2,1)}, bf16[64,4224]{1,0:T(8,128)(2,1)}) custom-call(bf16[128,2048]{1,0:T(8,128)(2,1)} %tok_ref.1, bf16[128,2048]{1,0:T(8,128)(2,1)} %cot_ref.1, f32[8,128]{1,0:T(8,128)} %bitcast.31, s32[8,128]{1,0:T(8,128)} %bitcast.32), custom_call_target="tpu_custom_call" | custom-call | bytes 2097152 | tf_op jit(solution)/shard_map/pallas_call | solution.py:53
  3.3 2.9 %collective-permute-start = (bf16[64,4224]{1,0:T(8,128)(2,1)}, bf16[64,4224]{1,0:T(8,128)(2,1)}, u32[]{:S(2)}, u32[]{:S(2)}) collective-permute-start(bf16[64,4224]{1,0:T(8,128)(2,1)} %get-tuple-element.102.refs_0_), channel_id=1, source_target_pairs={{0,1},{1,3},{2,0},{3,5},{4,2},{5,7},{6,4},{7,6},{8,9},{9,11},{10,8... | collective-permute-start | bytes 1622024 | tf_op jit(solution)/shard_map/ppermute | solution.py:133
  6.4 1.9 %collective-permute-start.1 = (bf16[64,4224]{1,0:T(8,128)(2,1)}, bf16[64,4224]{1,0:T(8,128)(2,1)}, u32[]{:S(2)}, u32[]{:S(2)}) collective-permute-start(bf16[64,4224]{1,0:T(8,128)(2,1)} %get-tuple-element.103.refs_1_), channel_id=1, source_target_pairs={{0,1},{1,3},{2,0},{3,5},{4,2},{5,7},{6,4},{7,6},{8,9},{9,11},{10,8... | collective-permute-start | bytes 1622024 | tf_op jit(solution)/shard_map/ppermute | solution.py:133
  8.4 2.0 %collective-permute-start.5 = (bf16[1024,384]{1,0:T(8,128)(2,1)}, bf16[1024,384]{1,0:T(8,128)(2,1)}, u32[]{:S(2)}, u32[]{:S(2)}) collective-permute-start(bf16[1024,384]{1,0:T(8,128)(2,1)} %bitcast.29), channel_id=1, source_target_pairs={{0,16},{8,24},{16,0},{24,8},{1,17},{9,25},{17,1},{25,9},{2,18},{10... | collective-permute-start | bytes 2359304 | tf_op jit(solution)/shard_map/ppermute | solution.py:139
  10.4 9.4 %collective-permute-done.refs_6_ = bf16[64,4224]{1,0:T(8,128)(2,1)} collective-permute-done((bf16[64,4224]{1,0:T(8,128)(2,1)}, bf16[64,4224]{1,0:T(8,128)(2,1)}, u32[]{:S(2)}, u32[]{:S(2)}) %collective-permute-start) | collective-permute-done | bytes 540704 | tf_op jit(solution)/shard_map/ppermute | solution.py:133
  19.8 2.0 %collective-permute-done.2.refs_3_ = bf16[64,4224]{1,0:T(8,128)(2,1)} collective-permute-done((bf16[64,4224]{1,0:T(8,128)(2,1)}, bf16[64,4224]{1,0:T(8,128)(2,1)}, u32[]{:S(2)}, u32[]{:S(2)}) %collective-permute-start.2) | collective-permute-done | bytes 540704 | tf_op jit(solution)/shard_map/ppermute | solution.py:133
  21.8 8.7 %collective-permute-done.1.refs_2_ = bf16[64,4224]{1,0:T(8,128)(2,1)} collective-permute-done((bf16[64,4224]{1,0:T(8,128)(2,1)}, bf16[64,4224]{1,0:T(8,128)(2,1)}, u32[]{:S(2)}, u32[]{:S(2)}) %collective-permute-start.1) | collective-permute-done | bytes 540704 | tf_op jit(solution)/shard_map/ppermute | solution.py:133
  30.5 1.4 collective-permute-done.3.refs_7_
  32.8 1.7 %collective-permute-start.9 = (bf16[64,4224]{1,0:T(8,128)(2,1)}, bf16[64,4224]{1,0:T(8,128)(2,1)}, u32[]{:S(2)}, u32[]{:S(2)}) collective-permute-start(bf16[64,4224]{1,0:T(8,128)(2,1)} %collective-permute-done.2.refs_3_), channel_id=1, source_target_pairs={{0,2},{1,0},{2,4},{3,1},{4,6},{5,3},{6,7},{7,5},{8,10},{9,8},{10,1... | collective-permute-start | bytes 1622024 | tf_op jit(solution)/shard_map/ppermute | solution.py:133
  34.8 0.6 collective-permute-done.4
  35.5 0.9 copy-done.11
  36.3 1.6 collective-permute-start.7
  38.3 0.7 copy-done.12
  39.2 1.6 collective-permute-start.12
  40.8 1.3 constant_dynamic-update-slice_fusion.3
  42.1 1.3 constant_dynamic-update-slice_fusion.2.in_ref
  43.4 4.5 %collective-permute-done.10.refs_9_ = bf16[64,4224]{1,0:T(8,128)(2,1)} collective-permute-done((bf16[64,4224]{1,0:T(8,128)(2,1)}, bf16[64,4224]{1,0:T(8,128)(2,1)}, u32[]{:S(2)}, u32[]{:S(2)}) %collective-permute-start.10) | collective-permute-done | bytes 540704 | tf_op jit(solution)/shard_map/ppermute | solution.py:133
  47.9 10.7 %collective-permute-done.9.refs_5_ = bf16[64,4224]{1,0:T(8,128)(2,1)} collective-permute-done((bf16[64,4224]{1,0:T(8,128)(2,1)}, bf16[64,4224]{1,0:T(8,128)(2,1)}, u32[]{:S(2)}, u32[]{:S(2)}) %collective-permute-start.9) | collective-permute-done | bytes 540704 | tf_op jit(solution)/shard_map/ppermute | solution.py:133
  58.6 1.5 collective-permute-done.7.refs_8_
  60.6 1.6 %collective-permute-start.17 = (bf16[64,4224]{1,0:T(8,128)(2,1)}, bf16[64,4224]{1,0:T(8,128)(2,1)S(1)}, u32[]{:S(2)}, u32[]{:S(2)}) collective-permute-start(bf16[64,4224]{1,0:T(8,128)(2,1)} %collective-permute-done.10.refs_9_), channel_id=1, source_target_pairs={{0,2},{1,0},{2,4},{3,1},{4,6},{5,3},{6,7},{7,5},{8,10},{9,8},{10,1... | collective-permute-start | bytes 1622024 | tf_op jit(solution)/shard_map/ppermute | solution.py:133
  62.7 1.6 collective-permute-start.15
  64.7 1.5 broadcast_select_fusion.3
  66.2 1.5 broadcast_select_fusion.1
  67.7 1.8 %pad_maximum_fusion.out_ref = bf16[768,2048]{1,0:T(8,128)(2,1)} fusion(bf16[192,2048]{1,0:T(8,128)(2,1)S(1)} %get-tuple-element.192, bf16[192,2048]{1,0:T(8,128)(2,1)S(1)} %get-tuple-element.191, bf16[192,2048]{1,0:T(8,128)(2,1)S(1)} %get-tuple-element.190, bf16[192,2048]{1,0:T(8,128)(2,1)S(1)} %get-tuple-element.189), kind=kLoop, calls=%fused_computation | loop fusion | flops 12582912 | bytes 6291456 | tf_op jit(solution)/shard_map/concatenate | solution.py:184
  69.6 12.8 %shard_map.104 = (bf16[640,768]{1,0:T(8,128)(2,1)S(1)}, bf16[640,768]{1,0:T(8,128)(2,1)}, bf16[640,2048]{1,0:T(8,128)(2,1)}, bf16[640,2048]{1,0:T(8,128)(2,1)}, bf16[640,2048]{1,0:T(8,128)(2,1)}) custom-call(s32[2]{0:T(128)S(1)} %fusion.20.id_ref, bf16[2048,768]{1,0:T(8,128)(2,1)} %copy-done.1, bf16[768,2048]{1,0:T(8,128)(2,1)} %pad_maximum_fusion.out_ref, ...), custom_call_target="tpu_custom_call" | custom-call | flops 1048576 | bytes 65536 | tf_op jit(solution)/shard_map/pallas_call | solution.py:101
  82.4 1.6 %collective-permute-start.19 = (bf16[64,4224]{1,0:T(8,128)(2,1)S(1)}, bf16[64,4224]{1,0:T(8,128)(2,1)S(1)}, u32[]{:S(2)}, u32[]{:S(2)}) collective-permute-start(bf16[64,4224]{1,0:T(8,128)(2,1)S(1)} %collective-permute-done.17.refs_3_), channel_id=1, source_target_pairs={{0,2},{1,0},{2,4},{3,1},{4,6},{5,3},{6,7},{7,5},{8,10},{9,8},{10,1... | collective-permute-start | bytes 1622024 | tf_op jit(solution)/shard_map/ppermute | solution.py:133
  84.4 3.2 %collective-permute-done.15.refs_1_ = bf16[64,4224]{1,0:T(8,128)(2,1)S(1)} collective-permute-done((bf16[64,4224]{1,0:T(8,128)(2,1)}, bf16[64,4224]{1,0:T(8,128)(2,1)S(1)}, u32[]{:S(2)}, u32[]{:S(2)}) %collective-permute-start.15) | collective-permute-done | bytes 540704 | tf_op jit(solution)/shard_map/ppermute | solution.py:133
  87.6 1.6 %collective-permute-done.14.refs_0_ = bf16[64,4224]{1,0:T(8,128)(2,1)S(1)} collective-permute-done((bf16[64,4224]{1,0:T(8,128)(2,1)}, bf16[64,4224]{1,0:T(8,128)(2,1)S(1)}, u32[]{:S(2)}, u32[]{:S(2)}) %collective-permute-start.14) | collective-permute-done | bytes 540704 | tf_op jit(solution)/shard_map/ppermute | solution.py:133
  89.2 3.7 %fusion.4 = f32[2048,384]{1,0:T(8,128)S(1)} fusion(bf16[640,2048]{1,0:T(8,128)(2,1)} %get-tuple-element.155, bf16[640,768]{1,0:T(8,128)(2,1)} %get-tuple-element.156), kind=kOutput, calls=%fused_computation.36 | convolution fusion | flops 1006632960 | bytes 6258688 | tf_op jit(solution)/shard_map/dot_general | solution.py:218
  93.0 1.4 fusion.6
  94.8 3.3 %shard_map.105 = (bf16[256,768]{1,0:T(8,128)(2,1)S(1)}, bf16[256,768]{1,0:T(8,128)(2,1)S(1)}, bf16[256,2048]{1,0:T(8,128)(2,1)S(1)}, bf16[256,2048]{1,0:T(8,128)(2,1)S(1)}, bf16[256,2048]{1,0:T(8,128)(2,1)S(1)}) custom-call(s32[2]{0:T(128)S(1)} %fusion.20.id_ref, bf16[2048,768]{1,0:T(8,128)(2,1)S(1)} %copy-done.2, bf16[768,2048]{1,0:T(8,128)(2,1)S(1)} %copy-done, ...), custom_call_target="tpu_custom_call" | custom-call | flops 1048576 | bytes 65536 | tf_op jit(solution)/shard_map/pallas_call | solution.py:101
  98.2 0.7 convolution_add_fusion.2
  98.9 0.6 convolution_add_fusion.3
  100.1 1.6 collective-permute-start.23
  101.7 3.3 %shard_map.106 = (bf16[128,768]{1,0:T(8,128)(2,1)S(1)}, bf16[128,768]{1,0:T(8,128)(2,1)S(1)}, bf16[128,2048]{1,0:T(8,128)(2,1)S(1)}, bf16[128,2048]{1,0:T(8,128)(2,1)S(1)}, bf16[128,2048]{1,0:T(8,128)(2,1)S(1)}) custom-call(s32[2]{0:T(128)S(1)} %fusion.20.id_ref, bf16[2048,768]{1,0:T(8,128)(2,1)S(1)} %copy-done.2, bf16[768,2048]{1,0:T(8,128)(2,1)S(1)} %copy-done, ...), custom_call_target="tpu_custom_call" | custom-call | flops 1048576 | bytes 65536 | tf_op jit(solution)/shard_map/pallas_call | solution.py:101
  105.0 0.6 convolution_add_fusion.1
  105.8 0.6 convolution_add_fusion
  108.1 1.6 collective-permute-start.21
  110.1 5.3 %collective-permute-done.20 = bf16[64,2048]{1,0:T(8,128)(2,1)S(1)} collective-permute-done((bf16[64,2048]{1,0:T(8,128)(2,1)S(1)}, bf16[64,2048]{1,0:T(8,128)(2,1)S(1)}, u32[]{:S(2)}, u32[]{:S(2)}) %collective-permute-start.20) | collective-permute-done | bytes 262176 | tf_op jit(solution)/shard_map/ppermute | solution.py:133
  115.4 1.0 collective-permute-done.21
  117.2 1.6 collective-permute-start.29
  118.8 1.6 collective-permute-start.30
  121.5 0.6 fusion.8
  122.1 0.6 fusion.14
  122.7 1.5 add_add_fusion
  124.1 1.8 %collective-permute-done.28 = bf16[64,2048]{1,0:T(8,128)(2,1)S(1)} collective-permute-done((bf16[64,2048]{1,0:T(8,128)(2,1)S(1)}, bf16[64,2048]{1,0:T(8,128)(2,1)S(1)}, u32[]{:S(2)}, u32[]{:S(2)}) %collective-permute-start.28) | collective-permute-done | bytes 262176 | tf_op jit(solution)/shard_map/ppermute | solution.py:133
  126.0 1.6 collective-permute-start.27
  127.5 0.7 fusion.10
  128.3 1.6 collective-permute-start.36
  130.4 1.9 %collective-permute-done.27 = bf16[64,2048]{1,0:T(8,128)(2,1)S(1)} collective-permute-done((bf16[64,2048]{1,0:T(8,128)(2,1)S(1)}, bf16[64,2048]{1,0:T(8,128)(2,1)S(1)}, u32[]{:S(2)}, u32[]{:S(2)}) %collective-permute-start.27) | collective-permute-done | bytes 262176 | tf_op jit(solution)/shard_map/ppermute | solution.py:133
  132.3 1.6 collective-permute-done.31
  134.8 1.6 collective-permute-start.33
  136.8 2.7 %collective-permute-done.36 = bf16[64,2048]{1,0:T(8,128)(2,1)S(1)} collective-permute-done((bf16[64,2048]{1,0:T(8,128)(2,1)S(1)}, bf16[64,2048]{1,0:T(8,128)(2,1)S(1)}, u32[]{:S(2)}, u32[]{:S(2)}) %collective-permute-start.36) | collective-permute-done | bytes 262176 | tf_op jit(solution)/shard_map/ppermute | solution.py:139
  139.5 1.6 collective-permute-start.35
  141.1 0.6 fusion.16
  141.9 1.2 collective-permute-done.37
  143.0 1.5 collective-permute-start.40
  145.1 1.0 collective-permute-done.35
  146.7 1.6 collective-permute-start.39
  148.3 1.8 %add_add_fusion.1 = f32[2048,384]{1,0:T(8,128)S(1)} fusion(f32[2048,384]{1,0:T(8,128)S(1)} %fusion.16, f32[2048,384]{1,0:T(8,128)S(1)} %fusion.10, bf16[640,2048]{1,0:T(8,128)(2,1)S(1)} %copy-done.6, bf16[640,768]{1,0:T(8,128)(2,1)S(1)} %copy-done.13), kind=kOutput, calls=%fused_computation.2 | convolution fusion | flops 1008205824 | bytes 12550144 | tf_op jit(solution)/shard_map/dot_general | solution.py:218
  150.2 6.8 %collective-permute-done.41 = bf16[320,384]{1,0:T(8,128)(2,1)S(1)} collective-permute-done((bf16[320,384]{1,0:T(8,128)(2,1)S(1)}, bf16[320,384]{1,0:T(8,128)(2,1)S(1)}, u32[]{:S(2)}, u32[]{:S(2)}) %collective-permute-start.41) | collective-permute-done | bytes 245792 | tf_op jit(solution)/shard_map/ppermute | solution.py:139
  157.3 0.8 pad_maximum_fusion.1
  158.1 1.6 fusion
  159.7 1.5 fusion.1
  (96 shorter events, 12.4 us)
Async XLA Ops:
  3.3 16.4 %collective-permute-start = (bf16[64,4224]{1,0:T(8,128)(2,1)}, bf16[64,4224]{1,0:T(8,128)(2,1)}, u32[]{:S(2)}, u32[]{:S(2)}) collective-permute-start(bf16[64,4224]{1,0:T(8,128)(2,1)} %get-tuple-element.102.refs_0_), channel_id=1, source_target_pairs={{0,1},{1,3},{2,0},{3,5},{4,2},{5,7},{6,4},{7,6},{8,9},{9,11},{10,8... | collective-permute-start | bytes 1622024 | tf_op jit(solution)/shard_map/ppermute | solution.py:133
  6.3 15.5 %collective-permute-start.2 = (bf16[64,4224]{1,0:T(8,128)(2,1)}, bf16[64,4224]{1,0:T(8,128)(2,1)}, u32[]{:S(2)}, u32[]{:S(2)}) collective-permute-start(bf16[64,4224]{1,0:T(8,128)(2,1)} %get-tuple-element.102.refs_0_), channel_id=1, source_target_pairs={{0,2},{1,0},{2,4},{3,1},{4,6},{5,3},{6,7},{7,5},{8,10},{9,8},{10,1... | collective-permute-start | bytes 1622024 | tf_op jit(solution)/shard_map/ppermute | solution.py:133
  6.4 24.2 %collective-permute-start.1 = (bf16[64,4224]{1,0:T(8,128)(2,1)}, bf16[64,4224]{1,0:T(8,128)(2,1)}, u32[]{:S(2)}, u32[]{:S(2)}) collective-permute-start(bf16[64,4224]{1,0:T(8,128)(2,1)} %get-tuple-element.103.refs_1_), channel_id=1, source_target_pairs={{0,1},{1,3},{2,0},{3,5},{4,2},{5,7},{6,4},{7,6},{8,9},{9,11},{10,8... | collective-permute-start | bytes 1622024 | tf_op jit(solution)/shard_map/ppermute | solution.py:133
  8.3 23.6 %collective-permute-start.3 = (bf16[64,4224]{1,0:T(8,128)(2,1)}, bf16[64,4224]{1,0:T(8,128)(2,1)}, u32[]{:S(2)}, u32[]{:S(2)}) collective-permute-start(bf16[64,4224]{1,0:T(8,128)(2,1)} %get-tuple-element.103.refs_1_), channel_id=1, source_target_pairs={{0,2},{1,0},{2,4},{3,1},{4,6},{5,3},{6,7},{7,5},{8,10},{9,8},{10,1... | collective-permute-start | bytes 1622024 | tf_op jit(solution)/shard_map/ppermute | solution.py:133
  8.4 23.5 %collective-permute-start.5 = (bf16[1024,384]{1,0:T(8,128)(2,1)}, bf16[1024,384]{1,0:T(8,128)(2,1)}, u32[]{:S(2)}, u32[]{:S(2)}) collective-permute-start(bf16[1024,384]{1,0:T(8,128)(2,1)} %bitcast.29), channel_id=1, source_target_pairs={{0,16},{8,24},{16,0},{24,8},{1,17},{9,25},{17,1},{25,9},{2,18},{10... | collective-permute-start | bytes 2359304 | tf_op jit(solution)/shard_map/ppermute | solution.py:139
  31.9 3.5 %collective-permute-start.4 = (bf16[1024,384]{1,0:T(8,128)(2,1)}, bf16[1024,384]{1,0:T(8,128)(2,1)S(1)}, u32[]{:S(2)}, u32[]{:S(2)}) collective-permute-start(bf16[1024,384]{1,0:T(8,128)(2,1)} %bitcast.30), channel_id=1, source_target_pairs={{0,8},{8,0},{16,24},{24,16},{1,9},{9,1},{17,25},{25,17},{2,10},{10... | collective-permute-start | bytes 2359304 | tf_op jit(solution)/shard_map/ppermute | solution.py:136
  31.9 7.3 %collective-permute-start.6 = (bf16[1024,384]{1,0:T(8,128)(2,1)}, bf16[1024,384]{1,0:T(8,128)(2,1)}, u32[]{:S(2)}, u32[]{:S(2)}) collective-permute-start(bf16[1024,384]{1,0:T(8,128)(2,1)} %collective-permute-done.5), channel_id=1, source_target_pairs={{0,8},{8,0},{16,24},{24,16},{1,9},{9,1},{17,25},{25,17},{2,10},{10... | collective-permute-start | bytes 2359304 | tf_op jit(solution)/shard_map/ppermute | solution.py:136
  32.4 5.7 %copy-start.10 = (bf16[1,1024,384]{2,1,0:T(8,128)(2,1)S(1)}, bf16[1,1024,384]{2,1,0:T(8,128)(2,1)}, u32[]{:S(2)}) copy-start(bf16[1,1024,384]{2,1,0:T(8,128)(2,1)} %param.12) | copy-start | bytes 2359300
  32.4 15.4 %collective-permute-start.10 = (bf16[64,4224]{1,0:T(8,128)(2,1)}, bf16[64,4224]{1,0:T(8,128)(2,1)}, u32[]{:S(2)}, u32[]{:S(2)}) collective-permute-start(bf16[64,4224]{1,0:T(8,128)(2,1)} %collective-permute-done.3.refs_7_), channel_id=1, source_target_pairs={{0,2},{1,0},{2,4},{3,1},{4,6},{5,3},{6,7},{7,5},{8,10},{9,8},{10,1... | collective-permute-start | bytes 1622024 | tf_op jit(solution)/shard_map/ppermute | solution.py:133
  32.8 25.8 %collective-permute-start.9 = (bf16[64,4224]{1,0:T(8,128)(2,1)}, bf16[64,4224]{1,0:T(8,128)(2,1)}, u32[]{:S(2)}, u32[]{:S(2)}) collective-permute-start(bf16[64,4224]{1,0:T(8,128)(2,1)} %collective-permute-done.2.refs_3_), channel_id=1, source_target_pairs={{0,2},{1,0},{2,4},{3,1},{4,6},{5,3},{6,7},{7,5},{8,10},{9,8},{10,1... | collective-permute-start | bytes 1622024 | tf_op jit(solution)/shard_map/ppermute | solution.py:133
  34.5 24.0 %collective-permute-start.8 = (bf16[64,4224]{1,0:T(8,128)(2,1)}, bf16[64,4224]{1,0:T(8,128)(2,1)}, u32[]{:S(2)}, u32[]{:S(2)}) collective-permute-start(bf16[64,4224]{1,0:T(8,128)(2,1)} %collective-permute-done.1.refs_2_), channel_id=1, source_target_pairs={{0,1},{1,3},{2,0},{3,5},{4,2},{5,7},{6,4},{7,6},{8,9},{9,11},{10,8... | collective-permute-start | bytes 1622024 | tf_op jit(solution)/shard_map/ppermute | solution.py:133
  35.5 0.9 copy-start.11
  36.3 23.8 %collective-permute-start.7 = (bf16[64,4224]{1,0:T(8,128)(2,1)}, bf16[64,4224]{1,0:T(8,128)(2,1)}, u32[]{:S(2)}, u32[]{:S(2)}) collective-permute-start(bf16[64,4224]{1,0:T(8,128)(2,1)} %collective-permute-done.refs_6_), channel_id=1, source_target_pairs={{0,1},{1,3},{2,0},{3,5},{4,2},{5,7},{6,4},{7,6},{8,9},{9,11},{10,8... | collective-permute-start | bytes 1622024 | tf_op jit(solution)/shard_map/ppermute | solution.py:133
  37.9 1.1 copy-start.12
  39.2 20.9 %collective-permute-start.12 = (bf16[192,2048]{1,0:T(8,128)(2,1)}, bf16[192,2048]{1,0:T(8,128)(2,1)}, u32[]{:S(2)}, u32[]{:S(2)}) collective-permute-start(bf16[192,2048]{1,0:T(8,128)(2,1)} %bitcast.3), channel_id=1, source_target_pairs={{0,16},{8,24},{16,0},{24,8},{1,17},{9,25},{17,1},{25,9},{2,18},{10... | collective-permute-start | bytes 2359304 | tf_op jit(solution)/shard_map/ppermute | solution.py:139
  43.4 24.3 %copy-start.1 = (bf16[2048,768]{1,0:T(8,128)(2,1)}, bf16[2048,768]{1,0:T(8,128)(2,1)S(1)}, u32[]{:S(2)}) copy-start(bf16[2048,768]{1,0:T(8,128)(2,1)S(1)} %constant_dynamic-update-slice_fusion.2.in_ref) | copy-start | bytes 9437188
  60.1 4.2 %collective-permute-start.11 = (bf16[192,2048]{1,0:T(8,128)(2,1)}, bf16[192,2048]{1,0:T(8,128)(2,1)}, u32[]{:S(2)}, u32[]{:S(2)}) collective-permute-start(bf16[192,2048]{1,0:T(8,128)(2,1)} %bitcast.3), channel_id=1, source_target_pairs={{0,8},{8,0},{16,24},{24,16},{1,9},{9,1},{17,25},{25,17},{2,10},{10... | collective-permute-start | bytes 2359304 | tf_op jit(solution)/shard_map/ppermute | solution.py:136
  60.1 6.1 %collective-permute-start.13 = (bf16[192,2048]{1,0:T(8,128)(2,1)}, bf16[192,2048]{1,0:T(8,128)(2,1)}, u32[]{:S(2)}, u32[]{:S(2)}) collective-permute-start(bf16[192,2048]{1,0:T(8,128)(2,1)} %collective-permute-done.12), channel_id=1, source_target_pairs={{0,8},{8,0},{16,24},{24,16},{1,9},{9,1},{17,25},{25,17},{2,10},{10... | collective-permute-start | bytes 2359304 | tf_op jit(solution)/shard_map/ppermute | solution.py:136
  60.6 21.7 %collective-permute-start.17 = (bf16[64,4224]{1,0:T(8,128)(2,1)}, bf16[64,4224]{1,0:T(8,128)(2,1)S(1)}, u32[]{:S(2)}, u32[]{:S(2)}) collective-permute-start(bf16[64,4224]{1,0:T(8,128)(2,1)} %collective-permute-done.10.refs_9_), channel_id=1, source_target_pairs={{0,2},{1,0},{2,4},{3,1},{4,6},{5,3},{6,7},{7,5},{8,10},{9,8},{10,1... | collective-permute-start | bytes 1622024 | tf_op jit(solution)/shard_map/ppermute | solution.py:133
  62.3 21.7 %collective-permute-start.16 = (bf16[64,4224]{1,0:T(8,128)(2,1)}, bf16[64,4224]{1,0:T(8,128)(2,1)S(1)}, u32[]{:S(2)}, u32[]{:S(2)}) collective-permute-start(bf16[64,4224]{1,0:T(8,128)(2,1)} %collective-permute-done.7.refs_8_), channel_id=1, source_target_pairs={{0,1},{1,3},{2,0},{3,5},{4,2},{5,7},{6,4},{7,6},{8,9},{9,11},{10,8... | collective-permute-start | bytes 1622024 | tf_op jit(solution)/shard_map/ppermute | solution.py:133
  62.7 24.9 %collective-permute-start.15 = (bf16[64,4224]{1,0:T(8,128)(2,1)}, bf16[64,4224]{1,0:T(8,128)(2,1)S(1)}, u32[]{:S(2)}, u32[]{:S(2)}) collective-permute-start(bf16[64,4224]{1,0:T(8,128)(2,1)} %collective-permute-done.9.refs_5_), channel_id=1, source_target_pairs={{0,2},{1,0},{2,4},{3,1},{4,6},{5,3},{6,7},{7,5},{8,10},{9,8},{10,1... | collective-permute-start | bytes 1622024 | tf_op jit(solution)/shard_map/ppermute | solution.py:133
  64.3 24.9 %collective-permute-start.14 = (bf16[64,4224]{1,0:T(8,128)(2,1)}, bf16[64,4224]{1,0:T(8,128)(2,1)S(1)}, u32[]{:S(2)}, u32[]{:S(2)}) collective-permute-start(bf16[64,4224]{1,0:T(8,128)(2,1)} %collective-permute-done.8.refs_4_), channel_id=1, source_target_pairs={{0,1},{1,3},{2,0},{3,5},{4,2},{5,7},{6,4},{7,6},{8,9},{9,11},{10,8... | collective-permute-start | bytes 1622024 | tf_op jit(solution)/shard_map/ppermute | solution.py:133
  67.7 1.8 %copy-start.3 = (bf16[64,4224]{1,0:T(8,128)(2,1)S(1)}, bf16[64,4224]{1,0:T(8,128)(2,1)}, u32[]{:S(2)}) copy-start(bf16[64,4224]{1,0:T(8,128)(2,1)} %get-tuple-element.102.refs_0_) | copy-start | bytes 1622020
  67.7 1.8 %copy-start.4 = (bf16[64,4224]{1,0:T(8,128)(2,1)S(1)}, bf16[64,4224]{1,0:T(8,128)(2,1)}, u32[]{:S(2)}) copy-start(bf16[64,4224]{1,0:T(8,128)(2,1)} %get-tuple-element.103.refs_1_) | copy-start | bytes 1622020
  82.4 19.3 %collective-permute-start.19 = (bf16[64,4224]{1,0:T(8,128)(2,1)S(1)}, bf16[64,4224]{1,0:T(8,128)(2,1)S(1)}, u32[]{:S(2)}, u32[]{:S(2)}) collective-permute-start(bf16[64,4224]{1,0:T(8,128)(2,1)S(1)} %collective-permute-done.17.refs_3_), channel_id=1, source_target_pairs={{0,2},{1,0},{2,4},{3,1},{4,6},{5,3},{6,7},{7,5},{8,10},{9,8},{10,1... | collective-permute-start | bytes 1622024 | tf_op jit(solution)/shard_map/ppermute | solution.py:133
  84.0 17.7 %collective-permute-start.18 = (bf16[64,4224]{1,0:T(8,128)(2,1)S(1)}, bf16[64,4224]{1,0:T(8,128)(2,1)S(1)}, u32[]{:S(2)}, u32[]{:S(2)}) collective-permute-start(bf16[64,4224]{1,0:T(8,128)(2,1)S(1)} %collective-permute-done.16.refs_2_), channel_id=1, source_target_pairs={{0,1},{1,3},{2,0},{3,5},{4,2},{5,7},{6,4},{7,6},{8,9},{9,11},{10,8... | collective-permute-start | bytes 1622024 | tf_op jit(solution)/shard_map/ppermute | solution.py:133
  89.2 3.7 %copy-start.5 = (bf16[640,2048]{1,0:T(8,128)(2,1)S(1)}, bf16[640,2048]{1,0:T(8,128)(2,1)}, u32[]{:S(2)}) copy-start(bf16[640,2048]{1,0:T(8,128)(2,1)} %get-tuple-element.165) | copy-start | bytes 7864324
  89.2 5.2 %copy-start.2 = (bf16[2048,768]{1,0:T(8,128)(2,1)S(1)}, bf16[2048,768]{1,0:T(8,128)(2,1)}, u32[]{:S(2)}) copy-start(bf16[2048,768]{1,0:T(8,128)(2,1)} %copy-done.1) | copy-start | bytes 9437188
  93.0 1.9 %copy-start = (bf16[768,2048]{1,0:T(8,128)(2,1)S(1)}, bf16[768,2048]{1,0:T(8,128)(2,1)}, u32[]{:S(2)}) copy-start(bf16[768,2048]{1,0:T(8,128)(2,1)} %pad_maximum_fusion.out_ref) | copy-start | bytes 9437188
  99.6 10.5 %collective-permute-start.22 = (bf16[64,2048]{1,0:T(8,128)(2,1)S(1)}, bf16[64,2048]{1,0:T(8,128)(2,1)S(1)}, u32[]{:S(2)}, u32[]{:S(2)}) collective-permute-start(bf16[64,2048]{1,0:T(8,128)(2,1)S(1)} %get-tuple-element.195), channel_id=1, source_target_pairs={{0,1},{1,3},{2,0},{3,5},{4,2},{5,7},{6,4},{7,6},{8,9},{9,11},{10,8... | collective-permute-start | bytes 786440 | tf_op jit(solution)/shard_map/ppermute | solution.py:133
  100.1 10.0 %collective-permute-start.23 = (bf16[64,2048]{1,0:T(8,128)(2,1)S(1)}, bf16[64,2048]{1,0:T(8,128)(2,1)S(1)}, u32[]{:S(2)}, u32[]{:S(2)}) collective-permute-start(bf16[64,2048]{1,0:T(8,128)(2,1)S(1)} %get-tuple-element.196), channel_id=1, source_target_pairs={{0,2},{1,0},{2,4},{3,1},{4,6},{5,3},{6,7},{7,5},{8,10},{9,8},{10,1... | collective-permute-start | bytes 786440 | tf_op jit(solution)/shard_map/ppermute | solution.py:133
  105.7 2.4 %collective-permute-start.24 = (bf16[192,2048]{1,0:T(8,128)(2,1)S(1)}, bf16[192,2048]{1,0:T(8,128)(2,1)S(1)}, u32[]{:S(2)}, u32[]{:S(2)}) collective-permute-start(bf16[192,2048]{1,0:T(8,128)(2,1)S(1)} %dynamic-slice_convert_fusion.3), channel_id=1, source_target_pairs={{0,8},{8,0},{16,24},{24,16},{1,9},{9,1},{17,25},{25,17},{2,10},{10... | collective-permute-start | bytes 2359304 | tf_op jit(solution)/shard_map/ppermute | solution.py:136
  106.5 3.4 %collective-permute-start.25 = (bf16[1024,384]{1,0:T(8,128)(2,1)S(1)}, bf16[1024,384]{1,0:T(8,128)(2,1)S(1)}, u32[]{:S(2)}, u32[]{:S(2)}) collective-permute-start(bf16[1024,384]{1,0:T(8,128)(2,1)S(1)} %dynamic-slice_convert_fusion.2), channel_id=1, source_target_pairs={{0,8},{8,0},{16,24},{24,16},{1,9},{9,1},{17,25},{25,17},{2,10},{10... | collective-permute-start | bytes 2359304 | tf_op jit(solution)/shard_map/ppermute | solution.py:136
  107.1 8.3 %collective-permute-start.20 = (bf16[64,2048]{1,0:T(8,128)(2,1)S(1)}, bf16[64,2048]{1,0:T(8,128)(2,1)S(1)}, u32[]{:S(2)}, u32[]{:S(2)}) collective-permute-start(bf16[64,2048]{1,0:T(8,128)(2,1)S(1)} %get-tuple-element.205), channel_id=1, source_target_pairs={{0,1},{1,3},{2,0},{3,5},{4,2},{5,7},{6,4},{7,6},{8,9},{9,11},{10,8... | collective-permute-start | bytes 786440 | tf_op jit(solution)/shard_map/ppermute | solution.py:133
  108.1 8.4 %copy-start.7 = (bf16[640,2048]{1,0:T(8,128)(2,1)S(1)}, bf16[640,2048]{1,0:T(8,128)(2,1)}, u32[]{:S(2)}) copy-start(bf16[640,2048]{1,0:T(8,128)(2,1)} %get-tuple-element.112) | copy-start | bytes 7864324
  108.1 8.3 %collective-permute-start.21 = (bf16[64,2048]{1,0:T(8,128)(2,1)S(1)}, bf16[64,2048]{1,0:T(8,128)(2,1)S(1)}, u32[]{:S(2)}, u32[]{:S(2)}) collective-permute-start(bf16[64,2048]{1,0:T(8,128)(2,1)S(1)} %get-tuple-element.204), channel_id=1, source_target_pairs={{0,2},{1,0},{2,4},{3,1},{4,6},{5,3},{6,7},{7,5},{8,10},{9,8},{10,1... | collective-permute-start | bytes 786440 | tf_op jit(solution)/shard_map/ppermute | solution.py:133
  116.7 9.3 %collective-permute-start.28 = (bf16[64,2048]{1,0:T(8,128)(2,1)S(1)}, bf16[64,2048]{1,0:T(8,128)(2,1)S(1)}, u32[]{:S(2)}, u32[]{:S(2)}) collective-permute-start(bf16[64,2048]{1,0:T(8,128)(2,1)S(1)} %get-tuple-element.178), channel_id=1, source_target_pairs={{0,1},{1,3},{2,0},{3,5},{4,2},{5,7},{6,4},{7,6},{8,9},{9,11},{10,8... | collective-permute-start | bytes 786440 | tf_op jit(solution)/shard_map/ppermute | solution.py:133
  117.2 11.1 %collective-permute-start.29 = (bf16[64,2048]{1,0:T(8,128)(2,1)S(1)}, bf16[64,2048]{1,0:T(8,128)(2,1)S(1)}, u32[]{:S(2)}, u32[]{:S(2)}) collective-permute-start(bf16[64,2048]{1,0:T(8,128)(2,1)S(1)} %get-tuple-element.177), channel_id=1, source_target_pairs={{0,2},{1,0},{2,4},{3,1},{4,6},{5,3},{6,7},{7,5},{8,10},{9,8},{10,1... | collective-permute-start | bytes 786440 | tf_op jit(solution)/shard_map/ppermute | solution.py:133
  118.8 11.1 %collective-permute-start.30 = (bf16[64,2048]{1,0:T(8,128)(2,1)S(1)}, bf16[64,2048]{1,0:T(8,128)(2,1)S(1)}, u32[]{:S(2)}, u32[]{:S(2)}) collective-permute-start(bf16[64,2048]{1,0:T(8,128)(2,1)S(1)} %get-tuple-element.201), channel_id=1, source_target_pairs={{0,16},{8,24},{16,0},{24,8},{1,17},{9,25},{17,1},{25,9},{2,18},{10... | collective-permute-start | bytes 786440 | tf_op jit(solution)/shard_map/ppermute | solution.py:139
  120.5 13.5 %collective-permute-start.31 = (bf16[352,384]{1,0:T(8,128)(2,1)S(1)}, bf16[352,384]{1,0:T(8,128)(2,1)S(1)}, u32[]{:S(2)}, u32[]{:S(2)}) collective-permute-start(bf16[352,384]{1,0:T(8,128)(2,1)S(1)} %get-tuple-element.203), channel_id=1, source_target_pairs={{0,16},{8,24},{16,0},{24,8},{1,17},{9,25},{17,1},{25,9},{2,18},{10... | collective-permute-start | bytes 811016 | tf_op jit(solution)/shard_map/ppermute | solution.py:139
  121.0 9.4 %collective-permute-start.26 = (bf16[64,2048]{1,0:T(8,128)(2,1)S(1)}, bf16[64,2048]{1,0:T(8,128)(2,1)S(1)}, u32[]{:S(2)}, u32[]{:S(2)}) collective-permute-start(bf16[64,2048]{1,0:T(8,128)(2,1)S(1)} %get-tuple-element.194), channel_id=1, source_target_pairs={{0,1},{1,3},{2,0},{3,5},{4,2},{5,7},{6,4},{7,6},{8,9},{9,11},{10,8... | collective-permute-start | bytes 786440 | tf_op jit(solution)/shard_map/ppermute | solution.py:133
  126.0 6.4 %collective-permute-start.27 = (bf16[64,2048]{1,0:T(8,128)(2,1)S(1)}, bf16[64,2048]{1,0:T(8,128)(2,1)S(1)}, u32[]{:S(2)}, u32[]{:S(2)}) collective-permute-start(bf16[64,2048]{1,0:T(8,128)(2,1)S(1)} %get-tuple-element.193), channel_id=1, source_target_pairs={{0,2},{1,0},{2,4},{3,1},{4,6},{5,3},{6,7},{7,5},{8,10},{9,8},{10,1... | collective-permute-start | bytes 786440 | tf_op jit(solution)/shard_map/ppermute | solution.py:133
  128.3 11.2 %collective-permute-start.36 = (bf16[64,2048]{1,0:T(8,128)(2,1)S(1)}, bf16[64,2048]{1,0:T(8,128)(2,1)S(1)}, u32[]{:S(2)}, u32[]{:S(2)}) collective-permute-start(bf16[64,2048]{1,0:T(8,128)(2,1)S(1)} %get-tuple-element.200), channel_id=1, source_target_pairs={{0,16},{8,24},{16,0},{24,8},{1,17},{9,25},{17,1},{25,9},{2,18},{10... | collective-permute-start | bytes 786440 | tf_op jit(solution)/shard_map/ppermute | solution.py:139
  129.9 13.2 %collective-permute-start.37 = (bf16[352,384]{1,0:T(8,128)(2,1)S(1)}, bf16[352,384]{1,0:T(8,128)(2,1)S(1)}, u32[]{:S(2)}, u32[]{:S(2)}) collective-permute-start(bf16[352,384]{1,0:T(8,128)(2,1)S(1)} %get-tuple-element.202), channel_id=1, source_target_pairs={{0,16},{8,24},{16,0},{24,8},{1,17},{9,25},{17,1},{25,9},{2,18},{10... | collective-permute-start | bytes 811016 | tf_op jit(solution)/shard_map/ppermute | solution.py:139
  134.3 8.8 %collective-permute-start.32 = (bf16[64,2048]{1,0:T(8,128)(2,1)S(1)}, bf16[64,2048]{1,0:T(8,128)(2,1)S(1)}, u32[]{:S(2)}, u32[]{:S(2)}) collective-permute-start(bf16[64,2048]{1,0:T(8,128)(2,1)S(1)} %get-tuple-element.175), channel_id=1, source_target_pairs={{0,1},{1,3},{2,0},{3,5},{4,2},{5,7},{6,4},{7,6},{8,9},{9,11},{10,8... | collective-permute-start | bytes 786440 | tf_op jit(solution)/shard_map/ppermute | solution.py:133
  134.8 9.8 %collective-permute-start.33 = (bf16[64,2048]{1,0:T(8,128)(2,1)S(1)}, bf16[64,2048]{1,0:T(8,128)(2,1)S(1)}, u32[]{:S(2)}, u32[]{:S(2)}) collective-permute-start(bf16[64,2048]{1,0:T(8,128)(2,1)S(1)} %get-tuple-element.174), channel_id=1, source_target_pairs={{0,2},{1,0},{2,4},{3,1},{4,6},{5,3},{6,7},{7,5},{8,10},{9,8},{10,1... | collective-permute-start | bytes 786440 | tf_op jit(solution)/shard_map/ppermute | solution.py:133
  136.3 8.7 %collective-permute-start.34 = (bf16[64,2048]{1,0:T(8,128)(2,1)S(1)}, bf16[64,2048]{1,0:T(8,128)(2,1)S(1)}, u32[]{:S(2)}, u32[]{:S(2)}) collective-permute-start(bf16[64,2048]{1,0:T(8,128)(2,1)S(1)} %get-tuple-element.176), channel_id=1, source_target_pairs={{0,1},{1,3},{2,0},{3,5},{4,2},{5,7},{6,4},{7,6},{8,9},{9,11},{10,8... | collective-permute-start | bytes 786440 | tf_op jit(solution)/shard_map/ppermute | solution.py:133
  139.5 8.8 %copy-start.6 = (bf16[640,2048]{1,0:T(8,128)(2,1)S(1)}, bf16[640,2048]{1,0:T(8,128)(2,1)}, u32[]{:S(2)}) copy-start(bf16[640,2048]{1,0:T(8,128)(2,1)} %get-tuple-element.155) | copy-start | bytes 7864324
  139.5 8.8 %copy-start.13 = (bf16[640,768]{1,0:T(8,128)(2,1)S(1)}, bf16[640,768]{1,0:T(8,128)(2,1)}, u32[]{:S(2)}) copy-start(bf16[640,768]{1,0:T(8,128)(2,1)} %get-tuple-element.156) | copy-start | bytes 2949124
  139.5 6.6 %collective-permute-start.35 = (bf16[64,2048]{1,0:T(8,128)(2,1)S(1)}, bf16[64,2048]{1,0:T(8,128)(2,1)S(1)}, u32[]{:S(2)}, u32[]{:S(2)}) collective-permute-start(bf16[64,2048]{1,0:T(8,128)(2,1)S(1)} %get-tuple-element.173), channel_id=1, source_target_pairs={{0,2},{1,0},{2,4},{3,1},{4,6},{5,3},{6,7},{7,5},{8,10},{9,8},{10,1... | collective-permute-start | bytes 786440 | tf_op jit(solution)/shard_map/ppermute | solution.py:133
  143.0 15.1 %collective-permute-start.43 = (bf16[192,2048]{1,0:T(8,128)(2,1)S(1)}, bf16[192,2048]{1,0:T(8,128)(2,1)S(1)}, u32[]{:S(2)}, u32[]{:S(2)}) collective-permute-start(bf16[192,2048]{1,0:T(8,128)(2,1)S(1)} %dynamic-slice_convert_fusion), channel_id=1, source_target_pairs={{0,8},{8,0},{16,24},{24,16},{1,9},{9,1},{17,25},{25,17},{2,10},{10... | collective-permute-start | bytes 2359304 | tf_op jit(solution)/shard_map/ppermute | solution.py:136
  143.0 14.0 %collective-permute-start.40 = (bf16[64,2048]{1,0:T(8,128)(2,1)S(1)}, bf16[64,2048]{1,0:T(8,128)(2,1)S(1)}, u32[]{:S(2)}, u32[]{:S(2)}) collective-permute-start(bf16[64,2048]{1,0:T(8,128)(2,1)S(1)} %get-tuple-element.199), channel_id=1, source_target_pairs={{0,16},{8,24},{16,0},{24,8},{1,17},{9,25},{17,1},{25,9},{2,18},{10... | collective-permute-start | bytes 786440 | tf_op jit(solution)/shard_map/ppermute | solution.py:139
  144.6 12.5 %collective-permute-start.41 = (bf16[320,384]{1,0:T(8,128)(2,1)S(1)}, bf16[320,384]{1,0:T(8,128)(2,1)S(1)}, u32[]{:S(2)}, u32[]{:S(2)}) collective-permute-start(bf16[320,384]{1,0:T(8,128)(2,1)S(1)} %slice.129), channel_id=1, source_target_pairs={{0,16},{8,24},{16,0},{24,8},{1,17},{9,25},{17,1},{25,9},{2,18},{10... | collective-permute-start | bytes 737288 | tf_op jit(solution)/shard_map/ppermute | solution.py:139
  146.2 10.8 %collective-permute-start.38 = (bf16[64,2048]{1,0:T(8,128)(2,1)S(1)}, bf16[64,2048]{1,0:T(8,128)(2,1)S(1)}, u32[]{:S(2)}, u32[]{:S(2)}) collective-permute-start(bf16[64,2048]{1,0:T(8,128)(2,1)S(1)} %get-tuple-element.172), channel_id=1, source_target_pairs={{0,1},{1,3},{2,0},{3,5},{4,2},{5,7},{6,4},{7,6},{8,9},{9,11},{10,8... | collective-permute-start | bytes 786440 | tf_op jit(solution)/shard_map/ppermute | solution.py:133
  146.7 10.3 %collective-permute-start.39 = (bf16[64,2048]{1,0:T(8,128)(2,1)S(1)}, bf16[64,2048]{1,0:T(8,128)(2,1)S(1)}, u32[]{:S(2)}, u32[]{:S(2)}) collective-permute-start(bf16[64,2048]{1,0:T(8,128)(2,1)S(1)} %get-tuple-element.171), channel_id=1, source_target_pairs={{0,2},{1,0},{2,4},{3,1},{4,6},{5,3},{6,7},{7,5},{8,10},{9,8},{10,1... | collective-permute-start | bytes 786440 | tf_op jit(solution)/shard_map/ppermute | solution.py:133
  150.1 8.1 %copy-start.8 = (f32[1,192,2048]{2,1,0:T(8,128)S(1)}, f32[1,192,2048]{2,1,0:T(8,128)}, u32[]{:S(2)}) copy-start(f32[1,192,2048]{2,1,0:T(8,128)} %param.15) | copy-start | bytes 4718596
  157.0 2.7 %collective-permute-start.42 = (bf16[1024,384]{1,0:T(8,128)(2,1)S(1)}, bf16[1024,384]{1,0:T(8,128)(2,1)S(1)}, u32[]{:S(2)}, u32[]{:S(2)}) collective-permute-start(bf16[1024,384]{1,0:T(8,128)(2,1)S(1)} %dynamic-slice_convert_fusion.1), channel_id=1, source_target_pairs={{0,8},{8,0},{16,24},{24,16},{1,9},{9,1},{17,25},{25,17},{2,10},{10... | collective-permute-start | bytes 2359304 | tf_op jit(solution)/shard_map/ppermute | solution.py:136
  158.1 1.6 copy-start.9

commit v4 on v3

--- a/solution.py
+++ b/solution.py
@@ -233,7 +233,7 @@
     def work_up_to(count):
         nonlocal done
         while done < count:
-            work(groups[done], after(full_in, *grads.values()), full_out)
+            work(groups[done], after(full_in, *grads.values()) if n > 16 else full_in, full_out)
             done += 1
             if done < len(groups):
                 for r in at_once:
@@ -245,7 +245,7 @@
             full_in = gather_in()
         if s == min(3, far):
             if far > 2:
-                hold(2, full_in)
+                got[-2][1], got[2][0] = after(got[-2][1], full_in), after(got[2][0], full_in)
             full_out = gather_out()
         if s == far > 2 and n <= 16:
             hold(s - 1, *work_up_to(within(far - 2)))

time: 162 us -> 158 us (0.975)
  waiting for transfers between devices: 67.6 us -> 63.9 us
  matrix products: 13.4 us -> 11.4 us
    ppermute x8, waiting for transfers between devices: 12.3 us -> 9.99 us  [shift_y(): lax.ppermute(x, 'dp', [(i, (i // 2 + r) % ny * 2 + i % 2) for i in range(...]
    dot_general x12, matrix products: 13.4 us -> 11.4 us  [add_up(): g = lax.dot_general(p, q, TN, preferred_element_type=f32)]
    unnamed x28 -> x30, local copies, waits for them, and re-layouts: 2.11 us -> 3.26 us
  transfers between devices with their start and end apart: 44 -> 44, of which waited for: 20 -> 20; matrix products, arithmetic and copies ran while one was open for 16% -> 15% of each run, Pallas kernels for 12% -> 13%
where the time goes in v4:
time: 158 us
  waiting for transfers between devices  63.9 us (40%)
  starting transfers between devices  41 us (26%)
  Pallas kernels  23.2 us (15%)
  matrix products  11.4 us (7%)
  other arithmetic  10.1 us (6%)
  local copies, waits for them, and re-layouts  7.01 us (4%)
    ppermute x28, waiting for transfers between devices, ring(): lax.ppermute(x, 'expert', [(i, order[(place[i] + step) % n]) for i in ran...  52.8 us
    ppermute x28, starting transfers between devices, ring(): lax.ppermute(x, 'expert', [(i, order[(place[i] + step) % n]) for i in ran...  29.5 us
    pallas_call x3, Pallas kernels, expert_rows(): pl.pallas_call(kernel, in_specs=[pl.BlockSpec(memory_space=pltpu.SMEM)] +...  20.4 us
    dot_general x12, matrix products, add_up(): g = lax.dot_general(p, q, TN, preferred_element_type=f32)  11.4 us
    ppermute x8, waiting for transfers between devices, shift_y(): lax.ppermute(x, 'dp', [(i, (i // 2 + r) % ny * 2 + i % 2) for i in range(...  9.99 us
    ppermute x8, starting transfers between devices, shift_y(): lax.ppermute(x, 'dp', [(i, (i // 2 + r) % ny * 2 + i % 2) for i in range(...  9.76 us
    unnamed x30, local copies, waits for them, and re-layouts  3.26 us
  transfers between devices with their start and end apart: 44, of which 20 were waited for; matrix products, arithmetic and copies ran while one was open for 15% of the time, Pallas kernels for 13%

profile of v4, /device:TPU:0, one launch (start us, length us, event | category | flops | bytes accessed | tf_op | source)
XLA Modules:
  0.0 157.6 jit_solution(13352965763783246204)
XLA Ops:
  0.6 2.7 %shard_map.103 = (bf16[64,4224]{1,0:T(8,128)(2,1)}, bf16[64,4224]{1,0:T(8,128)(2,1)}) custom-call(bf16[128,2048]{1,0:T(8,128)(2,1)} %tok_ref.1, bf16[128,2048]{1,0:T(8,128)(2,1)} %cot_ref.1, f32[8,128]{1,0:T(8,128)} %bitcast.31, s32[8,128]{1,0:T(8,128)} %bitcast.32), custom_call_target="tpu_custom_call" | custom-call | bytes 2097152 | tf_op jit(solution)/shard_map/pallas_call | solution.py:53
  3.3 3.0 %collective-permute-start.3 = (bf16[64,4224]{1,0:T(8,128)(2,1)}, bf16[64,4224]{1,0:T(8,128)(2,1)}, u32[]{:S(2)}, u32[]{:S(2)}) collective-permute-start(bf16[64,4224]{1,0:T(8,128)(2,1)} %get-tuple-element.97.refs_1_), channel_id=1, source_target_pairs={{0,2},{1,0},{2,4},{3,1},{4,6},{5,3},{6,7},{7,5},{8,10},{9,8},{10,1... | collective-permute-start | bytes 1622024 | tf_op jit(solution)/shard_map/ppermute | solution.py:133
  6.4 2.0 %collective-permute-start.2 = (bf16[64,4224]{1,0:T(8,128)(2,1)}, bf16[64,4224]{1,0:T(8,128)(2,1)}, u32[]{:S(2)}, u32[]{:S(2)}) collective-permute-start(bf16[64,4224]{1,0:T(8,128)(2,1)} %get-tuple-element.96.refs_0_), channel_id=1, source_target_pairs={{0,2},{1,0},{2,4},{3,1},{4,6},{5,3},{6,7},{7,5},{8,10},{9,8},{10,1... | collective-permute-start | bytes 1622024 | tf_op jit(solution)/shard_map/ppermute | solution.py:133
  8.4 2.0 %collective-permute-start.5 = (bf16[1024,384]{1,0:T(8,128)(2,1)}, bf16[1024,384]{1,0:T(8,128)(2,1)}, u32[]{:S(2)}, u32[]{:S(2)}) collective-permute-start(bf16[1024,384]{1,0:T(8,128)(2,1)} %bitcast.29), channel_id=1, source_target_pairs={{0,16},{8,24},{16,0},{24,8},{1,17},{9,25},{17,1},{25,9},{2,18},{10... | collective-permute-start | bytes 2359304 | tf_op jit(solution)/shard_map/ppermute | solution.py:139
  10.4 9.3 %collective-permute-done.3.refs_7_ = bf16[64,4224]{1,0:T(8,128)(2,1)} collective-permute-done((bf16[64,4224]{1,0:T(8,128)(2,1)}, bf16[64,4224]{1,0:T(8,128)(2,1)}, u32[]{:S(2)}, u32[]{:S(2)}) %collective-permute-start.3) | collective-permute-done | bytes 540704 | tf_op jit(solution)/shard_map/ppermute | solution.py:133
  19.7 2.2 %collective-permute-done.1.refs_2_ = bf16[64,4224]{1,0:T(8,128)(2,1)} collective-permute-done((bf16[64,4224]{1,0:T(8,128)(2,1)}, bf16[64,4224]{1,0:T(8,128)(2,1)}, u32[]{:S(2)}, u32[]{:S(2)}) %collective-permute-start.1) | collective-permute-done | bytes 540704 | tf_op jit(solution)/shard_map/ppermute | solution.py:133
  21.9 8.6 %collective-permute-done.2.refs_3_ = bf16[64,4224]{1,0:T(8,128)(2,1)} collective-permute-done((bf16[64,4224]{1,0:T(8,128)(2,1)}, bf16[64,4224]{1,0:T(8,128)(2,1)}, u32[]{:S(2)}, u32[]{:S(2)}) %collective-permute-start.2) | collective-permute-done | bytes 540704 | tf_op jit(solution)/shard_map/ppermute | solution.py:133
  30.5 1.5 collective-permute-done.refs_6_
  32.8 1.6 %collective-permute-start.8 = (bf16[64,4224]{1,0:T(8,128)(2,1)}, bf16[64,4224]{1,0:T(8,128)(2,1)}, u32[]{:S(2)}, u32[]{:S(2)}) collective-permute-start(bf16[64,4224]{1,0:T(8,128)(2,1)} %collective-permute-done.1.refs_2_), channel_id=1, source_target_pairs={{0,1},{1,3},{2,0},{3,5},{4,2},{5,7},{6,4},{7,6},{8,9},{9,11},{10,8... | collective-permute-start | bytes 1622024 | tf_op jit(solution)/shard_map/ppermute | solution.py:133
  34.9 0.7 collective-permute-done.4
  35.5 0.9 copy-done.11
  36.4 1.6 %collective-permute-start.10 = (bf16[64,4224]{1,0:T(8,128)(2,1)}, bf16[64,4224]{1,0:T(8,128)(2,1)}, u32[]{:S(2)}, u32[]{:S(2)}) collective-permute-start(bf16[64,4224]{1,0:T(8,128)(2,1)} %collective-permute-done.3.refs_7_), channel_id=1, source_target_pairs={{0,2},{1,0},{2,4},{3,1},{4,6},{5,3},{6,7},{7,5},{8,10},{9,8},{10,1... | collective-permute-start | bytes 1622024 | tf_op jit(solution)/shard_map/ppermute | solution.py:133
  38.4 0.7 copy-done.12
  39.3 1.6 %collective-permute-start.12 = (bf16[192,2048]{1,0:T(8,128)(2,1)}, bf16[192,2048]{1,0:T(8,128)(2,1)}, u32[]{:S(2)}, u32[]{:S(2)}) collective-permute-start(bf16[192,2048]{1,0:T(8,128)(2,1)} %bitcast.3), channel_id=1, source_target_pairs={{0,16},{8,24},{16,0},{24,8},{1,17},{9,25},{17,1},{25,9},{2,18},{10... | collective-permute-start | bytes 2359304 | tf_op jit(solution)/shard_map/ppermute | solution.py:139
  40.9 1.3 constant_dynamic-update-slice_fusion.3
  42.2 1.3 constant_dynamic-update-slice_fusion.2.in_ref
  43.5 6.5 %collective-permute-done.9.refs_5_ = bf16[64,4224]{1,0:T(8,128)(2,1)} collective-permute-done((bf16[64,4224]{1,0:T(8,128)(2,1)}, bf16[64,4224]{1,0:T(8,128)(2,1)}, u32[]{:S(2)}, u32[]{:S(2)}) %collective-permute-start.9) | collective-permute-done | bytes 540704 | tf_op jit(solution)/shard_map/ppermute | solution.py:133
  50.0 8.7 %collective-permute-done.8.refs_4_ = bf16[64,4224]{1,0:T(8,128)(2,1)} collective-permute-done((bf16[64,4224]{1,0:T(8,128)(2,1)}, bf16[64,4224]{1,0:T(8,128)(2,1)}, u32[]{:S(2)}, u32[]{:S(2)}) %collective-permute-start.8) | collective-permute-done | bytes 540704 | tf_op jit(solution)/shard_map/ppermute | solution.py:133
  58.7 1.4 collective-permute-done.10.refs_9_
  60.6 1.6 %collective-permute-start.14 = (bf16[64,4224]{1,0:T(8,128)(2,1)}, bf16[64,4224]{1,0:T(8,128)(2,1)S(1)}, u32[]{:S(2)}, u32[]{:S(2)}) collective-permute-start(bf16[64,4224]{1,0:T(8,128)(2,1)} %collective-permute-done.7.refs_8_), channel_id=1, source_target_pairs={{0,1},{1,3},{2,0},{3,5},{4,2},{5,7},{6,4},{7,6},{8,9},{9,11},{10,8... | collective-permute-start | bytes 1622024 | tf_op jit(solution)/shard_map/ppermute | solution.py:133
  62.6 1.6 %collective-permute-start.16 = (bf16[64,4224]{1,0:T(8,128)(2,1)}, bf16[64,4224]{1,0:T(8,128)(2,1)}, u32[]{:S(2)}, u32[]{:S(2)}) collective-permute-start(bf16[64,4224]{1,0:T(8,128)(2,1)} %collective-permute-done.8.refs_4_), channel_id=1, source_target_pairs={{0,1},{1,3},{2,0},{3,5},{4,2},{5,7},{6,4},{7,6},{8,9},{9,11},{10,8... | collective-permute-start | bytes 1622024 | tf_op jit(solution)/shard_map/ppermute | solution.py:133
  64.7 1.5 broadcast_select_fusion.3
  66.2 1.5 broadcast_select_fusion.1
  67.7 1.8 %pad_maximum_fusion.out_ref = bf16[768,2048]{1,0:T(8,128)(2,1)} fusion(bf16[192,2048]{1,0:T(8,128)(2,1)S(1)} %get-tuple-element.184, bf16[192,2048]{1,0:T(8,128)(2,1)S(1)} %get-tuple-element.183, bf16[192,2048]{1,0:T(8,128)(2,1)S(1)} %get-tuple-element.182, bf16[192,2048]{1,0:T(8,128)(2,1)S(1)} %get-tuple-element.181), kind=kLoop, calls=%fused_computation | loop fusion | flops 12582912 | bytes 6291456 | tf_op jit(solution)/shard_map/concatenate | solution.py:184
  69.5 13.0 %shard_map.104 = (bf16[640,768]{1,0:T(8,128)(2,1)S(1)}, bf16[640,768]{1,0:T(8,128)(2,1)}, bf16[640,2048]{1,0:T(8,128)(2,1)}, bf16[640,2048]{1,0:T(8,128)(2,1)}, bf16[640,2048]{1,0:T(8,128)(2,1)}) custom-call(s32[2]{0:T(128)S(1)} %fusion.20.id_ref, bf16[2048,768]{1,0:T(8,128)(2,1)} %copy-done.1, bf16[768,2048]{1,0:T(8,128)(2,1)} %pad_maximum_fusion.out_ref, ...), custom_call_target="tpu_custom_call" | custom-call | flops 1048576 | bytes 65536 | tf_op jit(solution)/shard_map/pallas_call | solution.py:101
  82.5 1.6 %collective-permute-start.15 = (bf16[64,4224]{1,0:T(8,128)(2,1)S(1)}, bf16[64,4224]{1,0:T(8,128)(2,1)S(1)}, u32[]{:S(2)}, u32[]{:S(2)}) collective-permute-start(bf16[64,4224]{1,0:T(8,128)(2,1)S(1)} %collective-permute-done.14.refs_2_), channel_id=1, source_target_pairs={{0,1},{1,3},{2,0},{3,5},{4,2},{5,7},{6,4},{7,6},{8,9},{9,11},{10,8... | collective-permute-start | bytes 1622024 | tf_op jit(solution)/shard_map/ppermute | solution.py:133
  84.6 4.7 %collective-permute-done.17.refs_1_ = bf16[64,4224]{1,0:T(8,128)(2,1)} collective-permute-done((bf16[64,4224]{1,0:T(8,128)(2,1)}, bf16[64,4224]{1,0:T(8,128)(2,1)}, u32[]{:S(2)}, u32[]{:S(2)}) %collective-permute-start.17) | collective-permute-done | bytes 540704 | tf_op jit(solution)/shard_map/ppermute | solution.py:133
  89.3 4.2 %shard_map.105 = (bf16[256,768]{1,0:T(8,128)(2,1)S(1)}, bf16[256,768]{1,0:T(8,128)(2,1)S(1)}, bf16[256,2048]{1,0:T(8,128)(2,1)S(1)}, bf16[256,2048]{1,0:T(8,128)(2,1)S(1)}, bf16[256,2048]{1,0:T(8,128)(2,1)S(1)}) custom-call(s32[2]{0:T(128)S(1)} %fusion.20.id_ref, bf16[2048,768]{1,0:T(8,128)(2,1)S(1)} %copy-done.2, bf16[768,2048]{1,0:T(8,128)(2,1)S(1)} %copy-done, ...), custom_call_target="tpu_custom_call" | custom-call | flops 1048576 | bytes 65536 | tf_op jit(solution)/shard_map/pallas_call | solution.py:101
  93.5 1.6 %collective-permute-start.22 = (bf16[64,2048]{1,0:T(8,128)(2,1)S(1)}, bf16[64,2048]{1,0:T(8,128)(2,1)S(1)}, u32[]{:S(2)}, u32[]{:S(2)}) collective-permute-start(bf16[64,2048]{1,0:T(8,128)(2,1)S(1)} %get-tuple-element.187), channel_id=1, source_target_pairs={{0,1},{1,3},{2,0},{3,5},{4,2},{5,7},{6,4},{7,6},{8,9},{9,11},{10,8... | collective-permute-start | bytes 786440 | tf_op jit(solution)/shard_map/ppermute | solution.py:133
  95.6 1.4 fusion.6
  97.1 0.6 convolution_add_fusion.3
  97.7 1.1 copy-done.6
  99.0 1.7 %fusion.4 = f32[2048,384]{1,0:T(8,128)S(1)} fusion(bf16[640,2048]{1,0:T(8,128)(2,1)S(1)} %copy-done.6, bf16[640,768]{1,0:T(8,128)(2,1)S(1)} %copy-done.13), kind=kOutput, calls=%fused_computation.36 | convolution fusion | flops 1006632960 | bytes 6258688 | tf_op jit(solution)/shard_map/dot_general | solution.py:218
  100.8 0.7 convolution_add_fusion.2
  101.5 3.3 %shard_map.106 = (bf16[128,768]{1,0:T(8,128)(2,1)S(1)}, bf16[128,768]{1,0:T(8,128)(2,1)S(1)}, bf16[128,2048]{1,0:T(8,128)(2,1)S(1)}, bf16[128,2048]{1,0:T(8,128)(2,1)S(1)}, bf16[128,2048]{1,0:T(8,128)(2,1)S(1)}) custom-call(s32[2]{0:T(128)S(1)} %fusion.20.id_ref, bf16[2048,768]{1,0:T(8,128)(2,1)S(1)} %copy-done.2, bf16[768,2048]{1,0:T(8,128)(2,1)S(1)} %copy-done, ...), custom_call_target="tpu_custom_call" | custom-call | flops 1048576 | bytes 65536 | tf_op jit(solution)/shard_map/pallas_call | solution.py:101
  105.6 0.6 convolution_add_fusion
  107.9 1.6 %collective-permute-start.20 = (bf16[64,2048]{1,0:T(8,128)(2,1)S(1)}, bf16[64,2048]{1,0:T(8,128)(2,1)S(1)}, u32[]{:S(2)}, u32[]{:S(2)}) collective-permute-start(bf16[64,2048]{1,0:T(8,128)(2,1)S(1)} %get-tuple-element.197), channel_id=1, source_target_pairs={{0,1},{1,3},{2,0},{3,5},{4,2},{5,7},{6,4},{7,6},{8,9},{9,11},{10,8... | collective-permute-start | bytes 786440 | tf_op jit(solution)/shard_map/ppermute | solution.py:133
  109.9 5.3 %collective-permute-done.21 = bf16[64,2048]{1,0:T(8,128)(2,1)S(1)} collective-permute-done((bf16[64,2048]{1,0:T(8,128)(2,1)S(1)}, bf16[64,2048]{1,0:T(8,128)(2,1)S(1)}, u32[]{:S(2)}, u32[]{:S(2)}) %collective-permute-start.21) | collective-permute-done | bytes 262176 | tf_op jit(solution)/shard_map/ppermute | solution.py:133
  115.2 1.0 collective-permute-done.20
  116.7 1.6 %collective-permute-start.30 = (bf16[64,2048]{1,0:T(8,128)(2,1)S(1)}, bf16[64,2048]{1,0:T(8,128)(2,1)S(1)}, u32[]{:S(2)}, u32[]{:S(2)}) collective-permute-start(bf16[64,2048]{1,0:T(8,128)(2,1)S(1)} %get-tuple-element.193), channel_id=1, source_target_pairs={{0,16},{8,24},{16,0},{24,8},{1,17},{9,25},{17,1},{25,9},{2,18},{10... | collective-permute-start | bytes 786440 | tf_op jit(solution)/shard_map/ppermute | solution.py:139
  118.7 1.6 %collective-permute-start.26 = (bf16[64,2048]{1,0:T(8,128)(2,1)S(1)}, bf16[64,2048]{1,0:T(8,128)(2,1)S(1)}, u32[]{:S(2)}, u32[]{:S(2)}) collective-permute-start(bf16[64,2048]{1,0:T(8,128)(2,1)S(1)} %get-tuple-element.186), channel_id=1, source_target_pairs={{0,1},{1,3},{2,0},{3,5},{4,2},{5,7},{6,4},{7,6},{8,9},{9,11},{10,8... | collective-permute-start | bytes 786440 | tf_op jit(solution)/shard_map/ppermute | solution.py:133
  121.3 0.7 fusion.10
  122.0 0.6 fusion.16
  122.6 1.8 %add_add_fusion.1 = f32[2048,384]{1,0:T(8,128)S(1)} fusion(f32[2048,384]{1,0:T(8,128)S(1)} %fusion.16, f32[2048,384]{1,0:T(8,128)S(1)} %fusion.10, bf16[640,2048]{1,0:T(8,128)(2,1)S(1)} %copy-done.6, bf16[640,768]{1,0:T(8,128)(2,1)S(1)} %copy-done.14), kind=kOutput, calls=%fused_computation.2 | convolution fusion | flops 1008205824 | bytes 12550144 | tf_op jit(solution)/shard_map/dot_general | solution.py:218
  124.5 1.5 collective-permute-done.30
  126.0 1.6 %collective-permute-start.28 = (bf16[64,2048]{1,0:T(8,128)(2,1)S(1)}, bf16[64,2048]{1,0:T(8,128)(2,1)S(1)}, u32[]{:S(2)}, u32[]{:S(2)}) collective-permute-start(bf16[64,2048]{1,0:T(8,128)(2,1)S(1)} %get-tuple-element.170), channel_id=1, source_target_pairs={{0,1},{1,3},{2,0},{3,5},{4,2},{5,7},{6,4},{7,6},{8,9},{9,11},{10,8... | collective-permute-start | bytes 786440 | tf_op jit(solution)/shard_map/ppermute | solution.py:133
  128.2 1.6 %collective-permute-start.36 = (bf16[64,2048]{1,0:T(8,128)(2,1)S(1)}, bf16[64,2048]{1,0:T(8,128)(2,1)S(1)}, u32[]{:S(2)}, u32[]{:S(2)}) collective-permute-start(bf16[64,2048]{1,0:T(8,128)(2,1)S(1)} %get-tuple-element.192), channel_id=1, source_target_pairs={{0,16},{8,24},{16,0},{24,8},{1,17},{9,25},{17,1},{25,9},{2,18},{10... | collective-permute-start | bytes 786440 | tf_op jit(solution)/shard_map/ppermute | solution.py:139
  130.3 0.8 collective-permute-done.29
  131.1 1.2 collective-permute-done.28
  133.3 0.8 collective-permute-start.33
  134.1 1.2 collective-permute-start.32
  135.3 2.2 %collective-permute-done.36 = bf16[64,2048]{1,0:T(8,128)(2,1)S(1)} collective-permute-done((bf16[64,2048]{1,0:T(8,128)(2,1)S(1)}, bf16[64,2048]{1,0:T(8,128)(2,1)S(1)}, u32[]{:S(2)}, u32[]{:S(2)}) %collective-permute-start.36) | collective-permute-done | bytes 262176 | tf_op jit(solution)/shard_map/ppermute | solution.py:139
  137.5 1.6 %collective-permute-start.34 = (bf16[64,2048]{1,0:T(8,128)(2,1)S(1)}, bf16[64,2048]{1,0:T(8,128)(2,1)S(1)}, u32[]{:S(2)}, u32[]{:S(2)}) collective-permute-start(bf16[64,2048]{1,0:T(8,128)(2,1)S(1)} %get-tuple-element.168), channel_id=1, source_target_pairs={{0,1},{1,3},{2,0},{3,5},{4,2},{5,7},{6,4},{7,6},{8,9},{9,11},{10,8... | collective-permute-start | bytes 786440 | tf_op jit(solution)/shard_map/ppermute | solution.py:133
  139.7 1.8 %collective-permute-done.37 = bf16[352,384]{1,0:T(8,128)(2,1)S(1)} collective-permute-done((bf16[352,384]{1,0:T(8,128)(2,1)S(1)}, bf16[352,384]{1,0:T(8,128)(2,1)S(1)}, u32[]{:S(2)}, u32[]{:S(2)}) %collective-permute-start.37) | collective-permute-done | bytes 270368 | tf_op jit(solution)/shard_map/ppermute | solution.py:139
  141.5 1.5 collective-permute-start.41
  143.5 1.5 collective-permute-done.34
  145.1 0.9 collective-permute-start.39
  146.0 1.2 collective-permute-start.38
  147.2 1.4 add_add_fusion
  148.8 1.6 %collective-permute-done.41 = bf16[320,384]{1,0:T(8,128)(2,1)S(1)} collective-permute-done((bf16[320,384]{1,0:T(8,128)(2,1)S(1)}, bf16[320,384]{1,0:T(8,128)(2,1)S(1)}, u32[]{:S(2)}, u32[]{:S(2)}) %collective-permute-start.41) | collective-permute-done | bytes 245792 | tf_op jit(solution)/shard_map/ppermute | solution.py:139
  150.4 2.9 %collective-permute-done.40 = bf16[64,2048]{1,0:T(8,128)(2,1)S(1)} collective-permute-done((bf16[64,2048]{1,0:T(8,128)(2,1)S(1)}, bf16[64,2048]{1,0:T(8,128)(2,1)S(1)}, u32[]{:S(2)}, u32[]{:S(2)}) %collective-permute-start.40) | collective-permute-done | bytes 262176 | tf_op jit(solution)/shard_map/ppermute | solution.py:139
  153.5 0.8 pad_maximum_fusion.1
  154.3 1.5 fusion.1
  156.1 1.6 fusion
  (98 shorter events, 13.0 us)
Async XLA Ops:
  3.3 16.4 %collective-permute-start.3 = (bf16[64,4224]{1,0:T(8,128)(2,1)}, bf16[64,4224]{1,0:T(8,128)(2,1)}, u32[]{:S(2)}, u32[]{:S(2)}) collective-permute-start(bf16[64,4224]{1,0:T(8,128)(2,1)} %get-tuple-element.97.refs_1_), channel_id=1, source_target_pairs={{0,2},{1,0},{2,4},{3,1},{4,6},{5,3},{6,7},{7,5},{8,10},{9,8},{10,1... | collective-permute-start | bytes 1622024 | tf_op jit(solution)/shard_map/ppermute | solution.py:133
  6.4 15.5 %collective-permute-start.1 = (bf16[64,4224]{1,0:T(8,128)(2,1)}, bf16[64,4224]{1,0:T(8,128)(2,1)}, u32[]{:S(2)}, u32[]{:S(2)}) collective-permute-start(bf16[64,4224]{1,0:T(8,128)(2,1)} %get-tuple-element.97.refs_1_), channel_id=1, source_target_pairs={{0,1},{1,3},{2,0},{3,5},{4,2},{5,7},{6,4},{7,6},{8,9},{9,11},{10,8... | collective-permute-start | bytes 1622024 | tf_op jit(solution)/shard_map/ppermute | solution.py:133
  6.4 24.1 %collective-permute-start.2 = (bf16[64,4224]{1,0:T(8,128)(2,1)}, bf16[64,4224]{1,0:T(8,128)(2,1)}, u32[]{:S(2)}, u32[]{:S(2)}) collective-permute-start(bf16[64,4224]{1,0:T(8,128)(2,1)} %get-tuple-element.96.refs_0_), channel_id=1, source_target_pairs={{0,2},{1,0},{2,4},{3,1},{4,6},{5,3},{6,7},{7,5},{8,10},{9,8},{10,1... | collective-permute-start | bytes 1622024 | tf_op jit(solution)/shard_map/ppermute | solution.py:133
  8.4 23.6 %collective-permute-start = (bf16[64,4224]{1,0:T(8,128)(2,1)}, bf16[64,4224]{1,0:T(8,128)(2,1)}, u32[]{:S(2)}, u32[]{:S(2)}) collective-permute-start(bf16[64,4224]{1,0:T(8,128)(2,1)} %get-tuple-element.96.refs_0_), channel_id=1, source_target_pairs={{0,1},{1,3},{2,0},{3,5},{4,2},{5,7},{6,4},{7,6},{8,9},{9,11},{10,8... | collective-permute-start | bytes 1622024 | tf_op jit(solution)/shard_map/ppermute | solution.py:133
  8.4 23.6 %collective-permute-start.5 = (bf16[1024,384]{1,0:T(8,128)(2,1)}, bf16[1024,384]{1,0:T(8,128)(2,1)}, u32[]{:S(2)}, u32[]{:S(2)}) collective-permute-start(bf16[1024,384]{1,0:T(8,128)(2,1)} %bitcast.29), channel_id=1, source_target_pairs={{0,16},{8,24},{16,0},{24,8},{1,17},{9,25},{17,1},{25,9},{2,18},{10... | collective-permute-start | bytes 2359304 | tf_op jit(solution)/shard_map/ppermute | solution.py:139
  32.0 3.5 %collective-permute-start.4 = (bf16[1024,384]{1,0:T(8,128)(2,1)}, bf16[1024,384]{1,0:T(8,128)(2,1)S(1)}, u32[]{:S(2)}, u32[]{:S(2)}) collective-permute-start(bf16[1024,384]{1,0:T(8,128)(2,1)} %bitcast.30), channel_id=1, source_target_pairs={{0,8},{8,0},{16,24},{24,16},{1,9},{9,1},{17,25},{25,17},{2,10},{10... | collective-permute-start | bytes 2359304 | tf_op jit(solution)/shard_map/ppermute | solution.py:136
  32.0 7.3 %collective-permute-start.6 = (bf16[1024,384]{1,0:T(8,128)(2,1)}, bf16[1024,384]{1,0:T(8,128)(2,1)}, u32[]{:S(2)}, u32[]{:S(2)}) collective-permute-start(bf16[1024,384]{1,0:T(8,128)(2,1)} %collective-permute-done.5), channel_id=1, source_target_pairs={{0,8},{8,0},{16,24},{24,16},{1,9},{9,1},{17,25},{25,17},{2,10},{10... | collective-permute-start | bytes 2359304 | tf_op jit(solution)/shard_map/ppermute | solution.py:136
  32.5 5.7 %copy-start.10 = (bf16[1,1024,384]{2,1,0:T(8,128)(2,1)S(1)}, bf16[1,1024,384]{2,1,0:T(8,128)(2,1)}, u32[]{:S(2)}) copy-start(bf16[1,1024,384]{2,1,0:T(8,128)(2,1)} %param.12) | copy-start | bytes 2359300
  32.5 26.1 %collective-permute-start.7 = (bf16[64,4224]{1,0:T(8,128)(2,1)}, bf16[64,4224]{1,0:T(8,128)(2,1)}, u32[]{:S(2)}, u32[]{:S(2)}) collective-permute-start(bf16[64,4224]{1,0:T(8,128)(2,1)} %collective-permute-done.refs_6_), channel_id=1, source_target_pairs={{0,1},{1,3},{2,0},{3,5},{4,2},{5,7},{6,4},{7,6},{8,9},{9,11},{10,8... | collective-permute-start | bytes 1622024 | tf_op jit(solution)/shard_map/ppermute | solution.py:133
  32.8 25.8 %collective-permute-start.8 = (bf16[64,4224]{1,0:T(8,128)(2,1)}, bf16[64,4224]{1,0:T(8,128)(2,1)}, u32[]{:S(2)}, u32[]{:S(2)}) collective-permute-start(bf16[64,4224]{1,0:T(8,128)(2,1)} %collective-permute-done.1.refs_2_), channel_id=1, source_target_pairs={{0,1},{1,3},{2,0},{3,5},{4,2},{5,7},{6,4},{7,6},{8,9},{9,11},{10,8... | collective-permute-start | bytes 1622024 | tf_op jit(solution)/shard_map/ppermute | solution.py:133
  34.5 15.5 %collective-permute-start.9 = (bf16[64,4224]{1,0:T(8,128)(2,1)}, bf16[64,4224]{1,0:T(8,128)(2,1)}, u32[]{:S(2)}, u32[]{:S(2)}) collective-permute-start(bf16[64,4224]{1,0:T(8,128)(2,1)} %collective-permute-done.2.refs_3_), channel_id=1, source_target_pairs={{0,2},{1,0},{2,4},{3,1},{4,6},{5,3},{6,7},{7,5},{8,10},{9,8},{10,1... | collective-permute-start | bytes 1622024 | tf_op jit(solution)/shard_map/ppermute | solution.py:133
  35.5 0.9 copy-start.11
  36.4 23.6 %collective-permute-start.10 = (bf16[64,4224]{1,0:T(8,128)(2,1)}, bf16[64,4224]{1,0:T(8,128)(2,1)}, u32[]{:S(2)}, u32[]{:S(2)}) collective-permute-start(bf16[64,4224]{1,0:T(8,128)(2,1)} %collective-permute-done.3.refs_7_), channel_id=1, source_target_pairs={{0,2},{1,0},{2,4},{3,1},{4,6},{5,3},{6,7},{7,5},{8,10},{9,8},{10,1... | collective-permute-start | bytes 1622024 | tf_op jit(solution)/shard_map/ppermute | solution.py:133
  38.0 1.1 copy-start.12
  39.3 20.7 %collective-permute-start.12 = (bf16[192,2048]{1,0:T(8,128)(2,1)}, bf16[192,2048]{1,0:T(8,128)(2,1)}, u32[]{:S(2)}, u32[]{:S(2)}) collective-permute-start(bf16[192,2048]{1,0:T(8,128)(2,1)} %bitcast.3), channel_id=1, source_target_pairs={{0,16},{8,24},{16,0},{24,8},{1,17},{9,25},{17,1},{25,9},{2,18},{10... | collective-permute-start | bytes 2359304 | tf_op jit(solution)/shard_map/ppermute | solution.py:139
  43.5 24.2 %copy-start.1 = (bf16[2048,768]{1,0:T(8,128)(2,1)}, bf16[2048,768]{1,0:T(8,128)(2,1)S(1)}, u32[]{:S(2)}) copy-start(bf16[2048,768]{1,0:T(8,128)(2,1)S(1)} %constant_dynamic-update-slice_fusion.2.in_ref) | copy-start | bytes 9437188
  60.0 4.2 %collective-permute-start.11 = (bf16[192,2048]{1,0:T(8,128)(2,1)}, bf16[192,2048]{1,0:T(8,128)(2,1)}, u32[]{:S(2)}, u32[]{:S(2)}) collective-permute-start(bf16[192,2048]{1,0:T(8,128)(2,1)} %bitcast.3), channel_id=1, source_target_pairs={{0,8},{8,0},{16,24},{24,16},{1,9},{9,1},{17,25},{25,17},{2,10},{10... | collective-permute-start | bytes 2359304 | tf_op jit(solution)/shard_map/ppermute | solution.py:136
  60.0 6.1 %collective-permute-start.13 = (bf16[192,2048]{1,0:T(8,128)(2,1)}, bf16[192,2048]{1,0:T(8,128)(2,1)}, u32[]{:S(2)}, u32[]{:S(2)}) collective-permute-start(bf16[192,2048]{1,0:T(8,128)(2,1)} %collective-permute-done.12), channel_id=1, source_target_pairs={{0,8},{8,0},{16,24},{24,16},{1,9},{9,1},{17,25},{25,17},{2,10},{10... | collective-permute-start | bytes 2359304 | tf_op jit(solution)/shard_map/ppermute | solution.py:136
  60.6 21.9 %collective-permute-start.14 = (bf16[64,4224]{1,0:T(8,128)(2,1)}, bf16[64,4224]{1,0:T(8,128)(2,1)S(1)}, u32[]{:S(2)}, u32[]{:S(2)}) collective-permute-start(bf16[64,4224]{1,0:T(8,128)(2,1)} %collective-permute-done.7.refs_8_), channel_id=1, source_target_pairs={{0,1},{1,3},{2,0},{3,5},{4,2},{5,7},{6,4},{7,6},{8,9},{9,11},{10,8... | collective-permute-start | bytes 1622024 | tf_op jit(solution)/shard_map/ppermute | solution.py:133
  62.2 21.9 %collective-permute-start.18 = (bf16[64,4224]{1,0:T(8,128)(2,1)}, bf16[64,4224]{1,0:T(8,128)(2,1)}, u32[]{:S(2)}, u32[]{:S(2)}) collective-permute-start(bf16[64,4224]{1,0:T(8,128)(2,1)} %collective-permute-done.10.refs_9_), channel_id=1, source_target_pairs={{0,2},{1,0},{2,4},{3,1},{4,6},{5,3},{6,7},{7,5},{8,10},{9,8},{10,1... | collective-permute-start | bytes 1622024 | tf_op jit(solution)/shard_map/ppermute | solution.py:133
  62.6 26.6 %collective-permute-start.16 = (bf16[64,4224]{1,0:T(8,128)(2,1)}, bf16[64,4224]{1,0:T(8,128)(2,1)}, u32[]{:S(2)}, u32[]{:S(2)}) collective-permute-start(bf16[64,4224]{1,0:T(8,128)(2,1)} %collective-permute-done.8.refs_4_), channel_id=1, source_target_pairs={{0,1},{1,3},{2,0},{3,5},{4,2},{5,7},{6,4},{7,6},{8,9},{9,11},{10,8... | collective-permute-start | bytes 1622024 | tf_op jit(solution)/shard_map/ppermute | solution.py:133
  64.2 25.1 %collective-permute-start.17 = (bf16[64,4224]{1,0:T(8,128)(2,1)}, bf16[64,4224]{1,0:T(8,128)(2,1)}, u32[]{:S(2)}, u32[]{:S(2)}) collective-permute-start(bf16[64,4224]{1,0:T(8,128)(2,1)} %collective-permute-done.9.refs_5_), channel_id=1, source_target_pairs={{0,2},{1,0},{2,4},{3,1},{4,6},{5,3},{6,7},{7,5},{8,10},{9,8},{10,1... | collective-permute-start | bytes 1622024 | tf_op jit(solution)/shard_map/ppermute | solution.py:133
  67.6 1.9 %copy-start.3 = (bf16[64,4224]{1,0:T(8,128)(2,1)S(1)}, bf16[64,4224]{1,0:T(8,128)(2,1)}, u32[]{:S(2)}) copy-start(bf16[64,4224]{1,0:T(8,128)(2,1)} %get-tuple-element.96.refs_0_) | copy-start | bytes 1622020
  67.7 1.9 %copy-start.4 = (bf16[64,4224]{1,0:T(8,128)(2,1)S(1)}, bf16[64,4224]{1,0:T(8,128)(2,1)}, u32[]{:S(2)}) copy-start(bf16[64,4224]{1,0:T(8,128)(2,1)} %get-tuple-element.97.refs_1_) | copy-start | bytes 1622020
  69.5 19.8 %copy-start = (bf16[768,2048]{1,0:T(8,128)(2,1)S(1)}, bf16[768,2048]{1,0:T(8,128)(2,1)}, u32[]{:S(2)}) copy-start(bf16[768,2048]{1,0:T(8,128)(2,1)} %pad_maximum_fusion.out_ref) | copy-start | bytes 9437188
  69.5 19.8 %copy-start.2 = (bf16[2048,768]{1,0:T(8,128)(2,1)S(1)}, bf16[2048,768]{1,0:T(8,128)(2,1)}, u32[]{:S(2)}) copy-start(bf16[2048,768]{1,0:T(8,128)(2,1)} %copy-done.1) | copy-start | bytes 9437188
  82.5 13.1 %copy-start.5 = (bf16[640,2048]{1,0:T(8,128)(2,1)S(1)}, bf16[640,2048]{1,0:T(8,128)(2,1)}, u32[]{:S(2)}) copy-start(bf16[640,2048]{1,0:T(8,128)(2,1)} %get-tuple-element.157) | copy-start | bytes 7864324
  82.5 19.0 %collective-permute-start.15 = (bf16[64,4224]{1,0:T(8,128)(2,1)S(1)}, bf16[64,4224]{1,0:T(8,128)(2,1)S(1)}, u32[]{:S(2)}, u32[]{:S(2)}) collective-permute-start(bf16[64,4224]{1,0:T(8,128)(2,1)S(1)} %collective-permute-done.14.refs_2_), channel_id=1, source_target_pairs={{0,1},{1,3},{2,0},{3,5},{4,2},{5,7},{6,4},{7,6},{8,9},{9,11},{10,8... | collective-permute-start | bytes 1622024 | tf_op jit(solution)/shard_map/ppermute | solution.py:133
  84.1 17.4 %collective-permute-start.19 = (bf16[64,4224]{1,0:T(8,128)(2,1)}, bf16[64,4224]{1,0:T(8,128)(2,1)S(1)}, u32[]{:S(2)}, u32[]{:S(2)}) collective-permute-start(bf16[64,4224]{1,0:T(8,128)(2,1)} %collective-permute-done.18.refs_3_), channel_id=1, source_target_pairs={{0,2},{1,0},{2,4},{3,1},{4,6},{5,3},{6,7},{7,5},{8,10},{9,8},{10,1... | collective-permute-start | bytes 1622024 | tf_op jit(solution)/shard_map/ppermute | solution.py:133
  93.5 16.4 %collective-permute-start.22 = (bf16[64,2048]{1,0:T(8,128)(2,1)S(1)}, bf16[64,2048]{1,0:T(8,128)(2,1)S(1)}, u32[]{:S(2)}, u32[]{:S(2)}) collective-permute-start(bf16[64,2048]{1,0:T(8,128)(2,1)S(1)} %get-tuple-element.187), channel_id=1, source_target_pairs={{0,1},{1,3},{2,0},{3,5},{4,2},{5,7},{6,4},{7,6},{8,9},{9,11},{10,8... | collective-permute-start | bytes 786440 | tf_op jit(solution)/shard_map/ppermute | solution.py:133
  95.2 14.8 %collective-permute-start.23 = (bf16[64,2048]{1,0:T(8,128)(2,1)S(1)}, bf16[64,2048]{1,0:T(8,128)(2,1)S(1)}, u32[]{:S(2)}, u32[]{:S(2)}) collective-permute-start(bf16[64,2048]{1,0:T(8,128)(2,1)S(1)} %get-tuple-element.188), channel_id=1, source_target_pairs={{0,2},{1,0},{2,4},{3,1},{4,6},{5,3},{6,7},{7,5},{8,10},{9,8},{10,1... | collective-permute-start | bytes 786440 | tf_op jit(solution)/shard_map/ppermute | solution.py:133
  97.0 1.7 %copy-start.6 = (bf16[640,2048]{1,0:T(8,128)(2,1)S(1)}, bf16[640,2048]{1,0:T(8,128)(2,1)}, u32[]{:S(2)}) copy-start(bf16[640,2048]{1,0:T(8,128)(2,1)} %get-tuple-element.147) | copy-start | bytes 7864324
  97.0 2.0 %copy-start.13 = (bf16[640,768]{1,0:T(8,128)(2,1)S(1)}, bf16[640,768]{1,0:T(8,128)(2,1)}, u32[]{:S(2)}) copy-start(bf16[640,768]{1,0:T(8,128)(2,1)} %get-tuple-element.148) | copy-start | bytes 2949124
  105.5 2.4 %collective-permute-start.24 = (bf16[192,2048]{1,0:T(8,128)(2,1)S(1)}, bf16[192,2048]{1,0:T(8,128)(2,1)S(1)}, u32[]{:S(2)}, u32[]{:S(2)}) collective-permute-start(bf16[192,2048]{1,0:T(8,128)(2,1)S(1)} %dynamic-slice_convert_fusion.3), channel_id=1, source_target_pairs={{0,8},{8,0},{16,24},{24,16},{1,9},{9,1},{17,25},{25,17},{2,10},{10... | collective-permute-start | bytes 2359304 | tf_op jit(solution)/shard_map/ppermute | solution.py:136
  106.3 3.4 %collective-permute-start.25 = (bf16[1024,384]{1,0:T(8,128)(2,1)S(1)}, bf16[1024,384]{1,0:T(8,128)(2,1)S(1)}, u32[]{:S(2)}, u32[]{:S(2)}) collective-permute-start(bf16[1024,384]{1,0:T(8,128)(2,1)S(1)} %dynamic-slice_convert_fusion.2), channel_id=1, source_target_pairs={{0,8},{8,0},{16,24},{24,16},{1,9},{9,1},{17,25},{25,17},{2,10},{10... | collective-permute-start | bytes 2359304 | tf_op jit(solution)/shard_map/ppermute | solution.py:136
  106.9 8.3 %collective-permute-start.21 = (bf16[64,2048]{1,0:T(8,128)(2,1)S(1)}, bf16[64,2048]{1,0:T(8,128)(2,1)S(1)}, u32[]{:S(2)}, u32[]{:S(2)}) collective-permute-start(bf16[64,2048]{1,0:T(8,128)(2,1)S(1)} %get-tuple-element.196), channel_id=1, source_target_pairs={{0,2},{1,0},{2,4},{3,1},{4,6},{5,3},{6,7},{7,5},{8,10},{9,8},{10,1... | collective-permute-start | bytes 786440 | tf_op jit(solution)/shard_map/ppermute | solution.py:133
  107.9 8.3 %collective-permute-start.20 = (bf16[64,2048]{1,0:T(8,128)(2,1)S(1)}, bf16[64,2048]{1,0:T(8,128)(2,1)S(1)}, u32[]{:S(2)}, u32[]{:S(2)}) collective-permute-start(bf16[64,2048]{1,0:T(8,128)(2,1)S(1)} %get-tuple-element.197), channel_id=1, source_target_pairs={{0,1},{1,3},{2,0},{3,5},{4,2},{5,7},{6,4},{7,6},{8,9},{9,11},{10,8... | collective-permute-start | bytes 786440 | tf_op jit(solution)/shard_map/ppermute | solution.py:133
  109.7 6.8 %copy-start.7 = (bf16[640,2048]{1,0:T(8,128)(2,1)S(1)}, bf16[640,2048]{1,0:T(8,128)(2,1)}, u32[]{:S(2)}) copy-start(bf16[640,2048]{1,0:T(8,128)(2,1)} %get-tuple-element.106) | copy-start | bytes 7864324
  116.7 9.3 %collective-permute-start.30 = (bf16[64,2048]{1,0:T(8,128)(2,1)S(1)}, bf16[64,2048]{1,0:T(8,128)(2,1)S(1)}, u32[]{:S(2)}, u32[]{:S(2)}) collective-permute-start(bf16[64,2048]{1,0:T(8,128)(2,1)S(1)} %get-tuple-element.193), channel_id=1, source_target_pairs={{0,16},{8,24},{16,0},{24,8},{1,17},{9,25},{17,1},{25,9},{2,18},{10... | collective-permute-start | bytes 786440 | tf_op jit(solution)/shard_map/ppermute | solution.py:139
  118.3 9.9 %collective-permute-start.27 = (bf16[64,2048]{1,0:T(8,128)(2,1)S(1)}, bf16[64,2048]{1,0:T(8,128)(2,1)S(1)}, u32[]{:S(2)}, u32[]{:S(2)}) collective-permute-start(bf16[64,2048]{1,0:T(8,128)(2,1)S(1)} %get-tuple-element.185), channel_id=1, source_target_pairs={{0,2},{1,0},{2,4},{3,1},{4,6},{5,3},{6,7},{7,5},{8,10},{9,8},{10,1... | collective-permute-start | bytes 786440 | tf_op jit(solution)/shard_map/ppermute | solution.py:133
  118.7 11.1 %collective-permute-start.26 = (bf16[64,2048]{1,0:T(8,128)(2,1)S(1)}, bf16[64,2048]{1,0:T(8,128)(2,1)S(1)}, u32[]{:S(2)}, u32[]{:S(2)}) collective-permute-start(bf16[64,2048]{1,0:T(8,128)(2,1)S(1)} %get-tuple-element.186), channel_id=1, source_target_pairs={{0,1},{1,3},{2,0},{3,5},{4,2},{5,7},{6,4},{7,6},{8,9},{9,11},{10,8... | collective-permute-start | bytes 786440 | tf_op jit(solution)/shard_map/ppermute | solution.py:133
  120.3 12.1 %collective-permute-start.31 = (bf16[352,384]{1,0:T(8,128)(2,1)S(1)}, bf16[352,384]{1,0:T(8,128)(2,1)S(1)}, u32[]{:S(2)}, u32[]{:S(2)}) collective-permute-start(bf16[352,384]{1,0:T(8,128)(2,1)S(1)} %get-tuple-element.195), channel_id=1, source_target_pairs={{0,16},{8,24},{16,0},{24,8},{1,17},{9,25},{17,1},{25,9},{2,18},{10... | collective-permute-start | bytes 811016 | tf_op jit(solution)/shard_map/ppermute | solution.py:139
  120.8 1.8 %copy-start.14 = (bf16[640,768]{1,0:T(8,128)(2,1)S(1)}, bf16[640,768]{1,0:T(8,128)(2,1)}, u32[]{:S(2)}) copy-start(bf16[640,768]{1,0:T(8,128)(2,1)} %get-tuple-element.148) | copy-start | bytes 2949124
  120.8 10.3 %collective-permute-start.29 = (bf16[64,2048]{1,0:T(8,128)(2,1)S(1)}, bf16[64,2048]{1,0:T(8,128)(2,1)S(1)}, u32[]{:S(2)}, u32[]{:S(2)}) collective-permute-start(bf16[64,2048]{1,0:T(8,128)(2,1)S(1)} %get-tuple-element.169), channel_id=1, source_target_pairs={{0,2},{1,0},{2,4},{3,1},{4,6},{5,3},{6,7},{7,5},{8,10},{9,8},{10,1... | collective-permute-start | bytes 786440 | tf_op jit(solution)/shard_map/ppermute | solution.py:133
  126.0 6.4 %collective-permute-start.28 = (bf16[64,2048]{1,0:T(8,128)(2,1)S(1)}, bf16[64,2048]{1,0:T(8,128)(2,1)S(1)}, u32[]{:S(2)}, u32[]{:S(2)}) collective-permute-start(bf16[64,2048]{1,0:T(8,128)(2,1)S(1)} %get-tuple-element.170), channel_id=1, source_target_pairs={{0,1},{1,3},{2,0},{3,5},{4,2},{5,7},{6,4},{7,6},{8,9},{9,11},{10,8... | collective-permute-start | bytes 786440 | tf_op jit(solution)/shard_map/ppermute | solution.py:133
  128.2 9.3 %collective-permute-start.36 = (bf16[64,2048]{1,0:T(8,128)(2,1)S(1)}, bf16[64,2048]{1,0:T(8,128)(2,1)S(1)}, u32[]{:S(2)}, u32[]{:S(2)}) collective-permute-start(bf16[64,2048]{1,0:T(8,128)(2,1)S(1)} %get-tuple-element.192), channel_id=1, source_target_pairs={{0,16},{8,24},{16,0},{24,8},{1,17},{9,25},{17,1},{25,9},{2,18},{10... | collective-permute-start | bytes 786440 | tf_op jit(solution)/shard_map/ppermute | solution.py:139
  129.8 11.7 %collective-permute-start.37 = (bf16[352,384]{1,0:T(8,128)(2,1)S(1)}, bf16[352,384]{1,0:T(8,128)(2,1)S(1)}, u32[]{:S(2)}, u32[]{:S(2)}) collective-permute-start(bf16[352,384]{1,0:T(8,128)(2,1)S(1)} %get-tuple-element.194), channel_id=1, source_target_pairs={{0,16},{8,24},{16,0},{24,8},{1,17},{9,25},{17,1},{25,9},{2,18},{10... | collective-permute-start | bytes 811016 | tf_op jit(solution)/shard_map/ppermute | solution.py:139
  132.8 10.2 %collective-permute-start.35 = (bf16[64,2048]{1,0:T(8,128)(2,1)S(1)}, bf16[64,2048]{1,0:T(8,128)(2,1)S(1)}, u32[]{:S(2)}, u32[]{:S(2)}) collective-permute-start(bf16[64,2048]{1,0:T(8,128)(2,1)S(1)} %get-tuple-element.165), channel_id=1, source_target_pairs={{0,2},{1,0},{2,4},{3,1},{4,6},{5,3},{6,7},{7,5},{8,10},{9,8},{10,1... | collective-permute-start | bytes 786440 | tf_op jit(solution)/shard_map/ppermute | solution.py:133
  133.3 10.3 %collective-permute-start.33 = (bf16[64,2048]{1,0:T(8,128)(2,1)S(1)}, bf16[64,2048]{1,0:T(8,128)(2,1)S(1)}, u32[]{:S(2)}, u32[]{:S(2)}) collective-permute-start(bf16[64,2048]{1,0:T(8,128)(2,1)S(1)} %get-tuple-element.166), channel_id=1, source_target_pairs={{0,2},{1,0},{2,4},{3,1},{4,6},{5,3},{6,7},{7,5},{8,10},{9,8},{10,1... | collective-permute-start | bytes 786440 | tf_op jit(solution)/shard_map/ppermute | solution.py:133
  134.1 9.4 %collective-permute-start.32 = (bf16[64,2048]{1,0:T(8,128)(2,1)S(1)}, bf16[64,2048]{1,0:T(8,128)(2,1)S(1)}, u32[]{:S(2)}, u32[]{:S(2)}) collective-permute-start(bf16[64,2048]{1,0:T(8,128)(2,1)S(1)} %get-tuple-element.167), channel_id=1, source_target_pairs={{0,1},{1,3},{2,0},{3,5},{4,2},{5,7},{6,4},{7,6},{8,9},{9,11},{10,8... | collective-permute-start | bytes 786440 | tf_op jit(solution)/shard_map/ppermute | solution.py:133
  137.5 7.5 %collective-permute-start.34 = (bf16[64,2048]{1,0:T(8,128)(2,1)S(1)}, bf16[64,2048]{1,0:T(8,128)(2,1)S(1)}, u32[]{:S(2)}, u32[]{:S(2)}) collective-permute-start(bf16[64,2048]{1,0:T(8,128)(2,1)S(1)} %get-tuple-element.168), channel_id=1, source_target_pairs={{0,1},{1,3},{2,0},{3,5},{4,2},{5,7},{6,4},{7,6},{8,9},{9,11},{10,8... | collective-permute-start | bytes 786440 | tf_op jit(solution)/shard_map/ppermute | solution.py:133
  141.5 8.9 %collective-permute-start.41 = (bf16[320,384]{1,0:T(8,128)(2,1)S(1)}, bf16[320,384]{1,0:T(8,128)(2,1)S(1)}, u32[]{:S(2)}, u32[]{:S(2)}) collective-permute-start(bf16[320,384]{1,0:T(8,128)(2,1)S(1)} %slice.129), channel_id=1, source_target_pairs={{0,16},{8,24},{16,0},{24,8},{1,17},{9,25},{17,1},{25,9},{2,18},{10... | collective-permute-start | bytes 737288 | tf_op jit(solution)/shard_map/ppermute | solution.py:139
  143.0 10.2 %collective-permute-start.40 = (bf16[64,2048]{1,0:T(8,128)(2,1)S(1)}, bf16[64,2048]{1,0:T(8,128)(2,1)S(1)}, u32[]{:S(2)}, u32[]{:S(2)}) collective-permute-start(bf16[64,2048]{1,0:T(8,128)(2,1)S(1)} %get-tuple-element.191), channel_id=1, source_target_pairs={{0,16},{8,24},{16,0},{24,8},{1,17},{9,25},{17,1},{25,9},{2,18},{10... | collective-permute-start | bytes 786440 | tf_op jit(solution)/shard_map/ppermute | solution.py:139
  143.5 10.8 %collective-permute-start.42 = (bf16[1024,384]{1,0:T(8,128)(2,1)S(1)}, bf16[1024,384]{1,0:T(8,128)(2,1)S(1)}, u32[]{:S(2)}, u32[]{:S(2)}) collective-permute-start(bf16[1024,384]{1,0:T(8,128)(2,1)S(1)} %dynamic-slice_convert_fusion.1), channel_id=1, source_target_pairs={{0,8},{8,0},{16,24},{24,16},{1,9},{9,1},{17,25},{25,17},{2,10},{10... | collective-permute-start | bytes 2359304 | tf_op jit(solution)/shard_map/ppermute | solution.py:136
  145.1 8.1 %collective-permute-start.39 = (bf16[64,2048]{1,0:T(8,128)(2,1)S(1)}, bf16[64,2048]{1,0:T(8,128)(2,1)S(1)}, u32[]{:S(2)}, u32[]{:S(2)}) collective-permute-start(bf16[64,2048]{1,0:T(8,128)(2,1)S(1)} %get-tuple-element.163), channel_id=1, source_target_pairs={{0,2},{1,0},{2,4},{3,1},{4,6},{5,3},{6,7},{7,5},{8,10},{9,8},{10,1... | collective-permute-start | bytes 786440 | tf_op jit(solution)/shard_map/ppermute | solution.py:133
  146.0 7.2 %collective-permute-start.38 = (bf16[64,2048]{1,0:T(8,128)(2,1)S(1)}, bf16[64,2048]{1,0:T(8,128)(2,1)S(1)}, u32[]{:S(2)}, u32[]{:S(2)}) collective-permute-start(bf16[64,2048]{1,0:T(8,128)(2,1)S(1)} %get-tuple-element.164), channel_id=1, source_target_pairs={{0,1},{1,3},{2,0},{3,5},{4,2},{5,7},{6,4},{7,6},{8,9},{9,11},{10,8... | collective-permute-start | bytes 786440 | tf_op jit(solution)/shard_map/ppermute | solution.py:133
  148.7 5.7 %copy-start.8 = (f32[1,1024,384]{2,1,0:T(8,128)S(1)}, f32[1,1024,384]{2,1,0:T(8,128)}, u32[]{:S(2)}) copy-start(f32[1,1024,384]{2,1,0:T(8,128)} %param.14) | copy-start | bytes 4718596
  150.4 5.4 %collective-permute-start.43 = (bf16[192,2048]{1,0:T(8,128)(2,1)S(1)}, bf16[192,2048]{1,0:T(8,128)(2,1)S(1)}, u32[]{:S(2)}, u32[]{:S(2)}) collective-permute-start(bf16[192,2048]{1,0:T(8,128)(2,1)S(1)} %dynamic-slice_convert_fusion), channel_id=1, source_target_pairs={{0,8},{8,0},{16,24},{24,16},{1,9},{9,1},{17,25},{25,17},{2,10},{10... | collective-permute-start | bytes 2359304 | tf_op jit(solution)/shard_map/ppermute | solution.py:136
  154.3 1.7 %copy-start.9 = (f32[1,192,2048]{2,1,0:T(8,128)S(1)}, f32[1,192,2048]{2,1,0:T(8,128)}, u32[]{:S(2)}) copy-start(f32[1,192,2048]{2,1,0:T(8,128)} %param.15) | copy-start | bytes 4718596

commit v5 on v4

--- a/solution.py
+++ b/solution.py
@@ -259,21 +259,21 @@
         for which in ("out", "in"):
             sums[which, r] = sums[which, r].astype(bf16)
 
-    count = max(1, min(3, far - 1))
+    count = min(4, far)
     theirs = {key: [] for key in sums if key[1]}
 
     def piece(key, i):
-        unit = -(-sums[key].shape[0] // (16 * count)) * 16
-        return sums[key][i * unit : (i + 1) * unit]
+        units = sums[key].shape[0] // 16
+        bounds = [0] + [units * (4 * j - 3) // (4 * count - 4) for j in range(1, count)] + [units]
+        return sums[key][16 * bounds[i] : 16 * bounds[i + 1]]
 
     ends = []
     flows = [(1, 0, far), (-1, 1, far)] + ([(1, 1, far - 1), (-1, 0, far - 1)] if far > 1 else [])
     accs = [dxs[sign * d if d < far else d, i] for sign, i, d in flows]
     for step in range(far):
-        i = step - 1 if far > 1 else 0
-        keys = list(theirs) if 0 <= i < count else []
+        keys = list(theirs) if step < count else []
         sent = [ring(acc, sign) for (sign, _, _), acc in zip(flows, accs)]
-        moved = [shift_y(piece(key, i), key[1]) for key in keys]
+        moved = [shift_y(piece(key, step), key[1]) for key in keys]
         tied = [sums[key] for key in theirs] if step == 0 else []
         out = lax.optimization_barrier((sent, moved, tied))
         sent, moved = out[0], out[1]

time: 158 us -> 158 us (level)
  starting transfers between devices: 41 us -> 43.1 us
  waiting for transfers between devices: 63.9 us -> 61.8 us
    ppermute x8 -> x10, starting transfers between devices: 9.76 us -> 11.9 us  [shift_y(): lax.ppermute(x, 'dp', [(i, (i // 2 + r) % ny * 2 + i % 2) for i in range(...]
    ppermute x8 -> x10, waiting for transfers between devices: 9.99 us -> 9.36 us  [shift_y(): lax.ppermute(x, 'dp', [(i, (i // 2 + r) % ny * 2 + i % 2) for i in range(...]
  transfers between devices with their start and end apart: 44 -> 46, of which waited for: 20 -> 21; matrix products, arithmetic and copies ran while one was open for 15% -> 15% of each run, Pallas kernels for 13% -> 13%
where the time goes in v5:
time: 158 us
  waiting for transfers between devices  61.8 us (39%)
  starting transfers between devices  43.1 us (27%)
  Pallas kernels  23.1 us (15%)
  matrix products  11.4 us (7%)
  other arithmetic  10.1 us (6%)
  local copies, waits for them, and re-layouts  6.98 us (4%)
    ppermute x28, waiting for transfers between devices, ring(): lax.ppermute(x, 'expert', [(i, order[(place[i] + step) % n]) for i in ran...  51.3 us
    ppermute x28, starting transfers between devices, ring(): lax.ppermute(x, 'expert', [(i, order[(place[i] + step) % n]) for i in ran...  29.5 us
    pallas_call x3, Pallas kernels, expert_rows(): pl.pallas_call(kernel, in_specs=[pl.BlockSpec(memory_space=pltpu.SMEM)] +...  20.4 us
    ppermute x10, starting transfers between devices, shift_y(): lax.ppermute(x, 'dp', [(i, (i // 2 + r) % ny * 2 + i % 2) for i in range(...  11.9 us
    dot_general x12, matrix products, add_up(): g = lax.dot_general(p, q, TN, preferred_element_type=f32)  11.4 us
    ppermute x10, waiting for transfers between devices, shift_y(): lax.ppermute(x, 'dp', [(i, (i // 2 + r) % ny * 2 + i % 2) for i in range(...  9.36 us
    unnamed x30, local copies, waits for them, and re-layouts  3.23 us
  transfers between devices with their start and end apart: 46, of which 21 were waited for; matrix products, arithmetic and copies ran while one was open for 15% of the time, Pallas kernels for 13%

profile of v5, /device:TPU:0, one launch (start us, length us, event | category | flops | bytes accessed | tf_op | source)
XLA Modules:
  0.0 157.7 jit_solution(9857013892876367158)
XLA Ops:
  0.6 2.7 %shard_map.103 = (bf16[64,4224]{1,0:T(8,128)(2,1)}, bf16[64,4224]{1,0:T(8,128)(2,1)}) custom-call(bf16[128,2048]{1,0:T(8,128)(2,1)} %tok_ref.1, bf16[128,2048]{1,0:T(8,128)(2,1)} %cot_ref.1, f32[8,128]{1,0:T(8,128)} %bitcast.31, s32[8,128]{1,0:T(8,128)} %bitcast.32), custom_call_target="tpu_custom_call" | custom-call | bytes 2097152 | tf_op jit(solution)/shard_map/pallas_call | solution.py:53
  3.3 3.0 %collective-permute-start.3 = (bf16[64,4224]{1,0:T(8,128)(2,1)}, bf16[64,4224]{1,0:T(8,128)(2,1)}, u32[]{:S(2)}, u32[]{:S(2)}) collective-permute-start(bf16[64,4224]{1,0:T(8,128)(2,1)} %get-tuple-element.99.refs_1_), channel_id=1, source_target_pairs={{0,2},{1,0},{2,4},{3,1},{4,6},{5,3},{6,7},{7,5},{8,10},{9,8},{10,1... | collective-permute-start | bytes 1622024 | tf_op jit(solution)/shard_map/ppermute | solution.py:133
  6.4 2.0 %collective-permute-start.2 = (bf16[64,4224]{1,0:T(8,128)(2,1)}, bf16[64,4224]{1,0:T(8,128)(2,1)}, u32[]{:S(2)}, u32[]{:S(2)}) collective-permute-start(bf16[64,4224]{1,0:T(8,128)(2,1)} %get-tuple-element.98.refs_0_), channel_id=1, source_target_pairs={{0,2},{1,0},{2,4},{3,1},{4,6},{5,3},{6,7},{7,5},{8,10},{9,8},{10,1... | collective-permute-start | bytes 1622024 | tf_op jit(solution)/shard_map/ppermute | solution.py:133
  8.4 2.0 %collective-permute-start.5 = (bf16[1024,384]{1,0:T(8,128)(2,1)}, bf16[1024,384]{1,0:T(8,128)(2,1)}, u32[]{:S(2)}, u32[]{:S(2)}) collective-permute-start(bf16[1024,384]{1,0:T(8,128)(2,1)} %bitcast.29), channel_id=1, source_target_pairs={{0,16},{8,24},{16,0},{24,8},{1,17},{9,25},{17,1},{25,9},{2,18},{10... | collective-permute-start | bytes 2359304 | tf_op jit(solution)/shard_map/ppermute | solution.py:139
  10.4 9.3 %collective-permute-done.3.refs_7_ = bf16[64,4224]{1,0:T(8,128)(2,1)} collective-permute-done((bf16[64,4224]{1,0:T(8,128)(2,1)}, bf16[64,4224]{1,0:T(8,128)(2,1)}, u32[]{:S(2)}, u32[]{:S(2)}) %collective-permute-start.3) | collective-permute-done | bytes 540704 | tf_op jit(solution)/shard_map/ppermute | solution.py:133
  19.7 2.2 %collective-permute-done.1.refs_2_ = bf16[64,4224]{1,0:T(8,128)(2,1)} collective-permute-done((bf16[64,4224]{1,0:T(8,128)(2,1)}, bf16[64,4224]{1,0:T(8,128)(2,1)}, u32[]{:S(2)}, u32[]{:S(2)}) %collective-permute-start.1) | collective-permute-done | bytes 540704 | tf_op jit(solution)/shard_map/ppermute | solution.py:133
  21.9 8.6 %collective-permute-done.2.refs_3_ = bf16[64,4224]{1,0:T(8,128)(2,1)} collective-permute-done((bf16[64,4224]{1,0:T(8,128)(2,1)}, bf16[64,4224]{1,0:T(8,128)(2,1)}, u32[]{:S(2)}, u32[]{:S(2)}) %collective-permute-start.2) | collective-permute-done | bytes 540704 | tf_op jit(solution)/shard_map/ppermute | solution.py:133
  30.4 1.5 collective-permute-done.refs_6_
  32.8 1.6 %collective-permute-start.8 = (bf16[64,4224]{1,0:T(8,128)(2,1)}, bf16[64,4224]{1,0:T(8,128)(2,1)}, u32[]{:S(2)}, u32[]{:S(2)}) collective-permute-start(bf16[64,4224]{1,0:T(8,128)(2,1)} %collective-permute-done.1.refs_2_), channel_id=1, source_target_pairs={{0,1},{1,3},{2,0},{3,5},{4,2},{5,7},{6,4},{7,6},{8,9},{9,11},{10,8... | collective-permute-start | bytes 1622024 | tf_op jit(solution)/shard_map/ppermute | solution.py:133
  34.9 0.7 collective-permute-done.4
  35.5 0.9 copy-done.11
  36.4 1.6 collective-permute-start.10
  38.4 0.7 copy-done.12
  39.3 1.6 %collective-permute-start.12 = (bf16[192,2048]{1,0:T(8,128)(2,1)}, bf16[192,2048]{1,0:T(8,128)(2,1)}, u32[]{:S(2)}, u32[]{:S(2)}) collective-permute-start(bf16[192,2048]{1,0:T(8,128)(2,1)} %bitcast.3), channel_id=1, source_target_pairs={{0,16},{8,24},{16,0},{24,8},{1,17},{9,25},{17,1},{25,9},{2,18},{10... | collective-permute-start | bytes 2359304 | tf_op jit(solution)/shard_map/ppermute | solution.py:139
  40.9 1.3 constant_dynamic-update-slice_fusion.3
  42.2 1.3 constant_dynamic-update-slice_fusion.2.in_ref
  43.5 6.5 %collective-permute-done.9.refs_5_ = bf16[64,4224]{1,0:T(8,128)(2,1)} collective-permute-done((bf16[64,4224]{1,0:T(8,128)(2,1)}, bf16[64,4224]{1,0:T(8,128)(2,1)}, u32[]{:S(2)}, u32[]{:S(2)}) %collective-permute-start.9) | collective-permute-done | bytes 540704 | tf_op jit(solution)/shard_map/ppermute | solution.py:133
  50.0 8.7 %collective-permute-done.8.refs_4_ = bf16[64,4224]{1,0:T(8,128)(2,1)} collective-permute-done((bf16[64,4224]{1,0:T(8,128)(2,1)}, bf16[64,4224]{1,0:T(8,128)(2,1)}, u32[]{:S(2)}, u32[]{:S(2)}) %collective-permute-start.8) | collective-permute-done | bytes 540704 | tf_op jit(solution)/shard_map/ppermute | solution.py:133
  58.7 1.4 collective-permute-done.10.refs_9_
  60.6 1.6 %collective-permute-start.14 = (bf16[64,4224]{1,0:T(8,128)(2,1)}, bf16[64,4224]{1,0:T(8,128)(2,1)S(1)}, u32[]{:S(2)}, u32[]{:S(2)}) collective-permute-start(bf16[64,4224]{1,0:T(8,128)(2,1)} %collective-permute-done.7.refs_8_), channel_id=1, source_target_pairs={{0,1},{1,3},{2,0},{3,5},{4,2},{5,7},{6,4},{7,6},{8,9},{9,11},{10,8... | collective-permute-start | bytes 1622024 | tf_op jit(solution)/shard_map/ppermute | solution.py:133
  62.6 1.6 %collective-permute-start.16 = (bf16[64,4224]{1,0:T(8,128)(2,1)}, bf16[64,4224]{1,0:T(8,128)(2,1)}, u32[]{:S(2)}, u32[]{:S(2)}) collective-permute-start(bf16[64,4224]{1,0:T(8,128)(2,1)} %collective-permute-done.8.refs_4_), channel_id=1, source_target_pairs={{0,1},{1,3},{2,0},{3,5},{4,2},{5,7},{6,4},{7,6},{8,9},{9,11},{10,8... | collective-permute-start | bytes 1622024 | tf_op jit(solution)/shard_map/ppermute | solution.py:133
  64.7 1.5 broadcast_select_fusion.3
  66.2 1.5 broadcast_select_fusion.1
  67.7 1.8 %pad_maximum_fusion.out_ref = bf16[768,2048]{1,0:T(8,128)(2,1)} fusion(bf16[192,2048]{1,0:T(8,128)(2,1)S(1)} %get-tuple-element.188, bf16[192,2048]{1,0:T(8,128)(2,1)S(1)} %get-tuple-element.187, bf16[192,2048]{1,0:T(8,128)(2,1)S(1)} %get-tuple-element.186, bf16[192,2048]{1,0:T(8,128)(2,1)S(1)} %get-tuple-element.185), kind=kLoop, calls=%fused_computation | loop fusion | flops 12582912 | bytes 6291456 | tf_op jit(solution)/shard_map/concatenate | solution.py:184
  69.5 12.9 %shard_map.104 = (bf16[640,768]{1,0:T(8,128)(2,1)S(1)}, bf16[640,768]{1,0:T(8,128)(2,1)}, bf16[640,2048]{1,0:T(8,128)(2,1)}, bf16[640,2048]{1,0:T(8,128)(2,1)}, bf16[640,2048]{1,0:T(8,128)(2,1)}) custom-call(s32[2]{0:T(128)S(1)} %fusion.20.id_ref, bf16[2048,768]{1,0:T(8,128)(2,1)} %copy-done.1, bf16[768,2048]{1,0:T(8,128)(2,1)} %pad_maximum_fusion.out_ref, ...), custom_call_target="tpu_custom_call" | custom-call | flops 1048576 | bytes 65536 | tf_op jit(solution)/shard_map/pallas_call | solution.py:101
  82.5 1.6 %collective-permute-start.15 = (bf16[64,4224]{1,0:T(8,128)(2,1)S(1)}, bf16[64,4224]{1,0:T(8,128)(2,1)S(1)}, u32[]{:S(2)}, u32[]{:S(2)}) collective-permute-start(bf16[64,4224]{1,0:T(8,128)(2,1)S(1)} %collective-permute-done.14.refs_2_), channel_id=1, source_target_pairs={{0,1},{1,3},{2,0},{3,5},{4,2},{5,7},{6,4},{7,6},{8,9},{9,11},{10,8... | collective-permute-start | bytes 1622024 | tf_op jit(solution)/shard_map/ppermute | solution.py:133
  84.6 4.7 %collective-permute-done.17.refs_1_ = bf16[64,4224]{1,0:T(8,128)(2,1)} collective-permute-done((bf16[64,4224]{1,0:T(8,128)(2,1)}, bf16[64,4224]{1,0:T(8,128)(2,1)}, u32[]{:S(2)}, u32[]{:S(2)}) %collective-permute-start.17) | collective-permute-done | bytes 540704 | tf_op jit(solution)/shard_map/ppermute | solution.py:133
  89.3 4.2 %shard_map.105 = (bf16[256,768]{1,0:T(8,128)(2,1)S(1)}, bf16[256,768]{1,0:T(8,128)(2,1)S(1)}, bf16[256,2048]{1,0:T(8,128)(2,1)S(1)}, bf16[256,2048]{1,0:T(8,128)(2,1)S(1)}, bf16[256,2048]{1,0:T(8,128)(2,1)S(1)}) custom-call(s32[2]{0:T(128)S(1)} %fusion.20.id_ref, bf16[2048,768]{1,0:T(8,128)(2,1)S(1)} %copy-done.2, bf16[768,2048]{1,0:T(8,128)(2,1)S(1)} %copy-done, ...), custom_call_target="tpu_custom_call" | custom-call | flops 1048576 | bytes 65536 | tf_op jit(solution)/shard_map/pallas_call | solution.py:101
  93.5 1.6 %collective-permute-start.22 = (bf16[64,2048]{1,0:T(8,128)(2,1)S(1)}, bf16[64,2048]{1,0:T(8,128)(2,1)S(1)}, u32[]{:S(2)}, u32[]{:S(2)}) collective-permute-start(bf16[64,2048]{1,0:T(8,128)(2,1)S(1)} %get-tuple-element.191), channel_id=1, source_target_pairs={{0,1},{1,3},{2,0},{3,5},{4,2},{5,7},{6,4},{7,6},{8,9},{9,11},{10,8... | collective-permute-start | bytes 786440 | tf_op jit(solution)/shard_map/ppermute | solution.py:133
  95.6 1.4 fusion.6
  97.1 0.6 convolution_add_fusion.3
  97.7 1.1 copy-done.6
  99.0 1.7 %fusion.4 = f32[2048,384]{1,0:T(8,128)S(1)} fusion(bf16[640,2048]{1,0:T(8,128)(2,1)S(1)} %copy-done.6, bf16[640,768]{1,0:T(8,128)(2,1)S(1)} %copy-done.13), kind=kOutput, calls=%fused_computation.36 | convolution fusion | flops 1006632960 | bytes 6258688 | tf_op jit(solution)/shard_map/dot_general | solution.py:218
  100.8 0.7 convolution_add_fusion.2
  101.5 3.3 %shard_map.106 = (bf16[128,768]{1,0:T(8,128)(2,1)S(1)}, bf16[128,768]{1,0:T(8,128)(2,1)S(1)}, bf16[128,2048]{1,0:T(8,128)(2,1)S(1)}, bf16[128,2048]{1,0:T(8,128)(2,1)S(1)}, bf16[128,2048]{1,0:T(8,128)(2,1)S(1)}) custom-call(s32[2]{0:T(128)S(1)} %fusion.20.id_ref, bf16[2048,768]{1,0:T(8,128)(2,1)S(1)} %copy-done.2, bf16[768,2048]{1,0:T(8,128)(2,1)S(1)} %copy-done, ...), custom_call_target="tpu_custom_call" | custom-call | flops 1048576 | bytes 65536 | tf_op jit(solution)/shard_map/pallas_call | solution.py:101
  105.6 0.6 convolution_add_fusion
  107.9 1.6 collective-permute-start.20
  109.7 1.6 %collective-permute-start.25 = (bf16[16,2048]{1,0:T(8,128)(2,1)S(1)}, bf16[16,2048]{1,0:T(8,128)(2,1)S(1)}, u32[]{:S(2)}, u32[]{:S(2)}) collective-permute-start(bf16[16,2048]{1,0:T(8,128)(2,1)S(1)} %slice.144), channel_id=1, source_target_pairs={{0,16},{8,24},{16,0},{24,8},{1,17},{9,25},{17,1},{25,9},{2,18},{10... | collective-permute-start | bytes 196616 | tf_op jit(solution)/shard_map/ppermute | solution.py:139
  112.1 3.1 %collective-permute-done.21 = bf16[64,2048]{1,0:T(8,128)(2,1)S(1)} collective-permute-done((bf16[64,2048]{1,0:T(8,128)(2,1)S(1)}, bf16[64,2048]{1,0:T(8,128)(2,1)S(1)}, u32[]{:S(2)}, u32[]{:S(2)}) %collective-permute-start.21) | collective-permute-done | bytes 262176 | tf_op jit(solution)/shard_map/ppermute | solution.py:133
  115.2 1.0 collective-permute-done.20
  116.7 1.6 %collective-permute-start.33 = (bf16[336,384]{1,0:T(8,128)(2,1)S(1)}, bf16[336,384]{1,0:T(8,128)(2,1)S(1)}, u32[]{:S(2)}, u32[]{:S(2)}) collective-permute-start(bf16[336,384]{1,0:T(8,128)(2,1)S(1)} %slice.133), channel_id=1, source_target_pairs={{0,16},{8,24},{16,0},{24,8},{1,17},{9,25},{17,1},{25,9},{2,18},{10... | collective-permute-start | bytes 774152 | tf_op jit(solution)/shard_map/ppermute | solution.py:139
  119.2 1.6 %collective-permute-start.28 = (bf16[64,2048]{1,0:T(8,128)(2,1)S(1)}, bf16[64,2048]{1,0:T(8,128)(2,1)S(1)}, u32[]{:S(2)}, u32[]{:S(2)}) collective-permute-start(bf16[64,2048]{1,0:T(8,128)(2,1)S(1)} %get-tuple-element.190), channel_id=1, source_target_pairs={{0,1},{1,3},{2,0},{3,5},{4,2},{5,7},{6,4},{7,6},{8,9},{9,11},{10,8... | collective-permute-start | bytes 786440 | tf_op jit(solution)/shard_map/ppermute | solution.py:133
  121.3 0.7 fusion.10
  122.0 0.6 fusion.16
  122.6 1.8 %add_add_fusion.1 = f32[2048,384]{1,0:T(8,128)S(1)} fusion(f32[2048,384]{1,0:T(8,128)S(1)} %fusion.16, f32[2048,384]{1,0:T(8,128)S(1)} %fusion.10, bf16[640,2048]{1,0:T(8,128)(2,1)S(1)} %copy-done.6, bf16[640,768]{1,0:T(8,128)(2,1)S(1)} %copy-done.14), kind=kOutput, calls=%fused_computation.2 | convolution fusion | flops 1008205824 | bytes 12550144 | tf_op jit(solution)/shard_map/dot_general | solution.py:218
  124.5 1.4 collective-permute-done.33
  125.9 1.6 collective-permute-start.30
  128.1 1.7 %collective-permute-done.32 = bf16[64,2048]{1,0:T(8,128)(2,1)S(1)} collective-permute-done((bf16[64,2048]{1,0:T(8,128)(2,1)S(1)}, bf16[64,2048]{1,0:T(8,128)(2,1)S(1)}, u32[]{:S(2)}, u32[]{:S(2)}) %collective-permute-start.32) | collective-permute-done | bytes 262176 | tf_op jit(solution)/shard_map/ppermute | solution.py:139
  129.8 1.5 collective-permute-start.38
  133.2 0.9 collective-permute-start.35
  134.1 1.1 collective-permute-start.34
  135.2 3.8 %collective-permute-done.38 = bf16[64,2048]{1,0:T(8,128)(2,1)S(1)} collective-permute-done((bf16[64,2048]{1,0:T(8,128)(2,1)S(1)}, bf16[64,2048]{1,0:T(8,128)(2,1)S(1)}, u32[]{:S(2)}, u32[]{:S(2)}) %collective-permute-start.38) | collective-permute-done | bytes 262176 | tf_op jit(solution)/shard_map/ppermute | solution.py:139
  139.1 1.6 collective-permute-start.36
  141.2 1.0 collective-permute-done.39
  142.2 1.5 collective-permute-start.43
  144.2 1.2 collective-permute-done.36
  145.6 0.8 collective-permute-start.41
  146.4 1.2 collective-permute-start.40
  147.6 1.4 add_add_fusion
  149.3 1.4 collective-permute-done.42
  150.7 2.5 %collective-permute-done.41 = bf16[64,2048]{1,0:T(8,128)(2,1)S(1)} collective-permute-done((bf16[64,2048]{1,0:T(8,128)(2,1)S(1)}, bf16[64,2048]{1,0:T(8,128)(2,1)S(1)}, u32[]{:S(2)}, u32[]{:S(2)}) %collective-permute-start.41) | collective-permute-done | bytes 262176 | tf_op jit(solution)/shard_map/ppermute | solution.py:133
  153.6 0.8 pad_maximum_fusion.1
  154.4 1.5 fusion.1
  156.1 1.6 fusion
  (106 shorter events, 14.2 us)
Async XLA Ops:
  3.3 16.4 %collective-permute-start.3 = (bf16[64,4224]{1,0:T(8,128)(2,1)}, bf16[64,4224]{1,0:T(8,128)(2,1)}, u32[]{:S(2)}, u32[]{:S(2)}) collective-permute-start(bf16[64,4224]{1,0:T(8,128)(2,1)} %get-tuple-element.99.refs_1_), channel_id=1, source_target_pairs={{0,2},{1,0},{2,4},{3,1},{4,6},{5,3},{6,7},{7,5},{8,10},{9,8},{10,1... | collective-permute-start | bytes 1622024 | tf_op jit(solution)/shard_map/ppermute | solution.py:133
  6.4 15.5 %collective-permute-start.1 = (bf16[64,4224]{1,0:T(8,128)(2,1)}, bf16[64,4224]{1,0:T(8,128)(2,1)}, u32[]{:S(2)}, u32[]{:S(2)}) collective-permute-start(bf16[64,4224]{1,0:T(8,128)(2,1)} %get-tuple-element.99.refs_1_), channel_id=1, source_target_pairs={{0,1},{1,3},{2,0},{3,5},{4,2},{5,7},{6,4},{7,6},{8,9},{9,11},{10,8... | collective-permute-start | bytes 1622024 | tf_op jit(solution)/shard_map/ppermute | solution.py:133
  6.4 24.1 %collective-permute-start.2 = (bf16[64,4224]{1,0:T(8,128)(2,1)}, bf16[64,4224]{1,0:T(8,128)(2,1)}, u32[]{:S(2)}, u32[]{:S(2)}) collective-permute-start(bf16[64,4224]{1,0:T(8,128)(2,1)} %get-tuple-element.98.refs_0_), channel_id=1, source_target_pairs={{0,2},{1,0},{2,4},{3,1},{4,6},{5,3},{6,7},{7,5},{8,10},{9,8},{10,1... | collective-permute-start | bytes 1622024 | tf_op jit(solution)/shard_map/ppermute | solution.py:133
  8.4 23.6 %collective-permute-start = (bf16[64,4224]{1,0:T(8,128)(2,1)}, bf16[64,4224]{1,0:T(8,128)(2,1)}, u32[]{:S(2)}, u32[]{:S(2)}) collective-permute-start(bf16[64,4224]{1,0:T(8,128)(2,1)} %get-tuple-element.98.refs_0_), channel_id=1, source_target_pairs={{0,1},{1,3},{2,0},{3,5},{4,2},{5,7},{6,4},{7,6},{8,9},{9,11},{10,8... | collective-permute-start | bytes 1622024 | tf_op jit(solution)/shard_map/ppermute | solution.py:133
  8.4 23.6 %collective-permute-start.5 = (bf16[1024,384]{1,0:T(8,128)(2,1)}, bf16[1024,384]{1,0:T(8,128)(2,1)}, u32[]{:S(2)}, u32[]{:S(2)}) collective-permute-start(bf16[1024,384]{1,0:T(8,128)(2,1)} %bitcast.29), channel_id=1, source_target_pairs={{0,16},{8,24},{16,0},{24,8},{1,17},{9,25},{17,1},{25,9},{2,18},{10... | collective-permute-start | bytes 2359304 | tf_op jit(solution)/shard_map/ppermute | solution.py:139
  32.0 3.5 %collective-permute-start.4 = (bf16[1024,384]{1,0:T(8,128)(2,1)}, bf16[1024,384]{1,0:T(8,128)(2,1)S(1)}, u32[]{:S(2)}, u32[]{:S(2)}) collective-permute-start(bf16[1024,384]{1,0:T(8,128)(2,1)} %bitcast.30), channel_id=1, source_target_pairs={{0,8},{8,0},{16,24},{24,16},{1,9},{9,1},{17,25},{25,17},{2,10},{10... | collective-permute-start | bytes 2359304 | tf_op jit(solution)/shard_map/ppermute | solution.py:136
  32.0 7.3 %collective-permute-start.6 = (bf16[1024,384]{1,0:T(8,128)(2,1)}, bf16[1024,384]{1,0:T(8,128)(2,1)}, u32[]{:S(2)}, u32[]{:S(2)}) collective-permute-start(bf16[1024,384]{1,0:T(8,128)(2,1)} %collective-permute-done.5), channel_id=1, source_target_pairs={{0,8},{8,0},{16,24},{24,16},{1,9},{9,1},{17,25},{25,17},{2,10},{10... | collective-permute-start | bytes 2359304 | tf_op jit(solution)/shard_map/ppermute | solution.py:136
  32.5 5.7 %copy-start.10 = (bf16[1,1024,384]{2,1,0:T(8,128)(2,1)S(1)}, bf16[1,1024,384]{2,1,0:T(8,128)(2,1)}, u32[]{:S(2)}) copy-start(bf16[1,1024,384]{2,1,0:T(8,128)(2,1)} %param.12) | copy-start | bytes 2359300
  32.5 26.1 %collective-permute-start.7 = (bf16[64,4224]{1,0:T(8,128)(2,1)}, bf16[64,4224]{1,0:T(8,128)(2,1)}, u32[]{:S(2)}, u32[]{:S(2)}) collective-permute-start(bf16[64,4224]{1,0:T(8,128)(2,1)} %collective-permute-done.refs_6_), channel_id=1, source_target_pairs={{0,1},{1,3},{2,0},{3,5},{4,2},{5,7},{6,4},{7,6},{8,9},{9,11},{10,8... | collective-permute-start | bytes 1622024 | tf_op jit(solution)/shard_map/ppermute | solution.py:133
  32.8 25.8 %collective-permute-start.8 = (bf16[64,4224]{1,0:T(8,128)(2,1)}, bf16[64,4224]{1,0:T(8,128)(2,1)}, u32[]{:S(2)}, u32[]{:S(2)}) collective-permute-start(bf16[64,4224]{1,0:T(8,128)(2,1)} %collective-permute-done.1.refs_2_), channel_id=1, source_target_pairs={{0,1},{1,3},{2,0},{3,5},{4,2},{5,7},{6,4},{7,6},{8,9},{9,11},{10,8... | collective-permute-start | bytes 1622024 | tf_op jit(solution)/shard_map/ppermute | solution.py:133
  34.5 15.5 %collective-permute-start.9 = (bf16[64,4224]{1,0:T(8,128)(2,1)}, bf16[64,4224]{1,0:T(8,128)(2,1)}, u32[]{:S(2)}, u32[]{:S(2)}) collective-permute-start(bf16[64,4224]{1,0:T(8,128)(2,1)} %collective-permute-done.2.refs_3_), channel_id=1, source_target_pairs={{0,2},{1,0},{2,4},{3,1},{4,6},{5,3},{6,7},{7,5},{8,10},{9,8},{10,1... | collective-permute-start | bytes 1622024 | tf_op jit(solution)/shard_map/ppermute | solution.py:133
  35.5 0.9 copy-start.11
  36.4 23.6 %collective-permute-start.10 = (bf16[64,4224]{1,0:T(8,128)(2,1)}, bf16[64,4224]{1,0:T(8,128)(2,1)}, u32[]{:S(2)}, u32[]{:S(2)}) collective-permute-start(bf16[64,4224]{1,0:T(8,128)(2,1)} %collective-permute-done.3.refs_7_), channel_id=1, source_target_pairs={{0,2},{1,0},{2,4},{3,1},{4,6},{5,3},{6,7},{7,5},{8,10},{9,8},{10,1... | collective-permute-start | bytes 1622024 | tf_op jit(solution)/shard_map/ppermute | solution.py:133
  38.0 1.1 copy-start.12
  39.3 20.7 %collective-permute-start.12 = (bf16[192,2048]{1,0:T(8,128)(2,1)}, bf16[192,2048]{1,0:T(8,128)(2,1)}, u32[]{:S(2)}, u32[]{:S(2)}) collective-permute-start(bf16[192,2048]{1,0:T(8,128)(2,1)} %bitcast.3), channel_id=1, source_target_pairs={{0,16},{8,24},{16,0},{24,8},{1,17},{9,25},{17,1},{25,9},{2,18},{10... | collective-permute-start | bytes 2359304 | tf_op jit(solution)/shard_map/ppermute | solution.py:139
  43.5 24.2 %copy-start.1 = (bf16[2048,768]{1,0:T(8,128)(2,1)}, bf16[2048,768]{1,0:T(8,128)(2,1)S(1)}, u32[]{:S(2)}) copy-start(bf16[2048,768]{1,0:T(8,128)(2,1)S(1)} %constant_dynamic-update-slice_fusion.2.in_ref) | copy-start | bytes 9437188
  60.0 4.2 %collective-permute-start.11 = (bf16[192,2048]{1,0:T(8,128)(2,1)}, bf16[192,2048]{1,0:T(8,128)(2,1)}, u32[]{:S(2)}, u32[]{:S(2)}) collective-permute-start(bf16[192,2048]{1,0:T(8,128)(2,1)} %bitcast.3), channel_id=1, source_target_pairs={{0,8},{8,0},{16,24},{24,16},{1,9},{9,1},{17,25},{25,17},{2,10},{10... | collective-permute-start | bytes 2359304 | tf_op jit(solution)/shard_map/ppermute | solution.py:136
  60.0 6.1 %collective-permute-start.13 = (bf16[192,2048]{1,0:T(8,128)(2,1)}, bf16[192,2048]{1,0:T(8,128)(2,1)}, u32[]{:S(2)}, u32[]{:S(2)}) collective-permute-start(bf16[192,2048]{1,0:T(8,128)(2,1)} %collective-permute-done.12), channel_id=1, source_target_pairs={{0,8},{8,0},{16,24},{24,16},{1,9},{9,1},{17,25},{25,17},{2,10},{10... | collective-permute-start | bytes 2359304 | tf_op jit(solution)/shard_map/ppermute | solution.py:136
  60.6 21.9 %collective-permute-start.14 = (bf16[64,4224]{1,0:T(8,128)(2,1)}, bf16[64,4224]{1,0:T(8,128)(2,1)S(1)}, u32[]{:S(2)}, u32[]{:S(2)}) collective-permute-start(bf16[64,4224]{1,0:T(8,128)(2,1)} %collective-permute-done.7.refs_8_), channel_id=1, source_target_pairs={{0,1},{1,3},{2,0},{3,5},{4,2},{5,7},{6,4},{7,6},{8,9},{9,11},{10,8... | collective-permute-start | bytes 1622024 | tf_op jit(solution)/shard_map/ppermute | solution.py:133
  62.2 21.9 %collective-permute-start.18 = (bf16[64,4224]{1,0:T(8,128)(2,1)}, bf16[64,4224]{1,0:T(8,128)(2,1)}, u32[]{:S(2)}, u32[]{:S(2)}) collective-permute-start(bf16[64,4224]{1,0:T(8,128)(2,1)} %collective-permute-done.10.refs_9_), channel_id=1, source_target_pairs={{0,2},{1,0},{2,4},{3,1},{4,6},{5,3},{6,7},{7,5},{8,10},{9,8},{10,1... | collective-permute-start | bytes 1622024 | tf_op jit(solution)/shard_map/ppermute | solution.py:133
  62.6 26.6 %collective-permute-start.16 = (bf16[64,4224]{1,0:T(8,128)(2,1)}, bf16[64,4224]{1,0:T(8,128)(2,1)}, u32[]{:S(2)}, u32[]{:S(2)}) collective-permute-start(bf16[64,4224]{1,0:T(8,128)(2,1)} %collective-permute-done.8.refs_4_), channel_id=1, source_target_pairs={{0,1},{1,3},{2,0},{3,5},{4,2},{5,7},{6,4},{7,6},{8,9},{9,11},{10,8... | collective-permute-start | bytes 1622024 | tf_op jit(solution)/shard_map/ppermute | solution.py:133
  64.2 25.1 %collective-permute-start.17 = (bf16[64,4224]{1,0:T(8,128)(2,1)}, bf16[64,4224]{1,0:T(8,128)(2,1)}, u32[]{:S(2)}, u32[]{:S(2)}) collective-permute-start(bf16[64,4224]{1,0:T(8,128)(2,1)} %collective-permute-done.9.refs_5_), channel_id=1, source_target_pairs={{0,2},{1,0},{2,4},{3,1},{4,6},{5,3},{6,7},{7,5},{8,10},{9,8},{10,1... | collective-permute-start | bytes 1622024 | tf_op jit(solution)/shard_map/ppermute | solution.py:133
  67.6 1.9 %copy-start.3 = (bf16[64,4224]{1,0:T(8,128)(2,1)S(1)}, bf16[64,4224]{1,0:T(8,128)(2,1)}, u32[]{:S(2)}) copy-start(bf16[64,4224]{1,0:T(8,128)(2,1)} %get-tuple-element.98.refs_0_) | copy-start | bytes 1622020
  67.7 1.9 %copy-start.4 = (bf16[64,4224]{1,0:T(8,128)(2,1)S(1)}, bf16[64,4224]{1,0:T(8,128)(2,1)}, u32[]{:S(2)}) copy-start(bf16[64,4224]{1,0:T(8,128)(2,1)} %get-tuple-element.99.refs_1_) | copy-start | bytes 1622020
  69.5 19.8 %copy-start = (bf16[768,2048]{1,0:T(8,128)(2,1)S(1)}, bf16[768,2048]{1,0:T(8,128)(2,1)}, u32[]{:S(2)}) copy-start(bf16[768,2048]{1,0:T(8,128)(2,1)} %pad_maximum_fusion.out_ref) | copy-start | bytes 9437188
  69.5 19.8 %copy-start.2 = (bf16[2048,768]{1,0:T(8,128)(2,1)S(1)}, bf16[2048,768]{1,0:T(8,128)(2,1)}, u32[]{:S(2)}) copy-start(bf16[2048,768]{1,0:T(8,128)(2,1)} %copy-done.1) | copy-start | bytes 9437188
  82.5 13.1 %copy-start.5 = (bf16[640,2048]{1,0:T(8,128)(2,1)S(1)}, bf16[640,2048]{1,0:T(8,128)(2,1)}, u32[]{:S(2)}) copy-start(bf16[640,2048]{1,0:T(8,128)(2,1)} %get-tuple-element.160) | copy-start | bytes 7864324
  82.5 19.0 %collective-permute-start.15 = (bf16[64,4224]{1,0:T(8,128)(2,1)S(1)}, bf16[64,4224]{1,0:T(8,128)(2,1)S(1)}, u32[]{:S(2)}, u32[]{:S(2)}) collective-permute-start(bf16[64,4224]{1,0:T(8,128)(2,1)S(1)} %collective-permute-done.14.refs_2_), channel_id=1, source_target_pairs={{0,1},{1,3},{2,0},{3,5},{4,2},{5,7},{6,4},{7,6},{8,9},{9,11},{10,8... | collective-permute-start | bytes 1622024 | tf_op jit(solution)/shard_map/ppermute | solution.py:133
  84.1 17.4 %collective-permute-start.19 = (bf16[64,4224]{1,0:T(8,128)(2,1)}, bf16[64,4224]{1,0:T(8,128)(2,1)S(1)}, u32[]{:S(2)}, u32[]{:S(2)}) collective-permute-start(bf16[64,4224]{1,0:T(8,128)(2,1)} %collective-permute-done.18.refs_3_), channel_id=1, source_target_pairs={{0,2},{1,0},{2,4},{3,1},{4,6},{5,3},{6,7},{7,5},{8,10},{9,8},{10,1... | collective-permute-start | bytes 1622024 | tf_op jit(solution)/shard_map/ppermute | solution.py:133
  93.5 18.0 %collective-permute-start.22 = (bf16[64,2048]{1,0:T(8,128)(2,1)S(1)}, bf16[64,2048]{1,0:T(8,128)(2,1)S(1)}, u32[]{:S(2)}, u32[]{:S(2)}) collective-permute-start(bf16[64,2048]{1,0:T(8,128)(2,1)S(1)} %get-tuple-element.191), channel_id=1, source_target_pairs={{0,1},{1,3},{2,0},{3,5},{4,2},{5,7},{6,4},{7,6},{8,9},{9,11},{10,8... | collective-permute-start | bytes 786440 | tf_op jit(solution)/shard_map/ppermute | solution.py:133
  95.2 16.9 %collective-permute-start.23 = (bf16[64,2048]{1,0:T(8,128)(2,1)S(1)}, bf16[64,2048]{1,0:T(8,128)(2,1)S(1)}, u32[]{:S(2)}, u32[]{:S(2)}) collective-permute-start(bf16[64,2048]{1,0:T(8,128)(2,1)S(1)} %get-tuple-element.192), channel_id=1, source_target_pairs={{0,2},{1,0},{2,4},{3,1},{4,6},{5,3},{6,7},{7,5},{8,10},{9,8},{10,1... | collective-permute-start | bytes 786440 | tf_op jit(solution)/shard_map/ppermute | solution.py:133
  97.0 1.7 %copy-start.6 = (bf16[640,2048]{1,0:T(8,128)(2,1)S(1)}, bf16[640,2048]{1,0:T(8,128)(2,1)}, u32[]{:S(2)}) copy-start(bf16[640,2048]{1,0:T(8,128)(2,1)} %get-tuple-element.149) | copy-start | bytes 7864324
  97.0 2.0 %copy-start.13 = (bf16[640,768]{1,0:T(8,128)(2,1)S(1)}, bf16[640,768]{1,0:T(8,128)(2,1)}, u32[]{:S(2)}) copy-start(bf16[640,768]{1,0:T(8,128)(2,1)} %get-tuple-element.150) | copy-start | bytes 2949124
  105.5 2.4 %collective-permute-start.24 = (bf16[192,2048]{1,0:T(8,128)(2,1)S(1)}, bf16[192,2048]{1,0:T(8,128)(2,1)S(1)}, u32[]{:S(2)}, u32[]{:S(2)}) collective-permute-start(bf16[192,2048]{1,0:T(8,128)(2,1)S(1)} %dynamic-slice_convert_fusion.3), channel_id=1, source_target_pairs={{0,8},{8,0},{16,24},{24,16},{1,9},{9,1},{17,25},{25,17},{2,10},{10... | collective-permute-start | bytes 2359304 | tf_op jit(solution)/shard_map/ppermute | solution.py:136
  106.3 3.4 %collective-permute-start.26 = (bf16[1024,384]{1,0:T(8,128)(2,1)S(1)}, bf16[1024,384]{1,0:T(8,128)(2,1)S(1)}, u32[]{:S(2)}, u32[]{:S(2)}) collective-permute-start(bf16[1024,384]{1,0:T(8,128)(2,1)S(1)} %dynamic-slice_convert_fusion.2), channel_id=1, source_target_pairs={{0,8},{8,0},{16,24},{24,16},{1,9},{9,1},{17,25},{25,17},{2,10},{10... | collective-permute-start | bytes 2359304 | tf_op jit(solution)/shard_map/ppermute | solution.py:136
  106.9 8.3 %collective-permute-start.21 = (bf16[64,2048]{1,0:T(8,128)(2,1)S(1)}, bf16[64,2048]{1,0:T(8,128)(2,1)S(1)}, u32[]{:S(2)}, u32[]{:S(2)}) collective-permute-start(bf16[64,2048]{1,0:T(8,128)(2,1)S(1)} %get-tuple-element.197), channel_id=1, source_target_pairs={{0,2},{1,0},{2,4},{3,1},{4,6},{5,3},{6,7},{7,5},{8,10},{9,8},{10,1... | collective-permute-start | bytes 786440 | tf_op jit(solution)/shard_map/ppermute | solution.py:133
  107.9 8.3 %collective-permute-start.20 = (bf16[64,2048]{1,0:T(8,128)(2,1)S(1)}, bf16[64,2048]{1,0:T(8,128)(2,1)S(1)}, u32[]{:S(2)}, u32[]{:S(2)}) collective-permute-start(bf16[64,2048]{1,0:T(8,128)(2,1)S(1)} %get-tuple-element.198), channel_id=1, source_target_pairs={{0,1},{1,3},{2,0},{3,5},{4,2},{5,7},{6,4},{7,6},{8,9},{9,11},{10,8... | collective-permute-start | bytes 786440 | tf_op jit(solution)/shard_map/ppermute | solution.py:133
  109.7 6.9 %copy-start.7 = (bf16[640,2048]{1,0:T(8,128)(2,1)S(1)}, bf16[640,2048]{1,0:T(8,128)(2,1)}, u32[]{:S(2)}) copy-start(bf16[640,2048]{1,0:T(8,128)(2,1)} %get-tuple-element.108) | copy-start | bytes 7864324
  109.7 6.5 %collective-permute-start.25 = (bf16[16,2048]{1,0:T(8,128)(2,1)S(1)}, bf16[16,2048]{1,0:T(8,128)(2,1)S(1)}, u32[]{:S(2)}, u32[]{:S(2)}) collective-permute-start(bf16[16,2048]{1,0:T(8,128)(2,1)S(1)} %slice.144), channel_id=1, source_target_pairs={{0,16},{8,24},{16,0},{24,8},{1,17},{9,25},{17,1},{25,9},{2,18},{10... | collective-permute-start | bytes 196616 | tf_op jit(solution)/shard_map/ppermute | solution.py:139
  111.5 4.7 %collective-permute-start.27 = (bf16[80,384]{1,0:T(8,128)(2,1)S(1)}, bf16[80,384]{1,0:T(8,128)(2,1)S(1)}, u32[]{:S(2)}, u32[]{:S(2)}) collective-permute-start(bf16[80,384]{1,0:T(8,128)(2,1)S(1)} %slice.145), channel_id=1, source_target_pairs={{0,16},{8,24},{16,0},{24,8},{1,17},{9,25},{17,1},{25,9},{2,18},{10... | collective-permute-start | bytes 184328 | tf_op jit(solution)/shard_map/ppermute | solution.py:139
  116.7 9.2 %collective-permute-start.33 = (bf16[336,384]{1,0:T(8,128)(2,1)S(1)}, bf16[336,384]{1,0:T(8,128)(2,1)S(1)}, u32[]{:S(2)}, u32[]{:S(2)}) collective-permute-start(bf16[336,384]{1,0:T(8,128)(2,1)S(1)} %slice.133), channel_id=1, source_target_pairs={{0,16},{8,24},{16,0},{24,8},{1,17},{9,25},{17,1},{25,9},{2,18},{10... | collective-permute-start | bytes 774152 | tf_op jit(solution)/shard_map/ppermute | solution.py:139
  118.3 11.5 %collective-permute-start.32 = (bf16[64,2048]{1,0:T(8,128)(2,1)S(1)}, bf16[64,2048]{1,0:T(8,128)(2,1)S(1)}, u32[]{:S(2)}, u32[]{:S(2)}) collective-permute-start(bf16[64,2048]{1,0:T(8,128)(2,1)S(1)} %get-tuple-element.196), channel_id=1, source_target_pairs={{0,16},{8,24},{16,0},{24,8},{1,17},{9,25},{17,1},{25,9},{2,18},{10... | collective-permute-start | bytes 786440 | tf_op jit(solution)/shard_map/ppermute | solution.py:139
  118.8 12.5 %collective-permute-start.29 = (bf16[64,2048]{1,0:T(8,128)(2,1)S(1)}, bf16[64,2048]{1,0:T(8,128)(2,1)S(1)}, u32[]{:S(2)}, u32[]{:S(2)}) collective-permute-start(bf16[64,2048]{1,0:T(8,128)(2,1)S(1)} %get-tuple-element.189), channel_id=1, source_target_pairs={{0,2},{1,0},{2,4},{3,1},{4,6},{5,3},{6,7},{7,5},{8,10},{9,8},{10,1... | collective-permute-start | bytes 786440 | tf_op jit(solution)/shard_map/ppermute | solution.py:133
  119.2 12.6 %collective-permute-start.28 = (bf16[64,2048]{1,0:T(8,128)(2,1)S(1)}, bf16[64,2048]{1,0:T(8,128)(2,1)S(1)}, u32[]{:S(2)}, u32[]{:S(2)}) collective-permute-start(bf16[64,2048]{1,0:T(8,128)(2,1)S(1)} %get-tuple-element.190), channel_id=1, source_target_pairs={{0,1},{1,3},{2,0},{3,5},{4,2},{5,7},{6,4},{7,6},{8,9},{9,11},{10,8... | collective-permute-start | bytes 786440 | tf_op jit(solution)/shard_map/ppermute | solution.py:133
  120.8 1.8 %copy-start.14 = (bf16[640,768]{1,0:T(8,128)(2,1)S(1)}, bf16[640,768]{1,0:T(8,128)(2,1)}, u32[]{:S(2)}) copy-start(bf16[640,768]{1,0:T(8,128)(2,1)} %get-tuple-element.150) | copy-start | bytes 2949124
  120.8 11.0 %collective-permute-start.31 = (bf16[64,2048]{1,0:T(8,128)(2,1)S(1)}, bf16[64,2048]{1,0:T(8,128)(2,1)S(1)}, u32[]{:S(2)}, u32[]{:S(2)}) collective-permute-start(bf16[64,2048]{1,0:T(8,128)(2,1)S(1)} %get-tuple-element.173), channel_id=1, source_target_pairs={{0,2},{1,0},{2,4},{3,1},{4,6},{5,3},{6,7},{7,5},{8,10},{9,8},{10,1... | collective-permute-start | bytes 786440 | tf_op jit(solution)/shard_map/ppermute | solution.py:133
  125.9 6.4 %collective-permute-start.30 = (bf16[64,2048]{1,0:T(8,128)(2,1)S(1)}, bf16[64,2048]{1,0:T(8,128)(2,1)S(1)}, u32[]{:S(2)}, u32[]{:S(2)}) collective-permute-start(bf16[64,2048]{1,0:T(8,128)(2,1)S(1)} %get-tuple-element.174), channel_id=1, source_target_pairs={{0,1},{1,3},{2,0},{3,5},{4,2},{5,7},{6,4},{7,6},{8,9},{9,11},{10,8... | collective-permute-start | bytes 786440 | tf_op jit(solution)/shard_map/ppermute | solution.py:133
  129.8 9.2 %collective-permute-start.38 = (bf16[64,2048]{1,0:T(8,128)(2,1)S(1)}, bf16[64,2048]{1,0:T(8,128)(2,1)S(1)}, u32[]{:S(2)}, u32[]{:S(2)}) collective-permute-start(bf16[64,2048]{1,0:T(8,128)(2,1)S(1)} %get-tuple-element.195), channel_id=1, source_target_pairs={{0,16},{8,24},{16,0},{24,8},{1,17},{9,25},{17,1},{25,9},{2,18},{10... | collective-permute-start | bytes 786440 | tf_op jit(solution)/shard_map/ppermute | solution.py:139
  131.3 10.9 %collective-permute-start.39 = (bf16[352,384]{1,0:T(8,128)(2,1)S(1)}, bf16[352,384]{1,0:T(8,128)(2,1)S(1)}, u32[]{:S(2)}, u32[]{:S(2)}) collective-permute-start(bf16[352,384]{1,0:T(8,128)(2,1)S(1)} %slice.135), channel_id=1, source_target_pairs={{0,16},{8,24},{16,0},{24,8},{1,17},{9,25},{17,1},{25,9},{2,18},{10... | collective-permute-start | bytes 811016 | tf_op jit(solution)/shard_map/ppermute | solution.py:139
  132.7 11.0 %collective-permute-start.37 = (bf16[64,2048]{1,0:T(8,128)(2,1)S(1)}, bf16[64,2048]{1,0:T(8,128)(2,1)S(1)}, u32[]{:S(2)}, u32[]{:S(2)}) collective-permute-start(bf16[64,2048]{1,0:T(8,128)(2,1)S(1)} %get-tuple-element.169), channel_id=1, source_target_pairs={{0,2},{1,0},{2,4},{3,1},{4,6},{5,3},{6,7},{7,5},{8,10},{9,8},{10,1... | collective-permute-start | bytes 786440 | tf_op jit(solution)/shard_map/ppermute | solution.py:133
  133.2 11.0 %collective-permute-start.35 = (bf16[64,2048]{1,0:T(8,128)(2,1)S(1)}, bf16[64,2048]{1,0:T(8,128)(2,1)S(1)}, u32[]{:S(2)}, u32[]{:S(2)}) collective-permute-start(bf16[64,2048]{1,0:T(8,128)(2,1)S(1)} %get-tuple-element.170), channel_id=1, source_target_pairs={{0,2},{1,0},{2,4},{3,1},{4,6},{5,3},{6,7},{7,5},{8,10},{9,8},{10,1... | collective-permute-start | bytes 786440 | tf_op jit(solution)/shard_map/ppermute | solution.py:133
  134.1 10.2 %collective-permute-start.34 = (bf16[64,2048]{1,0:T(8,128)(2,1)S(1)}, bf16[64,2048]{1,0:T(8,128)(2,1)S(1)}, u32[]{:S(2)}, u32[]{:S(2)}) collective-permute-start(bf16[64,2048]{1,0:T(8,128)(2,1)S(1)} %get-tuple-element.171), channel_id=1, source_target_pairs={{0,1},{1,3},{2,0},{3,5},{4,2},{5,7},{6,4},{7,6},{8,9},{9,11},{10,8... | collective-permute-start | bytes 786440 | tf_op jit(solution)/shard_map/ppermute | solution.py:133
  139.1 6.4 %collective-permute-start.36 = (bf16[64,2048]{1,0:T(8,128)(2,1)S(1)}, bf16[64,2048]{1,0:T(8,128)(2,1)S(1)}, u32[]{:S(2)}, u32[]{:S(2)}) collective-permute-start(bf16[64,2048]{1,0:T(8,128)(2,1)S(1)} %get-tuple-element.172), channel_id=1, source_target_pairs={{0,1},{1,3},{2,0},{3,5},{4,2},{5,7},{6,4},{7,6},{8,9},{9,11},{10,8... | collective-permute-start | bytes 786440 | tf_op jit(solution)/shard_map/ppermute | solution.py:133
  142.2 7.0 %collective-permute-start.43 = (bf16[256,384]{1,0:T(8,128)(2,1)S(1)}, bf16[256,384]{1,0:T(8,128)(2,1)S(1)}, u32[]{:S(2)}, u32[]{:S(2)}) collective-permute-start(bf16[256,384]{1,0:T(8,128)(2,1)S(1)} %slice.137), channel_id=1, source_target_pairs={{0,16},{8,24},{16,0},{24,8},{1,17},{9,25},{17,1},{25,9},{2,18},{10... | collective-permute-start | bytes 589832 | tf_op jit(solution)/shard_map/ppermute | solution.py:139
  143.7 7.0 %collective-permute-start.42 = (bf16[48,2048]{1,0:T(8,128)(2,1)S(1)}, bf16[48,2048]{1,0:T(8,128)(2,1)S(1)}, u32[]{:S(2)}, u32[]{:S(2)}) collective-permute-start(bf16[48,2048]{1,0:T(8,128)(2,1)S(1)} %slice.136), channel_id=1, source_target_pairs={{0,16},{8,24},{16,0},{24,8},{1,17},{9,25},{17,1},{25,9},{2,18},{10... | collective-permute-start | bytes 589832 | tf_op jit(solution)/shard_map/ppermute | solution.py:139
  144.2 10.2 %collective-permute-start.44 = (bf16[1024,384]{1,0:T(8,128)(2,1)S(1)}, bf16[1024,384]{1,0:T(8,128)(2,1)S(1)}, u32[]{:S(2)}, u32[]{:S(2)}) collective-permute-start(bf16[1024,384]{1,0:T(8,128)(2,1)S(1)} %dynamic-slice_convert_fusion.1), channel_id=1, source_target_pairs={{0,8},{8,0},{16,24},{24,16},{1,9},{9,1},{17,25},{25,17},{2,10},{10... | collective-permute-start | bytes 2359304 | tf_op jit(solution)/shard_map/ppermute | solution.py:136
  145.6 7.6 %collective-permute-start.41 = (bf16[64,2048]{1,0:T(8,128)(2,1)S(1)}, bf16[64,2048]{1,0:T(8,128)(2,1)S(1)}, u32[]{:S(2)}, u32[]{:S(2)}) collective-permute-start(bf16[64,2048]{1,0:T(8,128)(2,1)S(1)} %get-tuple-element.167), channel_id=1, source_target_pairs={{0,2},{1,0},{2,4},{3,1},{4,6},{5,3},{6,7},{7,5},{8,10},{9,8},{10,1... | collective-permute-start | bytes 786440 | tf_op jit(solution)/shard_map/ppermute | solution.py:133
  146.4 6.9 %collective-permute-start.40 = (bf16[64,2048]{1,0:T(8,128)(2,1)S(1)}, bf16[64,2048]{1,0:T(8,128)(2,1)S(1)}, u32[]{:S(2)}, u32[]{:S(2)}) collective-permute-start(bf16[64,2048]{1,0:T(8,128)(2,1)S(1)} %get-tuple-element.168), channel_id=1, source_target_pairs={{0,1},{1,3},{2,0},{3,5},{4,2},{5,7},{6,4},{7,6},{8,9},{9,11},{10,8... | collective-permute-start | bytes 786440 | tf_op jit(solution)/shard_map/ppermute | solution.py:133
  149.1 5.3 %copy-start.8 = (f32[1,1024,384]{2,1,0:T(8,128)S(1)}, f32[1,1024,384]{2,1,0:T(8,128)}, u32[]{:S(2)}) copy-start(f32[1,1024,384]{2,1,0:T(8,128)} %param.14) | copy-start | bytes 4718596
  149.2 6.7 %collective-permute-start.45 = (bf16[192,2048]{1,0:T(8,128)(2,1)S(1)}, bf16[192,2048]{1,0:T(8,128)(2,1)S(1)}, u32[]{:S(2)}, u32[]{:S(2)}) collective-permute-start(bf16[192,2048]{1,0:T(8,128)(2,1)S(1)} %dynamic-slice_convert_fusion), channel_id=1, source_target_pairs={{0,8},{8,0},{16,24},{24,16},{1,9},{9,1},{17,25},{25,17},{2,10},{10... | collective-permute-start | bytes 2359304 | tf_op jit(solution)/shard_map/ppermute | solution.py:136
  154.4 1.7 %copy-start.9 = (f32[1,192,2048]{2,1,0:T(8,128)S(1)}, f32[1,192,2048]{2,1,0:T(8,128)}, u32[]{:S(2)}) copy-start(f32[1,192,2048]{2,1,0:T(8,128)} %param.15) | copy-start | bytes 4718596
